TPU v7x, 32 devices: a whole 2x2x4 slice. The times are simulated.
32 devices in a mesh: tm: 8 (over z, y), member: 4 (over x, core).
Axes of the slice: x: 2, y: 2, z: 4, core: 2. Of those that a mesh axis runs over, the one named last changes fastest.
Arguments:
- queries: bfloat16 [16384, 512], P(('member', 'tm')), parts along dimension 0, may hold values from -12 to 12
- key_rows: bfloat16 [16384, 512], P(('member', 'tm')), parts along dimension 0, may hold values from -6 to 6
- value_rows: bfloat16 [16384, 512], P(('member', 'tm')), parts along dimension 0, may hold values from -6 to 6
- grad_output: bfloat16 [16384, 512], P(('member', 'tm')), parts along dimension 0, may hold values from -6 to 6
- extra_blocks: int32 [32, 16], P('member'), parts along dimension 0, may hold values from -1 to 255, as said below
Outputs:
- mixed_rows: bfloat16 [16384, 512], P(('member', 'tm')), parts along dimension 0
- query_grad: bfloat16 [16384, 512], P(('member', 'tm')), parts along dimension 0
- key_grad: bfloat16 [16384, 512], P(('member', 'tm')), parts along dimension 0
- value_grad: bfloat16 [16384, 512], P(('member', 'tm')), parts along dimension 0
There are 4 independent parts, one for each index of `member`. A program takes and returns all parts, laid end to end along the dimension named above; each array names one. Nothing has to cross between parts.
Inputs may be any that keep to these rules, and one draw needn't show every extreme that they name: `extra_blocks`: row b lists distinct sub-blocks of 16 rows, each inside an earlier block; -1 marks an empty entry, and empty entries stand after the others. From any one block a row takes either no sub-block or exactly 2.
All inputs are finite; a program needn't handle non-finite values.
Results may differ from a plain program's by a relative error of at most 0.035.
Values may be sent and summed in bfloat16 or wider, within the bound.
No kernel may reach another device: no remote copies, remote signals or barrier semaphores. Data moves between devices by JAX's collectives and lax.ppermute only.
A program may use at most 128 MiB of HBM per device.

v0:
```python
import functools
import math

import jax
import jax.numpy as jnp
from jax import lax
from jax.experimental import pallas as pl
from jax.experimental.pallas import tpu as pltpu
from jax.sharding import PartitionSpec as P

HD = 64
HG = 2
SUB = 16
CAP = 2
TILE = 256
LOWEST = -1e30
CAST = jnp.bfloat16
TOGETHER = 2


very_negative = -1e30


def from_behind(value, axis, by):
    peers = lax.axis_size(axis)
    pairs = [(i, i + by) for i in range(peers) if 0 <= i + by < peers]
    return lax.ppermute(value, axis, pairs)


def split_heads(values):
    return values.reshape(values.shape[0], values.shape[1] // HD, HD)


def forward_group(query_part, key_part, value_part, key_mask, scaling):
    scores = (
        jnp.einsum(
            "qhd,khd->hqk",
            split_heads(query_part),
            split_heads(key_part),
            preferred_element_type=jnp.float32,
        )
        * scaling
    )
    scores = jnp.where(key_mask[None], scores, very_negative)
    weights = jax.nn.softmax(scores, axis=-1)
    weights_low = weights.astype(jnp.bfloat16)
    mixed_heads = jnp.einsum(
        "hqk,khd->qhd", weights_low, split_heads(value_part), preferred_element_type=jnp.float32
    )
    mixed_part = mixed_heads.reshape(query_part.shape).astype(jnp.bfloat16)
    return (weights, weights_low, mixed_part)


def backward_group(
    query_part, key_part, value_part, grad_part, mixed_part, weights, weights_low, scaling
):
    grad_heads = split_heads(grad_part)
    row_delta = jnp.sum(
        grad_heads.astype(jnp.float32) * split_heads(mixed_part).astype(jnp.float32), axis=-1
    )
    row_delta = jnp.transpose(row_delta)[:, :, None]
    weight_grads = jnp.einsum(
        "qhd,khd->hqk", grad_heads, split_heads(value_part), preferred_element_type=jnp.float32
    )
    score_grads = (weights * (weight_grads - row_delta)).astype(jnp.bfloat16)
    query_grads = (
        jnp.einsum(
            "hqk,khd->qhd", score_grads, split_heads(key_part), preferred_element_type=jnp.float32
        )
        * scaling
    )
    key_grads = (
        jnp.einsum(
            "hqk,qhd->khd", score_grads, split_heads(query_part), preferred_element_type=jnp.float32
        )
        * scaling
    )
    value_grads = jnp.einsum(
        "hqk,qhd->khd", weights_low, grad_heads, preferred_element_type=jnp.float32
    )
    return (
        query_grads.reshape(query_part.shape),
        key_grads.reshape(key_part.shape),
        value_grads.reshape(key_part.shape),
    )


def block_plan(queries, key_rows, value_rows, grad_output, extra_blocks):
    devices = lax.axis_size("tm")
    position = lax.axis_index("tm")
    block_rows = queries.shape[0]
    model_width = queries.shape[1]
    per_block = block_rows // SUB
    group_width = HG * HD
    group_count = model_width // group_width
    scaling = 1.0 / math.sqrt(HD)
    distances = []
    reach = 1
    while reach < devices:
        distances.append(reach)
        reach = reach * 2
    key_value = jnp.concatenate([key_rows, value_rows], axis=1)
    partner_blocks = [from_behind(key_value, "tm", distance) for distance in distances]
    owner_table = jnp.where(extra_blocks >= 0, extra_blocks // per_block, -1)
    inside_table = jnp.where(extra_blocks >= 0, extra_blocks % per_block, 0)
    owned_here = owner_table == position
    ranked = jnp.cumsum(owned_here.astype(jnp.int32), axis=1) - 1
    slot_ids = jnp.arange(CAP, dtype=jnp.int32)
    chosen = owned_here[:, None, :] & (ranked[:, None, :] == slot_ids[None, :, None])
    send_valid = jnp.any(chosen, axis=2)
    send_index = jnp.sum(jnp.where(chosen, inside_table[:, None, :], 0), axis=2)
    key_value_subs = key_value.reshape(per_block, SUB * 2 * model_width)
    send_rows = jnp.take(key_value_subs, send_index.reshape(-1), axis=0).reshape(
        devices * CAP * SUB, 2 * model_width
    )
    extra_rows = lax.all_to_all(send_rows, "tm", split_axis=0, concat_axis=0, tiled=True)
    my_owners = lax.dynamic_index_in_dim(owner_table, position, 0, keepdims=False)
    owner_ids = jnp.arange(devices, dtype=jnp.int32)
    taken_count = jnp.sum((my_owners[None, :] == owner_ids[:, None]).astype(jnp.int32), axis=1)
    slot_live = taken_count[:, None] > slot_ids[None, :]
    extra_live = jnp.repeat(slot_live.reshape(-1), SUB)
    row_ids = jnp.arange(block_rows, dtype=jnp.int32)
    own_mask = row_ids[:, None] >= row_ids[None, :]
    partner_live = jnp.concatenate(
        [jnp.broadcast_to(position >= distance, (block_rows,)) for distance in distances]
    )
    far_live = jnp.concatenate([partner_live, extra_live])
    key_mask = jnp.concatenate(
        [own_mask, jnp.broadcast_to(far_live[None, :], (block_rows, far_live.shape[0]))], axis=1
    )
    all_keys = jnp.concatenate([key_value] + partner_blocks + [extra_rows], axis=0)

    def columns(array, group_index, offset):
        return array[
            :, offset + group_index * group_width : offset + (group_index + 1) * group_width
        ]

    mixed_parts, query_parts, key_parts, value_parts = ([], [], [], [])
    for group_index in range(group_count):
        query_part = columns(queries, group_index, 0)
        key_part = columns(all_keys, group_index, 0)
        value_part = columns(all_keys, group_index, model_width)
        weights, weights_low, mixed_part = forward_group(
            query_part, key_part, value_part, key_mask, scaling
        )
        mixed_parts.append(mixed_part)
        grads = backward_group(
            query_part,
            key_part,
            value_part,
            columns(grad_output, group_index, 0),
            mixed_part,
            weights,
            weights_low,
            scaling,
        )
        query_parts.append(grads[0])
        key_parts.append(grads[1])
        value_parts.append(grads[2])
    mixed_rows = jnp.concatenate(mixed_parts, axis=1)
    query_grad = jnp.concatenate(query_parts, axis=1).astype(jnp.bfloat16)
    grads_all = jnp.concatenate(
        [jnp.concatenate(key_parts, axis=1), jnp.concatenate(value_parts, axis=1)], axis=1
    )
    grad_total = grads_all[:block_rows]
    partner_terms = [
        grads_all[(1 + level) * block_rows : (2 + level) * block_rows]
        for level in range(len(distances))
    ]
    extra_terms = grads_all[(1 + len(distances)) * block_rows :]
    for level, distance in enumerate(distances):
        returned = from_behind(partner_terms[level].astype(jnp.bfloat16), "tm", -distance)
        grad_total = grad_total + returned.astype(jnp.float32)
    extra_back = lax.all_to_all(
        extra_terms.astype(jnp.bfloat16), "tm", split_axis=0, concat_axis=0, tiled=True
    )
    sub_ids = jnp.arange(per_block, dtype=jnp.int32)
    one_hot = (
        (send_index.reshape(-1)[None, :] == sub_ids[:, None]) & send_valid.reshape(-1)[None, :]
    ).astype(jnp.bfloat16)
    folded = jnp.dot(
        one_hot,
        extra_back.reshape(devices * CAP, SUB * 2 * model_width),
        preferred_element_type=jnp.float32,
    )
    grad_total = grad_total + folded.reshape(block_rows, 2 * model_width)
    key_grad = grad_total[:, :model_width].astype(jnp.bfloat16)
    value_grad = grad_total[:, model_width:].astype(jnp.bfloat16)
    return (mixed_rows, query_grad, key_grad, value_grad)


def nn(a, b):
    return lax.dot_general(a, b, (((1,), (0,)), ((), ())), preferred_element_type=jnp.float32)


def tn(a, b):
    return lax.dot_general(a, b, (((0,), (0,)), ((), ())), preferred_element_type=jnp.float32)


def by_eights(x, op):
    parts = [x[i : i + 8] for i in range(0, x.shape[0], 8)]
    while len(parts) > 1:
        parts = [op(*parts[i : i + 2]) if i + 1 < len(parts) else parts[i] for i in range(0, len(parts), 2)]
    return parts[0]


class Block:
    def __init__(self, b, partners, rows, first_query, queries, table, kv, block, scores, gathered, dacc):
        self.kv, self.scores, self.gathered, self.dacc, self.table, self.b = kv, scores, gathered, dacc, table, b
        self.queries = queries
        entries = table.shape[1]
        width = 2 * HD
        scaling = 1.0 / math.sqrt(HD)
        lane = lax.broadcasted_iota(jnp.int32, block.shape, 1)
        zero = jnp.zeros_like(block)
        self.q_part = jnp.where(lane < HD, block * CAST(scaling), zero)
        self.g_part = jnp.where(lane < HD, zero, block)
        self.block_t = jnp.transpose(block.astype(jnp.float32))
        row_t = lax.broadcasted_iota(jnp.int32, (width, queries), 0)
        self.q_t = jnp.where(row_t < HD, self.block_t * scaling, 0.0).astype(CAST)
        self.g_t = jnp.where(row_t < HD, 0.0, self.block_t).astype(CAST)
        self.chunks = []
        if first_query:
            self.chunks.append((b, 0, first_query, "all"))
        self.chunks.append((b, first_query, queries, "own"))
        for p in range(partners):
            self.chunks.append((b - (1 << p), 0, rows, "all"))
        self.extra_places = []
        if partners:
            self.live = jnp.int32(0)
            for e in range(entries):
                entry = table[b, e]
                self.live = self.live + (entry >= 0).astype(jnp.int32)
                entry = jnp.maximum(entry, 0)
                place = (entry // (rows // SUB), pl.multiple_of(entry % (rows // SUB) * SUB, SUB))
                self.extra_places.append(place)
                gathered[e * SUB : (e + 1) * SUB, :] = kv[place[0], pl.ds(place[1], SUB), :]
            self.chunks.append((None, 0, entries * SUB, "extra"))
        self.places = []
        at = 0
        for chunk in self.chunks:
            self.places.append(slice(at, at + chunk[2]))
            at += chunk[2]

    def keys(self, chunk):
        block, first, count, kind = chunk
        if kind == "extra":
            return self.gathered[...]
        return self.kv[block, first : first + count, :]

    def score(self):
        peak = jnp.full((8, self.queries), LOWEST, jnp.float32)
        for chunk, place in zip(self.chunks, self.places):
            s = nn(self.keys(chunk), self.q_t)
            row = lax.broadcasted_iota(jnp.int32, s.shape, 0)
            if chunk[3] == "own":
                s = jnp.where(row <= lax.broadcasted_iota(jnp.int32, s.shape, 1), s, LOWEST)
            if chunk[3] == "extra":
                s = jnp.where(row < self.live * SUB, s, LOWEST)
            self.scores[place, :] = s
            peak = jnp.maximum(peak, by_eights(s, jnp.maximum))
        self.top = jnp.max(peak, axis=0, keepdims=True)

    def mix(self):
        total = jnp.zeros((8, self.queries), jnp.float32)
        mixed = jnp.zeros((HD, self.queries), jnp.float32)
        for chunk, place in zip(self.chunks, self.places):
            w = jnp.exp(self.scores[place, :] - self.top)
            total = total + by_eights(w, jnp.add)
            mixed = mixed + tn(self.keys(chunk), w.astype(CAST))[HD:]
        total = jnp.sum(total, axis=0, keepdims=True)
        self.mixed = mixed / total
        low = self.mixed.astype(CAST).astype(jnp.float32)
        self.delta = jnp.sum(self.block_t[HD:] * low, axis=0, keepdims=True)
        self.norm = self.top + jnp.log(total)

    def grads(self):
        query_grad = jnp.zeros((HD, self.queries), jnp.float32)
        for chunk, place in zip(self.chunks, self.places):
            keys = self.keys(chunk)
            w = jnp.exp(self.scores[place, :] - self.norm)
            sg = (w * (nn(keys, self.g_t) - self.delta)).astype(CAST)
            query_grad = query_grad + tn(keys, sg)[:HD]
            part = nn(sg, self.q_part) + nn(w.astype(CAST), self.g_part)
            block, first, count, kind = chunk
            if kind == "extra":
                for e, (owner, at) in enumerate(self.extra_places):
                    self.dacc[owner, pl.ds(at, SUB), :] += part[e * SUB : (e + 1) * SUB]
            else:
                self.dacc[block, first : first + count, :] += part
        return jnp.transpose(jnp.concatenate([query_grad * (1.0 / math.sqrt(HD)), self.mixed], axis=0)).astype(CAST)


def attention_kernel(rows, first_query, queries, query_at, last, together, *refs):
    if first_query:
        table, kv, qd, before, out, dacc, scores, gathered = refs
        dacc[...] = before[...]
    else:
        table, kv, qd, out, dacc, scores, gathered = refs
        dacc[...] = jnp.zeros_like(dacc)
    blocks = kv.shape[0]
    levels = (blocks - 1).bit_length()
    out_at = rows if last else 0

    def run(partners, ids):
        work = [
            Block(b, partners, rows, first_query, queries, table, kv, qd[b, query_at : query_at + queries, :],
                  scores.at[i], gathered.at[i], dacc)
            for i, b in enumerate(ids)
        ]
        for w in work:
            w.score()
        for w in work:
            w.mix()
        for w in work:
            out[w.b, out_at : out_at + queries, :] = w.grads()
        if last:
            for w in work:
                out[w.b, :rows, :] = dacc[w.b].astype(CAST)

    for partners in range(levels, -1, -1):
        low = (1 << partners) >> 1
        high = min(1 << partners, blocks)
        group = math.gcd(together, high - low)

        def step(i, carry, partners=partners, high=high, group=group):
            run(partners, [high - 1 - i * group - j for j in range(group)])
            return carry

        if high - low > group:
            lax.fori_loop(0, (high - low) // group, step, 0)
        else:
            run(partners, [jnp.int32(high - 1 - j) for j in range(group)])


def attention(table, kv, qd, before, rows, first_query, queries, query_at, last, together=None):
    together = TOGETHER if together is None else together
    blocks, _, width = kv.shape
    entries = table.shape[1]
    levels = (blocks - 1).bit_length()
    whole = pl.BlockSpec(memory_space=pltpu.VMEM)
    sums = jax.ShapeDtypeStruct((blocks, rows, width), jnp.float32)
    if last:
        out_shape = jax.ShapeDtypeStruct((blocks, rows + queries, width), CAST)
        out_specs = whole
    else:
        out_shape = (jax.ShapeDtypeStruct((blocks, queries, width), CAST), sums)
        out_specs = (whole, whole)
    inputs = (table, kv, qd) + ((before,) if first_query else ())
    list_rows = first_query + queries + levels * rows + entries * SUB
    scratch = [
        pltpu.VMEM((together, list_rows, queries), jnp.float32),
        pltpu.VMEM((together, entries * SUB, width), CAST),
    ]
    if last:
        scratch = [pltpu.VMEM((blocks, rows, width), jnp.float32)] + scratch
    pairs = blocks * (levels + 1) * rows * queries
    return pl.pallas_call(
        functools.partial(attention_kernel, rows, first_query, queries, query_at, last, together),
        out_shape=out_shape,
        in_specs=[pl.BlockSpec(memory_space=pltpu.SMEM)] + [whole] * (len(inputs) - 1),
        out_specs=out_specs,
        scratch_shapes=scratch,
        cost_estimate=pl.CostEstimate(flops=pairs * HD * 2 * 6 * 4, transcendentals=2 * pairs, bytes_accessed=8 << 20),
        compiler_params=pltpu.CompilerParams(vmem_limit_bytes=56 * 1024 * 1024),
    )(*inputs)


def swap(x):
    return jnp.concatenate([x[:, HD:], x[:, :HD]], axis=1)


def interleave(first, second):
    lane = lax.broadcasted_iota(jnp.int32, first.shape, 1)
    return jnp.where(lane < HD, first, swap(second)), jnp.where(lane < HD, swap(first), second)


def pack_kernel(heads, pieces, *refs):
    inputs, out = refs[:-1], refs[-1]
    at = 0
    for first, second, low, count in pieces:
        for pair in range(heads // 2):
            lanes = slice(pair * 2 * HD, (pair + 1) * 2 * HD)
            both = interleave(inputs[first][low : low + count, lanes], inputs[second][low : low + count, lanes])
            out[2 * pair, at : at + count, :] = both[0]
            out[2 * pair + 1, at : at + count, :] = both[1]
        at += count


def pack(arrays, pieces):
    heads = arrays[0].shape[1] // HD
    total = sum(piece[3] for piece in pieces)
    whole = pl.BlockSpec(memory_space=pltpu.VMEM)
    return pl.pallas_call(
        functools.partial(pack_kernel, heads, pieces),
        out_shape=jax.ShapeDtypeStruct((heads, total, 2 * HD), CAST),
        in_specs=[whole] * len(arrays),
        out_specs=whole,
        cost_estimate=pl.CostEstimate(flops=0, transcendentals=0, bytes_accessed=8 * total * heads * HD),
    )(*arrays)


def unpack_kernel(heads, rows, early, late, mixed, query_grad, key_grad, value_grad):
    half = early.shape[1]
    for pair in range(heads // 2):
        lanes = slice(pair * 2 * HD, (pair + 1) * 2 * HD)
        query_grad[:half, lanes], mixed[:half, lanes] = interleave(early[2 * pair], early[2 * pair + 1])
        query_grad[half:, lanes], mixed[half:, lanes] = interleave(late[2 * pair, rows:], late[2 * pair + 1, rows:])
        key_grad[:, lanes], value_grad[:, lanes] = interleave(late[2 * pair, :rows], late[2 * pair + 1, :rows])


def unpack(early, late, rows):
    heads = early.shape[0]
    whole = pl.BlockSpec(memory_space=pltpu.VMEM)
    return pl.pallas_call(
        functools.partial(unpack_kernel, heads, rows),
        out_shape=(jax.ShapeDtypeStruct((rows, heads * HD), CAST),) * 4,
        in_specs=[whole] * 2,
        out_specs=(whole,) * 4,
    )(early, late)


def by_heads(packed):
    return lax.all_to_all(packed, "tm", split_axis=0, concat_axis=0, tiled=True)


def head_plan(queries, key_rows, value_rows, grad_output, extra_blocks):
    rows = queries.shape[0]
    half = rows // 2
    early = by_heads(
        pack((key_rows, value_rows, queries, grad_output), ((0, 1, 0, rows), (2, 3, 0, half)))
    )
    late_packed = pack((queries, grad_output), ((0, 1, half, half),))
    early, late_packed = lax.optimization_barrier((early, late_packed))
    late = by_heads(late_packed)
    early_rows, sums = attention(extra_blocks, early, early, None, rows, 0, half, rows, False)
    early_back = by_heads(early_rows)
    late_rows = attention(extra_blocks, early, late, sums, rows, half, half, 0, True)
    late_back = by_heads(late_rows)
    return unpack(early_back, late_back, rows)


def local(queries, key_rows, value_rows, grad_output, extra_blocks):
    if lax.axis_size("tm") == queries.shape[1] // HD:
        return head_plan(queries, key_rows, value_rows, grad_output, extra_blocks)
    return block_plan(queries, key_rows, value_rows, grad_output, extra_blocks)


def solution(mesh):
    placed = (
        P(("member", "tm"), None),
        P(("member", "tm"), None),
        P(("member", "tm"), None),
        P(("member", "tm"), None),
        P("member", None),
    )
    return jax.shard_map(
        local,
        mesh=mesh,
        in_specs=placed,
        out_specs=(
            P(("member", "tm"), None),
            P(("member", "tm"), None),
            P(("member", "tm"), None),
            P(("member", "tm"), None),
        ),
        check_vma=False,
    )
```

profile of v0, /device:TPU:0, one launch (start us, length us, event | category | flops | bytes accessed | tf_op | source)
XLA Modules:
  0.0 138.2 jit_solution(1303415625264332326)
XLA Ops:
  0.6 3.1 %shard_map.84 = bf16[8,768,128]{2,1,0:T(8,128)(2,1)} custom-call(bf16[512,512]{1,0:T(8,128)(2,1)} %refs_0_.4, bf16[512,512]{1,0:T(8,128)(2,1)} %refs_1_.2, bf16[512,512]{1,0:T(8,128)(2,1)} %refs_0_.5, bf16[512,512]{1,0:T(8,128)(2,1)} %refs_1_.3), custom_call_target="tpu_custom_call" | custom-call | bytes 3145728 | tf_op jit(solution)/shard_map/pallas_call | solution.py:394
  3.8 7.3 %all-to-all-start = ((bf16[8,768,128]{2,1,0:T(8,128)(2,1)}), bf16[8,768,128]{2,1,0:T(8,128)(2,1)S(1)}, u32[]{:S(2)}, u32[]{:S(2)}) async-start(bf16[8,768,128]{2,1,0:T(8,128)(2,1)} %shard_map.84), calls=%async_computation | async-start | bytes 3145728 | tf_op jit(solution)/shard_map/all_to_all | solution.py:424
  11.0 2.2 %shard_map.85 = bf16[8,256,128]{2,1,0:T(8,128)(2,1)} custom-call(bf16[512,512]{1,0:T(8,128)(2,1)} %refs_0_.5, bf16[512,512]{1,0:T(8,128)(2,1)} %refs_1_.3), custom_call_target="tpu_custom_call" | custom-call | bytes 1048576 | tf_op jit(solution)/shard_map/pallas_call | solution.py:394
  13.2 34.8 %all-to-all-done.refs_1_.refs_2_ = bf16[8,768,128]{2,1,0:T(8,128)(2,1)S(1)} async-done(((bf16[8,768,128]{2,1,0:T(8,128)(2,1)}), bf16[8,768,128]{2,1,0:T(8,128)(2,1)S(1)}, u32[]{:S(2)}, u32[]{:S(2)}) %all-to-all-start) | async-done | bytes 1572896 | tf_op jit(solution)/shard_map/all_to_all | solution.py:424
  48.1 0.0 copy-start.1
  48.1 3.6 %all-to-all-start.2 = ((bf16[8,256,128]{2,1,0:T(8,128)(2,1)}), bf16[8,256,128]{2,1,0:T(8,128)(2,1)S(1)}, u32[]{:S(2)}, u32[]{:S(2)}) async-start(bf16[8,256,128]{2,1,0:T(8,128)(2,1)} %shard_map.85), calls=%async_computation.2 | async-start | bytes 1048576 | tf_op jit(solution)/shard_map/all_to_all | solution.py:424
  51.7 0.0 copy-done.1
  51.7 16.0 %shard_map.86 = (bf16[8,256,128]{2,1,0:T(8,128)(2,1)}, f32[8,512,128]{2,1,0:T(8,128)}) custom-call(s32[8,16]{1,0:T(8,128)} %refs_0_.7, bf16[8,768,128]{2,1,0:T(8,128)(2,1)} %copy-done.1, bf16[8,768,128]{2,1,0:T(8,128)(2,1)} %copy-done.1), custom_call_target="tpu_custom_call" | custom-call | flops 12884901888 | bytes 8388608 | tf_op jit(solution)/shard_map/pallas_call | solution.py:358
  67.7 0.0 all-to-all-done.2.refs_2_
  67.7 0.0 copy-start.2
  67.7 6.0 %all-to-all-start.1 = ((bf16[8,256,128]{2,1,0:T(8,128)(2,1)}), bf16[8,256,128]{2,1,0:T(8,128)(2,1)S(1)}, u32[]{:S(2)}, u32[]{:S(2)}) async-start(bf16[8,256,128]{2,1,0:T(8,128)(2,1)} %get-tuple-element.9), calls=%async_computation.1 | async-start | bytes 1048576 | tf_op jit(solution)/shard_map/all_to_all | solution.py:424
  73.7 0.0 copy-done.2
  73.7 18.9 %shard_map.87 = bf16[8,768,128]{2,1,0:T(8,128)(2,1)} custom-call(s32[8,16]{1,0:T(8,128)} %refs_0_.7, bf16[8,768,128]{2,1,0:T(8,128)(2,1)} %copy-done.1, bf16[8,256,128]{2,1,0:T(8,128)(2,1)} %copy-done.2, f32[8,512,128]{2,1,0:T(8,128)} %get-tuple-element.11.refs_3_), custom_call_target="tpu_custom_call" | custom-call | flops 12884901888 | bytes 8388608 | tf_op jit(solution)/shard_map/pallas_call | solution.py:358
  92.6 0.0 all-to-all-done.1.early
  92.6 0.0 copy-start
  92.6 42.2 %all_to_all.20.late = bf16[8,768,128]{2,1,0:T(8,128)(2,1)} all-to-all(bf16[8,768,128]{2,1,0:T(8,128)(2,1)} %shard_map.87), channel_id=1, replica_groups=mesh['tm'=8,'member'=4] {'tm'}, dimensions={0} | all-to-all | bytes 3145728 | tf_op jit(solution)/shard_map/all_to_all | solution.py:424
  134.8 0.0 copy-done
  134.8 3.4 %shard_map.88 = (bf16[512,512]{1,0:T(8,128)(2,1)}, bf16[512,512]{1,0:T(8,128)(2,1)}, bf16[512,512]{1,0:T(8,128)(2,1)}, bf16[512,512]{1,0:T(8,128)(2,1)}) custom-call(bf16[8,256,128]{2,1,0:T(8,128)(2,1)} %copy-done, bf16[8,768,128]{2,1,0:T(8,128)(2,1)} %all_to_all.20.late), custom_call_target="tpu_custom_call" | custom-call | tf_op jit(solution)/shard_map/pallas_call | solution.py:415
Async XLA Ops:
  3.8 44.3 %all-to-all-start = ((bf16[8,768,128]{2,1,0:T(8,128)(2,1)}), bf16[8,768,128]{2,1,0:T(8,128)(2,1)S(1)}, u32[]{:S(2)}, u32[]{:S(2)}) async-start(bf16[8,768,128]{2,1,0:T(8,128)(2,1)} %shard_map.84), calls=%async_computation | async-start | bytes 3145728 | tf_op jit(solution)/shard_map/all_to_all | solution.py:424
  48.1 3.6 %copy-start.1 = (bf16[8,768,128]{2,1,0:T(8,128)(2,1)}, bf16[8,768,128]{2,1,0:T(8,128)(2,1)S(1)}, u32[]{:S(2)}) copy-start(bf16[8,768,128]{2,1,0:T(8,128)(2,1)S(1)} %all-to-all-done.refs_1_.refs_2_) | copy-start | bytes 4718596
  48.1 19.6 %all-to-all-start.2 = ((bf16[8,256,128]{2,1,0:T(8,128)(2,1)}), bf16[8,256,128]{2,1,0:T(8,128)(2,1)S(1)}, u32[]{:S(2)}, u32[]{:S(2)}) async-start(bf16[8,256,128]{2,1,0:T(8,128)(2,1)} %shard_map.85), calls=%async_computation.2 | async-start | bytes 1048576 | tf_op jit(solution)/shard_map/all_to_all | solution.py:424
  67.7 6.0 %copy-start.2 = (bf16[8,256,128]{2,1,0:T(8,128)(2,1)}, bf16[8,256,128]{2,1,0:T(8,128)(2,1)S(1)}, u32[]{:S(2)}) copy-start(bf16[8,256,128]{2,1,0:T(8,128)(2,1)S(1)} %all-to-all-done.2.refs_2_) | copy-start | bytes 1572868
  67.7 24.9 %all-to-all-start.1 = ((bf16[8,256,128]{2,1,0:T(8,128)(2,1)}), bf16[8,256,128]{2,1,0:T(8,128)(2,1)S(1)}, u32[]{:S(2)}, u32[]{:S(2)}) async-start(bf16[8,256,128]{2,1,0:T(8,128)(2,1)} %get-tuple-element.9), calls=%async_computation.1 | async-start | bytes 1048576 | tf_op jit(solution)/shard_map/all_to_all | solution.py:424
  92.6 42.2 %copy-start = (bf16[8,256,128]{2,1,0:T(8,128)(2,1)}, bf16[8,256,128]{2,1,0:T(8,128)(2,1)S(1)}, u32[]{:S(2)}) copy-start(bf16[8,256,128]{2,1,0:T(8,128)(2,1)S(1)} %all-to-all-done.1.early) | copy-start | bytes 1572868
where the time goes:
time: 139 us; the launch traced here: 138 us
  Pallas kernels  43.6 us (31%)
  blocking collectives  42.2 us (30%)
  waiting for transfers between devices  34.8 us (25%)
  starting transfers between devices  16.9 us (12%)
    all_to_all x1, blocking collectives, by_heads(): return lax.all_to_all(packed, 'tm', split_axis=0, concat_axis=0, tiled=True)  42.2 us
    pallas_call x2, Pallas kernels, attention(): pl.pallas_call(functools.partial(attention_kernel, rows, first_query, que...  34.9 us
    all_to_all x3, waiting for transfers between devices, by_heads(): return lax.all_to_all(packed, 'tm', split_axis=0, concat_axis=0, tiled=True)  34.8 us
    all_to_all x3, starting transfers between devices, by_heads(): return lax.all_to_all(packed, 'tm', split_axis=0, concat_axis=0, tiled=True)  16.9 us
    pallas_call x2, Pallas kernels, pack(): pl.pallas_call(functools.partial(pack_kernel, heads, pieces), out_shape=j...  5.33 us
    pallas_call x1, Pallas kernels, unpack(): pl.pallas_call(functools.partial(unpack_kernel, heads, rows), out_shape=(...  3.41 us
  transfers between devices with their start and end apart: 3, of which 1 were waited for; matrix products, arithmetic and copies ran while one was open for 0% of the time, Pallas kernels for 27%

commit v1 on v0

--- a/solution.py
+++ b/solution.py
@@ -193,10 +193,6 @@
     return lax.dot_general(a, b, (((1,), (0,)), ((), ())), preferred_element_type=jnp.float32)
 
 
-def tn(a, b):
-    return lax.dot_general(a, b, (((0,), (0,)), ((), ())), preferred_element_type=jnp.float32)
-
-
 def by_eights(x, op):
     parts = [x[i : i + 8] for i in range(0, x.shape[0], 8)]
     while len(parts) > 1:
@@ -204,17 +200,22 @@
     return parts[0]
 
 
+def wrapped(i, count):
+    return jnp.where(i < 0, i + count, jnp.where(i >= count, i - count, i))
+
+
 class Block:
-    def __init__(self, b, partners, rows, first_query, queries, table, kv, block, scores, gathered, dacc):
-        self.kv, self.scores, self.gathered, self.dacc, self.table, self.b = kv, scores, gathered, dacc, table, b
-        self.queries = queries
-        entries = table.shape[1]
+    def __init__(self, b, partners, rows, first_query, table, kv, kv_t, block, scores, gathered, sg, wl, dacc):
+        self.kv, self.kv_t, self.scores, self.gathered, self.dacc, self.b = kv, kv_t, scores, gathered, dacc, b
+        self.sg, self.wl = sg, wl
+        self.queries = queries = block.shape[0]
         width = 2 * HD
         scaling = 1.0 / math.sqrt(HD)
         lane = lax.broadcasted_iota(jnp.int32, block.shape, 1)
         zero = jnp.zeros_like(block)
-        self.q_part = jnp.where(lane < HD, block * CAST(scaling), zero)
-        self.g_part = jnp.where(lane < HD, zero, block)
+        q_part = jnp.where(lane < HD, block * CAST(scaling), zero)
+        g_part = jnp.where(lane < HD, zero, block)
+        self.qg_part = jnp.concatenate([q_part, g_part], axis=0)
         self.block_t = jnp.transpose(block.astype(jnp.float32))
         row_t = lax.broadcasted_iota(jnp.int32, (width, queries), 0)
         self.q_t = jnp.where(row_t < HD, self.block_t * scaling, 0.0).astype(CAST)
@@ -226,6 +227,7 @@
         for p in range(partners):
             self.chunks.append((b - (1 << p), 0, rows, "all"))
         self.extra_places = []
+        entries = min(table.shape[1], CAP * ((1 << partners) - 1))
         if partners:
             self.live = jnp.int32(0)
             for e in range(entries):
@@ -235,6 +237,7 @@
                 place = (entry // (rows // SUB), pl.multiple_of(entry % (rows // SUB) * SUB, SUB))
                 self.extra_places.append(place)
                 gathered[e * SUB : (e + 1) * SUB, :] = kv[place[0], pl.ds(place[1], SUB), :]
+            self.gathered_t = jnp.transpose(gathered[: entries * SUB, :].astype(jnp.float32)).astype(CAST)
             self.chunks.append((None, 0, entries * SUB, "extra"))
         self.places = []
         at = 0
@@ -245,8 +248,14 @@
     def keys(self, chunk):
         block, first, count, kind = chunk
         if kind == "extra":
-            return self.gathered[...]
+            return self.gathered[:count, :]
         return self.kv[block, first : first + count, :]
+
+    def keys_t(self, chunk):
+        block, first, count, kind = chunk
+        if kind == "extra":
+            return self.gathered_t
+        return self.kv_t[block, :, first : first + count]
 
     def score(self):
         peak = jnp.full((8, self.queries), LOWEST, jnp.float32)
@@ -267,7 +276,7 @@
         for chunk, place in zip(self.chunks, self.places):
             w = jnp.exp(self.scores[place, :] - self.top)
             total = total + by_eights(w, jnp.add)
-            mixed = mixed + tn(self.keys(chunk), w.astype(CAST))[HD:]
+            mixed = mixed + nn(self.keys_t(chunk)[HD:], w.astype(CAST))
         total = jnp.sum(total, axis=0, keepdims=True)
         self.mixed = mixed / total
         low = self.mixed.astype(CAST).astype(jnp.float32)
@@ -277,11 +286,13 @@
     def grads(self):
         query_grad = jnp.zeros((HD, self.queries), jnp.float32)
         for chunk, place in zip(self.chunks, self.places):
-            keys = self.keys(chunk)
             w = jnp.exp(self.scores[place, :] - self.norm)
-            sg = (w * (nn(keys, self.g_t) - self.delta)).astype(CAST)
-            query_grad = query_grad + tn(keys, sg)[:HD]
-            part = nn(sg, self.q_part) + nn(w.astype(CAST), self.g_part)
+            self.sg[place, :] = (w * (nn(self.keys(chunk), self.g_t) - self.delta)).astype(CAST)
+            self.wl[place, :] = w.astype(CAST)
+        for chunk, place in zip(self.chunks, self.places):
+            sg = self.sg[place, :]
+            query_grad = query_grad + nn(self.keys_t(chunk)[:HD], sg)
+            part = nn(jnp.concatenate([sg, self.wl[place, :]], axis=1), self.qg_part)
             block, first, count, kind = chunk
             if kind == "extra":
                 for e, (owner, at) in enumerate(self.extra_places):
@@ -291,21 +302,39 @@
         return jnp.transpose(jnp.concatenate([query_grad * (1.0 / math.sqrt(HD)), self.mixed], axis=0)).astype(CAST)
 
 
-def attention_kernel(rows, first_query, queries, query_at, last, together, *refs):
-    if first_query:
-        table, kv, qd, before, out, dacc, scores, gathered = refs
+def attention_kernel(blocks, rows, first_query, queries, together, *refs):
+    last = first_query + queries == rows
+    refs = list(refs)
+
+    def take(n):
+        got = refs[:n]
+        del refs[:n]
+        return got
+
+    me_ref, table = take(2)
+    early = take(blocks)
+    me = me_ref[0]
+    if last:
+        qd, before = take(2)
+        out = take(blocks)
+        kv, kv_t, scores, gathered, sg, wl, dacc, oq = take(8)
         dacc[...] = before[...]
     else:
-        table, kv, qd, out, dacc, scores, gathered = refs
+        oq, dacc, kv, kv_t, scores, gathered, sg, wl, qd = take(9)
         dacc[...] = jnp.zeros_like(dacc)
-    blocks = kv.shape[0]
+    for k in range(blocks):
+        b = wrapped(me - k, blocks)
+        keys = early[k][:rows, :]
+        kv[b] = keys
+        kv_t[b] = jnp.transpose(keys.astype(jnp.float32)).astype(CAST)
+        if not last:
+            qd[b] = early[k][rows:, :]
     levels = (blocks - 1).bit_length()
-    out_at = rows if last else 0
 
     def run(partners, ids):
         work = [
-            Block(b, partners, rows, first_query, queries, table, kv, qd[b, query_at : query_at + queries, :],
-                  scores.at[i], gathered.at[i], dacc)
+            Block(b, partners, rows, first_query, table, kv, kv_t, qd[b], scores.at[i], gathered.at[i], sg.at[i],
+                  wl.at[i], dacc)
             for i, b in enumerate(ids)
         ]
         for w in work:
@@ -313,10 +342,7 @@
         for w in work:
             w.mix()
         for w in work:
-            out[w.b, out_at : out_at + queries, :] = w.grads()
-        if last:
-            for w in work:
-                out[w.b, :rows, :] = dacc[w.b].astype(CAST)
+            oq[w.b] = w.grads()
 
     for partners in range(levels, -1, -1):
         low = (1 << partners) >> 1
@@ -331,35 +357,48 @@
             lax.fori_loop(0, (high - low) // group, step, 0)
         else:
             run(partners, [jnp.int32(high - 1 - j) for j in range(group)])
-
-
-def attention(table, kv, qd, before, rows, first_query, queries, query_at, last, together=None):
+    if last:
+        for k in range(blocks):
+            b = wrapped(me + k, blocks)
+            out[k][:rows, :] = dacc[b].astype(CAST)
+            out[k][rows:, :] = oq[b]
+
+
+def attention(me, table, early, late, before, rows, first_query, queries, together=None):
     together = TOGETHER if together is None else together
-    blocks, _, width = kv.shape
+    blocks = len(early)
+    width = early[0].shape[1]
     entries = table.shape[1]
     levels = (blocks - 1).bit_length()
+    last = first_query + queries == rows
     whole = pl.BlockSpec(memory_space=pltpu.VMEM)
-    sums = jax.ShapeDtypeStruct((blocks, rows, width), jnp.float32)
+    small = pl.BlockSpec(memory_space=pltpu.SMEM)
+    sums = (blocks, rows, width)
     if last:
-        out_shape = jax.ShapeDtypeStruct((blocks, rows + queries, width), CAST)
-        out_specs = whole
+        out_shape = [jax.ShapeDtypeStruct((rows + queries, width), CAST)] * blocks
+        inputs = [me, table] + list(early) + [late, before]
     else:
-        out_shape = (jax.ShapeDtypeStruct((blocks, queries, width), CAST), sums)
-        out_specs = (whole, whole)
-    inputs = (table, kv, qd) + ((before,) if first_query else ())
-    list_rows = first_query + queries + levels * rows + entries * SUB
+        out_shape = [jax.ShapeDtypeStruct((blocks, queries, width), CAST), jax.ShapeDtypeStruct(sums, jnp.float32)]
+        inputs = [me, table] + list(early)
+    extra_rows = min(entries, CAP * ((1 << levels) - 1)) * SUB
+    list_rows = first_query + queries + levels * rows + extra_rows
     scratch = [
+        pltpu.VMEM((blocks, rows, width), CAST),
+        pltpu.VMEM((blocks, width, rows), CAST),
         pltpu.VMEM((together, list_rows, queries), jnp.float32),
-        pltpu.VMEM((together, entries * SUB, width), CAST),
+        pltpu.VMEM((together, extra_rows, width), CAST),
+        pltpu.VMEM((together, list_rows, queries), CAST),
+        pltpu.VMEM((together, list_rows, queries), CAST),
     ]
     if last:
-        scratch = [pltpu.VMEM((blocks, rows, width), jnp.float32)] + scratch
+        scratch.append(pltpu.VMEM(sums, jnp.float32))
+    scratch.append(pltpu.VMEM((blocks, queries, width), CAST))
     pairs = blocks * (levels + 1) * rows * queries
     return pl.pallas_call(
-        functools.partial(attention_kernel, rows, first_query, queries, query_at, last, together),
-        out_shape=out_shape,
-        in_specs=[pl.BlockSpec(memory_space=pltpu.SMEM)] + [whole] * (len(inputs) - 1),
-        out_specs=out_specs,
+        functools.partial(attention_kernel, blocks, rows, first_query, queries, together),
+        out_shape=tuple(out_shape),
+        in_specs=[small] * 2 + [whole] * (len(inputs) - 2),
+        out_specs=(whole,) * len(out_shape),
         scratch_shapes=scratch,
         cost_estimate=pl.CostEstimate(flops=pairs * HD * 2 * 6 * 4, transcendentals=2 * pairs, bytes_accessed=8 << 20),
         compiler_params=pltpu.CompilerParams(vmem_limit_bytes=56 * 1024 * 1024),
@@ -375,69 +414,97 @@
     return jnp.where(lane < HD, first, swap(second)), jnp.where(lane < HD, swap(first), second)
 
 
-def pack_kernel(heads, pieces, *refs):
-    inputs, out = refs[:-1], refs[-1]
-    at = 0
-    for first, second, low, count in pieces:
-        for pair in range(heads // 2):
-            lanes = slice(pair * 2 * HD, (pair + 1) * 2 * HD)
+def pack_kernel(heads, pieces, apart, *refs):
+    me = refs[0][0]
+    inputs = refs[1 : 1 + 1 + max(max(piece[:2]) for piece in pieces)]
+    packed = refs[-1]
+    for pair in range(heads // 2):
+        lanes = slice(pair * 2 * HD, (pair + 1) * 2 * HD)
+        at = 0
+        for first, second, low, count in pieces:
             both = interleave(inputs[first][low : low + count, lanes], inputs[second][low : low + count, lanes])
-            out[2 * pair, at : at + count, :] = both[0]
-            out[2 * pair + 1, at : at + count, :] = both[1]
-        at += count
-
-
-def pack(arrays, pieces):
+            packed[2 * pair, at : at + count, :] = both[0]
+            packed[2 * pair + 1, at : at + count, :] = both[1]
+            at += count
+    if apart:
+        for k, out in enumerate(refs[1 + len(inputs) : -1]):
+            out[...] = packed[wrapped(me + k, heads)]
+
+
+def pack(me, arrays, pieces, apart):
     heads = arrays[0].shape[1] // HD
     total = sum(piece[3] for piece in pieces)
     whole = pl.BlockSpec(memory_space=pltpu.VMEM)
+    all_heads = (heads, total, 2 * HD)
+    if apart:
+        out_shape = (jax.ShapeDtypeStruct((total, 2 * HD), CAST),) * heads
+        out_specs = (whole,) * heads
+        scratch = [pltpu.VMEM(all_heads, CAST)]
+    else:
+        out_shape, out_specs, scratch = jax.ShapeDtypeStruct(all_heads, CAST), whole, []
     return pl.pallas_call(
-        functools.partial(pack_kernel, heads, pieces),
-        out_shape=jax.ShapeDtypeStruct((heads, total, 2 * HD), CAST),
-        in_specs=[whole] * len(arrays),
-        out_specs=whole,
+        functools.partial(pack_kernel, heads, pieces, apart),
+        out_shape=out_shape,
+        in_specs=[pl.BlockSpec(memory_space=pltpu.SMEM)] + [whole] * len(arrays),
+        out_specs=out_specs,
+        scratch_shapes=scratch,
         cost_estimate=pl.CostEstimate(flops=0, transcendentals=0, bytes_accessed=8 * total * heads * HD),
-    )(*arrays)
-
-
-def unpack_kernel(heads, rows, early, late, mixed, query_grad, key_grad, value_grad):
+    )(me, *arrays)
+
+
+def unpack_kernel(heads, rows, *refs):
+    me = refs[0][0]
+    early, late = refs[1], refs[2 : 2 + heads]
+    mixed, query_grad, key_grad, value_grad, ordered = refs[2 + heads :]
+    for k in range(heads):
+        ordered[wrapped(me - k, heads)] = late[k][...]
     half = early.shape[1]
     for pair in range(heads // 2):
         lanes = slice(pair * 2 * HD, (pair + 1) * 2 * HD)
+        even, odd = ordered[2 * pair], ordered[2 * pair + 1]
         query_grad[:half, lanes], mixed[:half, lanes] = interleave(early[2 * pair], early[2 * pair + 1])
-        query_grad[half:, lanes], mixed[half:, lanes] = interleave(late[2 * pair, rows:], late[2 * pair + 1, rows:])
-        key_grad[:, lanes], value_grad[:, lanes] = interleave(late[2 * pair, :rows], late[2 * pair + 1, :rows])
-
-
-def unpack(early, late, rows):
-    heads = early.shape[0]
+        query_grad[half:, lanes], mixed[half:, lanes] = interleave(even[rows:], odd[rows:])
+        key_grad[:, lanes], value_grad[:, lanes] = interleave(even[:rows], odd[:rows])
+
+
+def unpack(me, early, late, rows):
+    heads = len(late)
     whole = pl.BlockSpec(memory_space=pltpu.VMEM)
     return pl.pallas_call(
         functools.partial(unpack_kernel, heads, rows),
         out_shape=(jax.ShapeDtypeStruct((rows, heads * HD), CAST),) * 4,
-        in_specs=[whole] * 2,
+        in_specs=[pl.BlockSpec(memory_space=pltpu.SMEM)] + [whole] * (1 + heads),
         out_specs=(whole,) * 4,
-    )(early, late)
-
-
-def by_heads(packed):
+        scratch_shapes=[pltpu.VMEM((heads,) + late[0].shape, CAST)],
+    )(me, early, *late)
+
+
+def shifted_all(pieces):
+    count = len(pieces)
+    return [pieces[0]] + [
+        lax.ppermute(pieces[k], "tm", [(i, (i + k) % count) for i in range(count)]) for k in range(1, count)
+    ]
+
+
+def all_heads(packed):
     return lax.all_to_all(packed, "tm", split_axis=0, concat_axis=0, tiled=True)
 
 
 def head_plan(queries, key_rows, value_rows, grad_output, extra_blocks):
     rows = queries.shape[0]
     half = rows // 2
-    early = by_heads(
-        pack((key_rows, value_rows, queries, grad_output), ((0, 1, 0, rows), (2, 3, 0, half)))
-    )
-    late_packed = pack((queries, grad_output), ((0, 1, half, half),))
-    early, late_packed = lax.optimization_barrier((early, late_packed))
-    late = by_heads(late_packed)
-    early_rows, sums = attention(extra_blocks, early, early, None, rows, 0, half, rows, False)
-    early_back = by_heads(early_rows)
-    late_rows = attention(extra_blocks, early, late, sums, rows, half, half, 0, True)
-    late_back = by_heads(late_rows)
-    return unpack(early_back, late_back, rows)
+    me = lax.axis_index("tm").astype(jnp.int32).reshape(1)
+    early = shifted_all(
+        pack(me, (key_rows, value_rows, queries, grad_output), ((0, 1, 0, rows), (2, 3, 0, half)), True)
+    )
+    late_packed = pack(me, (queries, grad_output), ((0, 1, half, half),), False)
+    *early, late_packed = lax.optimization_barrier((*early, late_packed))
+    late = all_heads(late_packed)
+    early_rows, sums = attention(me, extra_blocks, early, None, None, rows, 0, half)
+    early_back = all_heads(early_rows)
+    late_rows = attention(me, extra_blocks, early, late, sums, rows, half, half)
+    late_back = shifted_all(late_rows)
+    return unpack(me, early_back, late_back, rows)
 
 
 def local(queries, key_rows, value_rows, grad_output, extra_blocks):

time: 139 us -> 126 us (0.906)
  the two profiles are of different devices: /device:TPU:0 before, /device:TPU:12 now
where the time goes in v1:
time: 126 us; the launch traced here: 125 us
  waiting for transfers between devices  56.7 us (45%)
  Pallas kernels  40 us (32%)
  starting transfers between devices  27.1 us (22%)
    ppermute x14, waiting for transfers between devices, shifted_all(): lax.ppermute(pieces[k], 'tm', [(i, (i + k) % count) for i in range(count)])  56.7 us
    pallas_call x2, Pallas kernels, attention(): pl.pallas_call(functools.partial(attention_kernel, blocks, rows, first_qu...  31.1 us
    ppermute x14, starting transfers between devices, shifted_all(): lax.ppermute(pieces[k], 'tm', [(i, (i + k) % count) for i in range(count)])  15.8 us
    all_to_all x2, starting transfers between devices, all_heads(): return lax.all_to_all(packed, 'tm', split_axis=0, concat_axis=0, tiled=True)  11.3 us
    pallas_call x2, Pallas kernels, pack(): pl.pallas_call(functools.partial(pack_kernel, heads, pieces, apart), out_...  5.39 us
    pallas_call x1, Pallas kernels, unpack(): pl.pallas_call(functools.partial(unpack_kernel, heads, rows), out_shape=(...  3.53 us
  transfers between devices with their start and end apart: 16, of which 11 were waited for; matrix products, arithmetic and copies ran while one was open for 0% of the time, Pallas kernels for 27%

profile of v1, /device:TPU:12, one launch (start us, length us, event | category | flops | bytes accessed | tf_op | source)
XLA Modules:
  0.0 125.2 jit_solution(13218818410081796694)
XLA Ops:
  0.6 3.1 %shard_map.84 = (bf16[768,128]{1,0:T(8,128)(2,1)}, bf16[768,128]{1,0:T(8,128)(2,1)}, bf16[768,128]{1,0:T(8,128)(2,1)}, bf16[768,128]{1,0:T(8,128)(2,1)}, bf16[76...) custom-call(s32[1]{0:T(128)} %bitcast.refs_0_, ...), custom_call_target="tpu_custom_call" | custom-call | bytes 3145728 | tf_op jit(solution)/shard_map/pallas_call | solution.py:445
  3.8 1.5 %collective-permute-start = (bf16[768,128]{1,0:T(8,128)(2,1)}, bf16[768,128]{1,0:T(8,128)(2,1)S(1)}, u32[]{:S(2)}, u32[]{:S(2)}) collective-permute-start(bf16[768,128]{1,0:T(8,128)(2,1)} %get-tuple-element.32), channel_id=1, source_target_pairs={{0,4},{4,8},{8,12},{12,16},{16,20},{20,24},{24,28},{28,0},{1,5},{5... | collective-permute-start | bytes 589832 | tf_op jit(solution)/shard_map/ppermute | solution.py:485
  5.3 1.6 %collective-permute-start.1 = (bf16[768,128]{1,0:T(8,128)(2,1)}, bf16[768,128]{1,0:T(8,128)(2,1)S(1)}, u32[]{:S(2)}, u32[]{:S(2)}) collective-permute-start(bf16[768,128]{1,0:T(8,128)(2,1)} %get-tuple-element.33), channel_id=1, source_target_pairs={{0,8},{4,12},{8,16},{12,20},{16,24},{20,28},{24,0},{28,4},{1,9},{5... | collective-permute-start | bytes 589832 | tf_op jit(solution)/shard_map/ppermute | solution.py:485
  6.9 1.2 collective-permute-start.2
  8.0 1.7 %collective-permute-start.3 = (bf16[768,128]{1,0:T(8,128)(2,1)}, bf16[768,128]{1,0:T(8,128)(2,1)S(1)}, u32[]{:S(2)}, u32[]{:S(2)}) collective-permute-start(bf16[768,128]{1,0:T(8,128)(2,1)} %get-tuple-element.35), channel_id=1, source_target_pairs={{0,16},{4,20},{8,24},{12,28},{16,0},{20,4},{24,8},{28,12},{1,17},{... | collective-permute-start | bytes 589832 | tf_op jit(solution)/shard_map/ppermute | solution.py:485
  9.7 1.3 %collective-permute-start.4 = (bf16[768,128]{1,0:T(8,128)(2,1)}, bf16[768,128]{1,0:T(8,128)(2,1)S(1)}, u32[]{:S(2)}, u32[]{:S(2)}) collective-permute-start(bf16[768,128]{1,0:T(8,128)(2,1)} %get-tuple-element.36), channel_id=1, source_target_pairs={{0,20},{4,24},{8,28},{12,0},{16,4},{20,8},{24,12},{28,16},{1,21},{... | collective-permute-start | bytes 589832 | tf_op jit(solution)/shard_map/ppermute | solution.py:485
  11.0 0.0 collective-permute-done.refs_3_
  11.0 1.2 collective-permute-start.5
  12.2 19.7 %collective-permute-done.1.refs_4_ = bf16[768,128]{1,0:T(8,128)(2,1)S(1)} collective-permute-done((bf16[768,128]{1,0:T(8,128)(2,1)}, bf16[768,128]{1,0:T(8,128)(2,1)S(1)}, u32[]{:S(2)}, u32[]{:S(2)}) %collective-permute-start.1) | collective-permute-done | bytes 196640 | tf_op jit(solution)/shard_map/ppermute | solution.py:485
  32.0 0.0 collective-permute-start.6
  32.0 2.3 %shard_map.85 = bf16[8,256,128]{2,1,0:T(8,128)(2,1)} custom-call(s32[1]{0:T(128)} %bitcast.refs_0_, bf16[512,512]{1,0:T(8,128)(2,1)} %refs_1_.5, bf16[512,512]{1,0:T(8,128)(2,1)} %refs_2_.3), custom_call_target="tpu_custom_call" | custom-call | bytes 1048576 | tf_op jit(solution)/shard_map/pallas_call | solution.py:445
  34.2 1.9 %collective-permute-done.2.refs_5_ = bf16[768,128]{1,0:T(8,128)(2,1)S(1)} collective-permute-done((bf16[768,128]{1,0:T(8,128)(2,1)}, bf16[768,128]{1,0:T(8,128)(2,1)S(1)}, u32[]{:S(2)}, u32[]{:S(2)}) %collective-permute-start.2) | collective-permute-done | bytes 196640 | tf_op jit(solution)/shard_map/ppermute | solution.py:485
  36.2 3.1 %collective-permute-done.3.refs_6_ = bf16[768,128]{1,0:T(8,128)(2,1)S(1)} collective-permute-done((bf16[768,128]{1,0:T(8,128)(2,1)}, bf16[768,128]{1,0:T(8,128)(2,1)S(1)}, u32[]{:S(2)}, u32[]{:S(2)}) %collective-permute-start.3) | collective-permute-done | bytes 196640 | tf_op jit(solution)/shard_map/ppermute | solution.py:485
  39.3 0.0 collective-permute-done.4.refs_7_
  39.3 1.8 %collective-permute-done.5.refs_8_ = bf16[768,128]{1,0:T(8,128)(2,1)S(1)} collective-permute-done((bf16[768,128]{1,0:T(8,128)(2,1)}, bf16[768,128]{1,0:T(8,128)(2,1)S(1)}, u32[]{:S(2)}, u32[]{:S(2)}) %collective-permute-start.5) | collective-permute-done | bytes 196640 | tf_op jit(solution)/shard_map/ppermute | solution.py:485
  41.0 1.1 collective-permute-done.6.refs_9_
  42.1 5.3 %all-to-all-start.1 = ((bf16[8,256,128]{2,1,0:T(8,128)(2,1)}), bf16[8,256,128]{2,1,0:T(8,128)(2,1)S(1)}, u32[]{:S(2)}, u32[]{:S(2)}) async-start(bf16[8,256,128]{2,1,0:T(8,128)(2,1)} %shard_map.85), calls=%async_computation.1 | async-start | bytes 1048576 | tf_op jit(solution)/shard_map/all_to_all | solution.py:490
  47.4 0.0 copy-done.9
  47.4 0.0 copy-done.10
  47.4 0.0 copy-done.11
  47.5 0.0 copy-done.12
  47.5 0.0 copy-done.13
  47.5 0.0 copy-done.14
  47.5 0.0 copy-done.15
  47.5 14.5 %shard_map.86 = (bf16[8,256,128]{2,1,0:T(8,128)(2,1)}, f32[8,512,128]{2,1,0:T(8,128)}) custom-call(s32[1]{0:T(128)} %bitcast.refs_0_, s32[8,16]{1,0:T(8,128)} %refs_1_.7, bf16[768,128]{1,0:T(8,128)(2,1)} %get-tuple-element.39.refs_2_, bf16[768,128]{1,0:T(8,128)(2,1)} %copy-done.9, bf16[768,128]{1,0:T(8,128)(2,1)} %copy-done.10, bf16[768,128]{1,0:T(8,128)(2,1)} %copy-done.11, ...), custom_call_target="tpu_custom_call" | custom-call | flops 12884901888 | bytes 8388608 | tf_op jit(solution)/shard_map/pallas_call | solution.py:397
  62.0 0.0 all-to-all-done.1.refs_10_
  62.0 6.0 %all-to-all-start = ((bf16[8,256,128]{2,1,0:T(8,128)(2,1)}), bf16[8,256,128]{2,1,0:T(8,128)(2,1)S(1)}, u32[]{:S(2)}, u32[]{:S(2)}) async-start(bf16[8,256,128]{2,1,0:T(8,128)(2,1)} %get-tuple-element.47), calls=%async_computation | async-start | bytes 1048576 | tf_op jit(solution)/shard_map/all_to_all | solution.py:490
  68.0 0.0 copy-done.1
  68.1 16.5 %shard_map.87 = (bf16[768,128]{1,0:T(8,128)(2,1)}, bf16[768,128]{1,0:T(8,128)(2,1)}, bf16[768,128]{1,0:T(8,128)(2,1)}, bf16[768,128]{1,0:T(8,128)(2,1)}, bf16[76...) custom-call(s32[1]{0:T(128)} %bitcast.refs_0_, ...), custom_call_target="tpu_custom_call" | custom-call | flops 12884901888 | bytes 8388608 | tf_op jit(solution)/shard_map/pallas_call | solution.py:397
  84.6 1.5 %collective-permute-start.7 = (bf16[768,128]{1,0:T(8,128)(2,1)}, bf16[768,128]{1,0:T(8,128)(2,1)S(1)}, u32[]{:S(2)}, u32[]{:S(2)}) collective-permute-start(bf16[768,128]{1,0:T(8,128)(2,1)} %get-tuple-element.51), channel_id=1, source_target_pairs={{0,4},{4,8},{8,12},{12,16},{16,20},{20,24},{24,28},{28,0},{1,5},{5... | collective-permute-start | bytes 589832 | tf_op jit(solution)/shard_map/ppermute | solution.py:485
  86.1 1.4 %collective-permute-start.8 = (bf16[768,128]{1,0:T(8,128)(2,1)}, bf16[768,128]{1,0:T(8,128)(2,1)S(1)}, u32[]{:S(2)}, u32[]{:S(2)}) collective-permute-start(bf16[768,128]{1,0:T(8,128)(2,1)} %get-tuple-element.52), channel_id=1, source_target_pairs={{0,8},{4,12},{8,16},{12,20},{16,24},{20,28},{24,0},{28,4},{1,9},{5... | collective-permute-start | bytes 589832 | tf_op jit(solution)/shard_map/ppermute | solution.py:485
  87.5 1.5 %collective-permute-start.9 = (bf16[768,128]{1,0:T(8,128)(2,1)}, bf16[768,128]{1,0:T(8,128)(2,1)S(1)}, u32[]{:S(2)}, u32[]{:S(2)}) collective-permute-start(bf16[768,128]{1,0:T(8,128)(2,1)} %get-tuple-element.53), channel_id=1, source_target_pairs={{0,12},{4,16},{8,20},{12,24},{16,28},{20,0},{24,4},{28,8},{1,13},{... | collective-permute-start | bytes 589832 | tf_op jit(solution)/shard_map/ppermute | solution.py:485
  89.0 1.5 %collective-permute-start.10 = (bf16[768,128]{1,0:T(8,128)(2,1)}, bf16[768,128]{1,0:T(8,128)(2,1)S(1)}, u32[]{:S(2)}, u32[]{:S(2)}) collective-permute-start(bf16[768,128]{1,0:T(8,128)(2,1)} %get-tuple-element.54), channel_id=1, source_target_pairs={{0,16},{4,20},{8,24},{12,28},{16,0},{20,4},{24,8},{28,12},{1,17},{... | collective-permute-start | bytes 589832 | tf_op jit(solution)/shard_map/ppermute | solution.py:485
  90.4 1.5 %collective-permute-start.11 = (bf16[768,128]{1,0:T(8,128)(2,1)}, bf16[768,128]{1,0:T(8,128)(2,1)S(1)}, u32[]{:S(2)}, u32[]{:S(2)}) collective-permute-start(bf16[768,128]{1,0:T(8,128)(2,1)} %get-tuple-element.55), channel_id=1, source_target_pairs={{0,20},{4,24},{8,28},{12,0},{16,4},{20,8},{24,12},{28,16},{1,21},{... | collective-permute-start | bytes 589832 | tf_op jit(solution)/shard_map/ppermute | solution.py:485
  91.9 1.6 %collective-permute-done.7.refs_3_ = bf16[768,128]{1,0:T(8,128)(2,1)S(1)} collective-permute-done((bf16[768,128]{1,0:T(8,128)(2,1)}, bf16[768,128]{1,0:T(8,128)(2,1)S(1)}, u32[]{:S(2)}, u32[]{:S(2)}) %collective-permute-start.7) | collective-permute-done | bytes 196640 | tf_op jit(solution)/shard_map/ppermute | solution.py:485
  93.5 0.0 collective-permute-start.12
  93.5 19.3 %collective-permute-done.8.refs_4_ = bf16[768,128]{1,0:T(8,128)(2,1)S(1)} collective-permute-done((bf16[768,128]{1,0:T(8,128)(2,1)}, bf16[768,128]{1,0:T(8,128)(2,1)S(1)}, u32[]{:S(2)}, u32[]{:S(2)}) %collective-permute-start.8) | collective-permute-done | bytes 196640 | tf_op jit(solution)/shard_map/ppermute | solution.py:485
  112.8 0.0 collective-permute-start.13
  112.8 0.0 all-to-all-done.refs_1_
  112.8 3.1 %collective-permute-done.9.refs_5_ = bf16[768,128]{1,0:T(8,128)(2,1)S(1)} collective-permute-done((bf16[768,128]{1,0:T(8,128)(2,1)}, bf16[768,128]{1,0:T(8,128)(2,1)S(1)}, u32[]{:S(2)}, u32[]{:S(2)}) %collective-permute-start.9) | collective-permute-done | bytes 196640 | tf_op jit(solution)/shard_map/ppermute | solution.py:485
  115.9 2.1 %collective-permute-done.10.refs_6_ = bf16[768,128]{1,0:T(8,128)(2,1)S(1)} collective-permute-done((bf16[768,128]{1,0:T(8,128)(2,1)}, bf16[768,128]{1,0:T(8,128)(2,1)S(1)}, u32[]{:S(2)}, u32[]{:S(2)}) %collective-permute-start.10) | collective-permute-done | bytes 196640 | tf_op jit(solution)/shard_map/ppermute | solution.py:485
  118.0 0.0 collective-permute-done.11.refs_7_
  118.0 1.5 %collective-permute-done.12.refs_8_ = bf16[768,128]{1,0:T(8,128)(2,1)S(1)} collective-permute-done((bf16[768,128]{1,0:T(8,128)(2,1)}, bf16[768,128]{1,0:T(8,128)(2,1)S(1)}, u32[]{:S(2)}, u32[]{:S(2)}) %collective-permute-start.12) | collective-permute-done | bytes 196640 | tf_op jit(solution)/shard_map/ppermute | solution.py:485
  119.6 1.4 %collective-permute-done.13.refs_9_ = bf16[768,128]{1,0:T(8,128)(2,1)S(1)} collective-permute-done((bf16[768,128]{1,0:T(8,128)(2,1)}, bf16[768,128]{1,0:T(8,128)(2,1)S(1)}, u32[]{:S(2)}, u32[]{:S(2)}) %collective-permute-start.13) | collective-permute-done | bytes 196640 | tf_op jit(solution)/shard_map/ppermute | solution.py:485
  121.0 0.0 copy-done.2
  121.0 0.0 copy-done.3
  121.0 0.6 copy-done.8
  121.7 3.5 %shard_map.88 = (bf16[512,512]{1,0:T(8,128)(2,1)}, bf16[512,512]{1,0:T(8,128)(2,1)}, bf16[512,512]{1,0:T(8,128)(2,1)}, bf16[512,512]{1,0:T(8,128)(2,1)}) custom-call(s32[1]{0:T(128)} %bitcast.refs_0_, bf16[8,256,128]{2,1,0:T(8,128)(2,1)} %copy-done, bf16[768,128]{1,0:T(8,128)(2,1)} %get-tuple-element.50.refs_2_, bf16[768,128]{1,0:T(8,128)(2,1)} %copy-done.2, ...), custom_call_target="tpu_custom_call" | custom-call | tf_op jit(solution)/shard_map/pallas_call | solution.py:473
  (21 shorter events, 0.0 us)
Async XLA Ops:
  3.8 7.3 %collective-permute-start = (bf16[768,128]{1,0:T(8,128)(2,1)}, bf16[768,128]{1,0:T(8,128)(2,1)S(1)}, u32[]{:S(2)}, u32[]{:S(2)}) collective-permute-start(bf16[768,128]{1,0:T(8,128)(2,1)} %get-tuple-element.32), channel_id=1, source_target_pairs={{0,4},{4,8},{8,12},{12,16},{16,20},{20,24},{24,28},{28,0},{1,5},{5... | collective-permute-start | bytes 589832 | tf_op jit(solution)/shard_map/ppermute | solution.py:485
  5.3 26.7 %collective-permute-start.1 = (bf16[768,128]{1,0:T(8,128)(2,1)}, bf16[768,128]{1,0:T(8,128)(2,1)S(1)}, u32[]{:S(2)}, u32[]{:S(2)}) collective-permute-start(bf16[768,128]{1,0:T(8,128)(2,1)} %get-tuple-element.33), channel_id=1, source_target_pairs={{0,8},{4,12},{8,16},{12,20},{16,24},{20,28},{24,0},{28,4},{1,9},{5... | collective-permute-start | bytes 589832 | tf_op jit(solution)/shard_map/ppermute | solution.py:485
  6.9 29.3 %collective-permute-start.2 = (bf16[768,128]{1,0:T(8,128)(2,1)}, bf16[768,128]{1,0:T(8,128)(2,1)S(1)}, u32[]{:S(2)}, u32[]{:S(2)}) collective-permute-start(bf16[768,128]{1,0:T(8,128)(2,1)} %get-tuple-element.34), channel_id=1, source_target_pairs={{0,12},{4,16},{8,20},{12,24},{16,28},{20,0},{24,4},{28,8},{1,13},{... | collective-permute-start | bytes 589832 | tf_op jit(solution)/shard_map/ppermute | solution.py:485
  8.0 31.2 %collective-permute-start.3 = (bf16[768,128]{1,0:T(8,128)(2,1)}, bf16[768,128]{1,0:T(8,128)(2,1)S(1)}, u32[]{:S(2)}, u32[]{:S(2)}) collective-permute-start(bf16[768,128]{1,0:T(8,128)(2,1)} %get-tuple-element.35), channel_id=1, source_target_pairs={{0,16},{4,20},{8,24},{12,28},{16,0},{20,4},{24,8},{28,12},{1,17},{... | collective-permute-start | bytes 589832 | tf_op jit(solution)/shard_map/ppermute | solution.py:485
  9.7 29.5 %collective-permute-start.4 = (bf16[768,128]{1,0:T(8,128)(2,1)}, bf16[768,128]{1,0:T(8,128)(2,1)S(1)}, u32[]{:S(2)}, u32[]{:S(2)}) collective-permute-start(bf16[768,128]{1,0:T(8,128)(2,1)} %get-tuple-element.36), channel_id=1, source_target_pairs={{0,20},{4,24},{8,28},{12,0},{16,4},{20,8},{24,12},{28,16},{1,21},{... | collective-permute-start | bytes 589832 | tf_op jit(solution)/shard_map/ppermute | solution.py:485
  11.0 36.4 %copy-start.9 = (bf16[768,128]{1,0:T(8,128)(2,1)}, bf16[768,128]{1,0:T(8,128)(2,1)S(1)}, u32[]{:S(2)}) copy-start(bf16[768,128]{1,0:T(8,128)(2,1)S(1)} %collective-permute-done.refs_3_) | copy-start | bytes 589828
  11.0 30.0 %collective-permute-start.5 = (bf16[768,128]{1,0:T(8,128)(2,1)}, bf16[768,128]{1,0:T(8,128)(2,1)S(1)}, u32[]{:S(2)}, u32[]{:S(2)}) collective-permute-start(bf16[768,128]{1,0:T(8,128)(2,1)} %get-tuple-element.37), channel_id=1, source_target_pairs={{0,24},{4,28},{8,0},{12,4},{16,8},{20,12},{24,16},{28,20},{1,25},{... | collective-permute-start | bytes 589832 | tf_op jit(solution)/shard_map/ppermute | solution.py:485
  32.0 15.5 %copy-start.10 = (bf16[768,128]{1,0:T(8,128)(2,1)}, bf16[768,128]{1,0:T(8,128)(2,1)S(1)}, u32[]{:S(2)}) copy-start(bf16[768,128]{1,0:T(8,128)(2,1)S(1)} %collective-permute-done.1.refs_4_) | copy-start | bytes 589828
  32.0 10.2 %collective-permute-start.6 = (bf16[768,128]{1,0:T(8,128)(2,1)}, bf16[768,128]{1,0:T(8,128)(2,1)S(1)}, u32[]{:S(2)}, u32[]{:S(2)}) collective-permute-start(bf16[768,128]{1,0:T(8,128)(2,1)} %get-tuple-element.38), channel_id=1, source_target_pairs={{0,28},{4,0},{8,4},{12,8},{16,12},{20,16},{24,20},{28,24},{1,29},{... | collective-permute-start | bytes 589832 | tf_op jit(solution)/shard_map/ppermute | solution.py:485
  36.2 11.3 %copy-start.11 = (bf16[768,128]{1,0:T(8,128)(2,1)}, bf16[768,128]{1,0:T(8,128)(2,1)S(1)}, u32[]{:S(2)}) copy-start(bf16[768,128]{1,0:T(8,128)(2,1)S(1)} %collective-permute-done.2.refs_5_) | copy-start | bytes 589828
  39.3 8.2 %copy-start.12 = (bf16[768,128]{1,0:T(8,128)(2,1)}, bf16[768,128]{1,0:T(8,128)(2,1)S(1)}, u32[]{:S(2)}) copy-start(bf16[768,128]{1,0:T(8,128)(2,1)S(1)} %collective-permute-done.3.refs_6_) | copy-start | bytes 589828
  39.3 8.2 %copy-start.13 = (bf16[768,128]{1,0:T(8,128)(2,1)}, bf16[768,128]{1,0:T(8,128)(2,1)S(1)}, u32[]{:S(2)}) copy-start(bf16[768,128]{1,0:T(8,128)(2,1)S(1)} %collective-permute-done.4.refs_7_) | copy-start | bytes 589828
  41.0 6.4 %copy-start.14 = (bf16[768,128]{1,0:T(8,128)(2,1)}, bf16[768,128]{1,0:T(8,128)(2,1)S(1)}, u32[]{:S(2)}) copy-start(bf16[768,128]{1,0:T(8,128)(2,1)S(1)} %collective-permute-done.5.refs_8_) | copy-start | bytes 589828
  42.1 5.3 %copy-start.15 = (bf16[768,128]{1,0:T(8,128)(2,1)}, bf16[768,128]{1,0:T(8,128)(2,1)S(1)}, u32[]{:S(2)}) copy-start(bf16[768,128]{1,0:T(8,128)(2,1)S(1)} %collective-permute-done.6.refs_9_) | copy-start | bytes 589828
  42.1 19.9 %all-to-all-start.1 = ((bf16[8,256,128]{2,1,0:T(8,128)(2,1)}), bf16[8,256,128]{2,1,0:T(8,128)(2,1)S(1)}, u32[]{:S(2)}, u32[]{:S(2)}) async-start(bf16[8,256,128]{2,1,0:T(8,128)(2,1)} %shard_map.85), calls=%async_computation.1 | async-start | bytes 1048576 | tf_op jit(solution)/shard_map/all_to_all | solution.py:490
  62.0 6.0 %copy-start.1 = (bf16[8,256,128]{2,1,0:T(8,128)(2,1)}, bf16[8,256,128]{2,1,0:T(8,128)(2,1)S(1)}, u32[]{:S(2)}) copy-start(bf16[8,256,128]{2,1,0:T(8,128)(2,1)S(1)} %all-to-all-done.1.refs_10_) | copy-start | bytes 1572868
  62.0 50.8 %all-to-all-start = ((bf16[8,256,128]{2,1,0:T(8,128)(2,1)}), bf16[8,256,128]{2,1,0:T(8,128)(2,1)S(1)}, u32[]{:S(2)}, u32[]{:S(2)}) async-start(bf16[8,256,128]{2,1,0:T(8,128)(2,1)} %get-tuple-element.47), calls=%async_computation | async-start | bytes 1048576 | tf_op jit(solution)/shard_map/all_to_all | solution.py:490
  84.6 8.9 %collective-permute-start.7 = (bf16[768,128]{1,0:T(8,128)(2,1)}, bf16[768,128]{1,0:T(8,128)(2,1)S(1)}, u32[]{:S(2)}, u32[]{:S(2)}) collective-permute-start(bf16[768,128]{1,0:T(8,128)(2,1)} %get-tuple-element.51), channel_id=1, source_target_pairs={{0,4},{4,8},{8,12},{12,16},{16,20},{20,24},{24,28},{28,0},{1,5},{5... | collective-permute-start | bytes 589832 | tf_op jit(solution)/shard_map/ppermute | solution.py:485
  86.1 26.7 %collective-permute-start.8 = (bf16[768,128]{1,0:T(8,128)(2,1)}, bf16[768,128]{1,0:T(8,128)(2,1)S(1)}, u32[]{:S(2)}, u32[]{:S(2)}) collective-permute-start(bf16[768,128]{1,0:T(8,128)(2,1)} %get-tuple-element.52), channel_id=1, source_target_pairs={{0,8},{4,12},{8,16},{12,20},{16,24},{20,28},{24,0},{28,4},{1,9},{5... | collective-permute-start | bytes 589832 | tf_op jit(solution)/shard_map/ppermute | solution.py:485
  87.5 28.4 %collective-permute-start.9 = (bf16[768,128]{1,0:T(8,128)(2,1)}, bf16[768,128]{1,0:T(8,128)(2,1)S(1)}, u32[]{:S(2)}, u32[]{:S(2)}) collective-permute-start(bf16[768,128]{1,0:T(8,128)(2,1)} %get-tuple-element.53), channel_id=1, source_target_pairs={{0,12},{4,16},{8,20},{12,24},{16,28},{20,0},{24,4},{28,8},{1,13},{... | collective-permute-start | bytes 589832 | tf_op jit(solution)/shard_map/ppermute | solution.py:485
  89.0 29.0 %collective-permute-start.10 = (bf16[768,128]{1,0:T(8,128)(2,1)}, bf16[768,128]{1,0:T(8,128)(2,1)S(1)}, u32[]{:S(2)}, u32[]{:S(2)}) collective-permute-start(bf16[768,128]{1,0:T(8,128)(2,1)} %get-tuple-element.54), channel_id=1, source_target_pairs={{0,16},{4,20},{8,24},{12,28},{16,0},{20,4},{24,8},{28,12},{1,17},{... | collective-permute-start | bytes 589832 | tf_op jit(solution)/shard_map/ppermute | solution.py:485
  90.4 27.6 %collective-permute-start.11 = (bf16[768,128]{1,0:T(8,128)(2,1)}, bf16[768,128]{1,0:T(8,128)(2,1)S(1)}, u32[]{:S(2)}, u32[]{:S(2)}) collective-permute-start(bf16[768,128]{1,0:T(8,128)(2,1)} %get-tuple-element.55), channel_id=1, source_target_pairs={{0,20},{4,24},{8,28},{12,0},{16,4},{20,8},{24,12},{28,16},{1,21},{... | collective-permute-start | bytes 589832 | tf_op jit(solution)/shard_map/ppermute | solution.py:485
  93.5 27.5 %copy-start.2 = (bf16[768,128]{1,0:T(8,128)(2,1)}, bf16[768,128]{1,0:T(8,128)(2,1)S(1)}, u32[]{:S(2)}) copy-start(bf16[768,128]{1,0:T(8,128)(2,1)S(1)} %collective-permute-done.7.refs_3_) | copy-start | bytes 589828
  93.5 26.1 %collective-permute-start.12 = (bf16[768,128]{1,0:T(8,128)(2,1)}, bf16[768,128]{1,0:T(8,128)(2,1)S(1)}, u32[]{:S(2)}, u32[]{:S(2)}) collective-permute-start(bf16[768,128]{1,0:T(8,128)(2,1)} %get-tuple-element.56), channel_id=1, source_target_pairs={{0,24},{4,28},{8,0},{12,4},{16,8},{20,12},{24,16},{28,20},{1,25},{... | collective-permute-start | bytes 589832 | tf_op jit(solution)/shard_map/ppermute | solution.py:485
  112.8 8.2 %copy-start.3 = (bf16[768,128]{1,0:T(8,128)(2,1)}, bf16[768,128]{1,0:T(8,128)(2,1)S(1)}, u32[]{:S(2)}) copy-start(bf16[768,128]{1,0:T(8,128)(2,1)S(1)} %collective-permute-done.8.refs_4_) | copy-start | bytes 589828
  112.8 8.2 %collective-permute-start.13 = (bf16[768,128]{1,0:T(8,128)(2,1)}, bf16[768,128]{1,0:T(8,128)(2,1)S(1)}, u32[]{:S(2)}, u32[]{:S(2)}) collective-permute-start(bf16[768,128]{1,0:T(8,128)(2,1)} %get-tuple-element.57), channel_id=1, source_target_pairs={{0,28},{4,0},{8,4},{12,8},{16,12},{20,16},{24,20},{28,24},{1,29},{... | collective-permute-start | bytes 589832 | tf_op jit(solution)/shard_map/ppermute | solution.py:485
  112.8 8.2 %copy-start = (bf16[8,256,128]{2,1,0:T(8,128)(2,1)}, bf16[8,256,128]{2,1,0:T(8,128)(2,1)S(1)}, u32[]{:S(2)}) copy-start(bf16[8,256,128]{2,1,0:T(8,128)(2,1)S(1)} %all-to-all-done.refs_1_) | copy-start | bytes 1572868
  115.9 5.1 %copy-start.4 = (bf16[768,128]{1,0:T(8,128)(2,1)}, bf16[768,128]{1,0:T(8,128)(2,1)S(1)}, u32[]{:S(2)}) copy-start(bf16[768,128]{1,0:T(8,128)(2,1)S(1)} %collective-permute-done.9.refs_5_) | copy-start | bytes 589828
  118.0 3.0 %copy-start.5 = (bf16[768,128]{1,0:T(8,128)(2,1)}, bf16[768,128]{1,0:T(8,128)(2,1)S(1)}, u32[]{:S(2)}) copy-start(bf16[768,128]{1,0:T(8,128)(2,1)S(1)} %collective-permute-done.10.refs_6_) | copy-start | bytes 589828
  118.0 3.0 %copy-start.6 = (bf16[768,128]{1,0:T(8,128)(2,1)}, bf16[768,128]{1,0:T(8,128)(2,1)S(1)}, u32[]{:S(2)}) copy-start(bf16[768,128]{1,0:T(8,128)(2,1)S(1)} %collective-permute-done.11.refs_7_) | copy-start | bytes 589828
  119.5 1.5 %copy-start.7 = (bf16[768,128]{1,0:T(8,128)(2,1)}, bf16[768,128]{1,0:T(8,128)(2,1)S(1)}, u32[]{:S(2)}) copy-start(bf16[768,128]{1,0:T(8,128)(2,1)S(1)} %collective-permute-done.12.refs_8_) | copy-start | bytes 589828
  121.0 0.7 copy-start.8

commit v2 on v1

--- a/solution.py
+++ b/solution.py
@@ -204,8 +204,17 @@
     return jnp.where(i < 0, i + count, jnp.where(i >= count, i - count, i))
 
 
+def in_turn(*steps):
+    steps = list(steps)
+    while steps:
+        for step in list(steps):
+            if next(step, steps) is steps:
+                steps.remove(step)
+
+
 class Block:
-    def __init__(self, b, partners, rows, first_query, table, kv, kv_t, block, scores, gathered, sg, wl, dacc):
+    def __init__(self, b, partners, rows, first_query, table, kv, kv_t, block, scores, gathered, sg, wl, dacc, oq):
+        self.oq = oq
         self.kv, self.kv_t, self.scores, self.gathered, self.dacc, self.b = kv, kv_t, scores, gathered, dacc, b
         self.sg, self.wl = sg, wl
         self.queries = queries = block.shape[0]
@@ -237,7 +246,7 @@
                 place = (entry // (rows // SUB), pl.multiple_of(entry % (rows // SUB) * SUB, SUB))
                 self.extra_places.append(place)
                 gathered[e * SUB : (e + 1) * SUB, :] = kv[place[0], pl.ds(place[1], SUB), :]
-            self.gathered_t = jnp.transpose(gathered[: entries * SUB, :].astype(jnp.float32)).astype(CAST)
+            self.gathered_t = jnp.transpose(gathered[: entries * SUB, :])
             self.chunks.append((None, 0, entries * SUB, "extra"))
         self.places = []
         at = 0
@@ -268,6 +277,7 @@
                 s = jnp.where(row < self.live * SUB, s, LOWEST)
             self.scores[place, :] = s
             peak = jnp.maximum(peak, by_eights(s, jnp.maximum))
+            yield
         self.top = jnp.max(peak, axis=0, keepdims=True)
 
     def mix(self):
@@ -277,18 +287,22 @@
             w = jnp.exp(self.scores[place, :] - self.top)
             total = total + by_eights(w, jnp.add)
             mixed = mixed + nn(self.keys_t(chunk)[HD:], w.astype(CAST))
+            yield
         total = jnp.sum(total, axis=0, keepdims=True)
         self.mixed = mixed / total
         low = self.mixed.astype(CAST).astype(jnp.float32)
         self.delta = jnp.sum(self.block_t[HD:] * low, axis=0, keepdims=True)
         self.norm = self.top + jnp.log(total)
 
-    def grads(self):
-        query_grad = jnp.zeros((HD, self.queries), jnp.float32)
+    def factors(self):
         for chunk, place in zip(self.chunks, self.places):
             w = jnp.exp(self.scores[place, :] - self.norm)
             self.sg[place, :] = (w * (nn(self.keys(chunk), self.g_t) - self.delta)).astype(CAST)
             self.wl[place, :] = w.astype(CAST)
+            yield
+
+    def products(self):
+        query_grad = jnp.zeros((HD, self.queries), jnp.float32)
         for chunk, place in zip(self.chunks, self.places):
             sg = self.sg[place, :]
             query_grad = query_grad + nn(self.keys_t(chunk)[:HD], sg)
@@ -299,7 +313,9 @@
                     self.dacc[owner, pl.ds(at, SUB), :] += part[e * SUB : (e + 1) * SUB]
             else:
                 self.dacc[block, first : first + count, :] += part
-        return jnp.transpose(jnp.concatenate([query_grad * (1.0 / math.sqrt(HD)), self.mixed], axis=0)).astype(CAST)
+            yield
+        both = jnp.concatenate([query_grad * (1.0 / math.sqrt(HD)), self.mixed], axis=0)
+        self.oq[self.b] = jnp.transpose(both).astype(CAST)
 
 
 def attention_kernel(blocks, rows, first_query, queries, together, *refs):
@@ -315,18 +331,19 @@
     early = take(blocks)
     me = me_ref[0]
     if last:
-        qd, before = take(2)
+        qd, sums = take(2)
         out = take(blocks)
-        kv, kv_t, scores, gathered, sg, wl, dacc, oq = take(8)
-        dacc[...] = before[...]
+        kv, kv_t, scores, gathered, sg, wl, dacc, held, moved, oq = take(10)
+        for b in range(blocks):
+            pltpu.make_async_copy(sums.at[b], held.at[b], moved.at[b]).start()
     else:
-        oq, dacc, kv, kv_t, scores, gathered, sg, wl, qd = take(9)
-        dacc[...] = jnp.zeros_like(dacc)
+        oq, sums, kv, kv_t, scores, gathered, sg, wl, dacc, held, moved, qd = take(12)
+    dacc[...] = jnp.zeros_like(dacc)
     for k in range(blocks):
         b = wrapped(me - k, blocks)
         keys = early[k][:rows, :]
         kv[b] = keys
-        kv_t[b] = jnp.transpose(keys.astype(jnp.float32)).astype(CAST)
+        kv_t[b] = jnp.transpose(keys)
         if not last:
             qd[b] = early[k][rows:, :]
     levels = (blocks - 1).bit_length()
@@ -334,15 +351,23 @@
     def run(partners, ids):
         work = [
             Block(b, partners, rows, first_query, table, kv, kv_t, qd[b], scores.at[i], gathered.at[i], sg.at[i],
-                  wl.at[i], dacc)
+                  wl.at[i], dacc, oq)
             for i, b in enumerate(ids)
         ]
         for w in work:
-            w.score()
+            in_turn(w.score())
         for w in work:
-            w.mix()
-        for w in work:
-            oq[w.b] = w.grads()
+            in_turn(w.mix())
+        in_turn(work[0].factors())
+        for now, then in zip(work, work[1:] + [None]):
+            if then:
+                in_turn(then.factors(), now.products())
+            else:
+                in_turn(now.products())
+        if not last:
+            for w in work:
+                held[w.b] = dacc[w.b]
+                pltpu.make_async_copy(held.at[w.b], sums.at[w.b], moved.at[w.b]).start()
 
     for partners in range(levels, -1, -1):
         low = (1 << partners) >> 1
@@ -357,10 +382,15 @@
             lax.fori_loop(0, (high - low) // group, step, 0)
         else:
             run(partners, [jnp.int32(high - 1 - j) for j in range(group)])
+    for b in range(blocks):
+        if last:
+            pltpu.make_async_copy(sums.at[b], held.at[b], moved.at[b]).wait()
+        else:
+            pltpu.make_async_copy(held.at[b], sums.at[b], moved.at[b]).wait()
     if last:
         for k in range(blocks):
             b = wrapped(me + k, blocks)
-            out[k][:rows, :] = dacc[b].astype(CAST)
+            out[k][:rows, :] = (dacc[b] + held[b]).astype(CAST)
             out[k][rows:, :] = oq[b]
 
 
@@ -373,6 +403,7 @@
     last = first_query + queries == rows
     whole = pl.BlockSpec(memory_space=pltpu.VMEM)
     small = pl.BlockSpec(memory_space=pltpu.SMEM)
+    apart = pl.BlockSpec(memory_space=pl.ANY)
     sums = (blocks, rows, width)
     if last:
         out_shape = [jax.ShapeDtypeStruct((rows + queries, width), CAST)] * blocks
@@ -390,15 +421,14 @@
         pltpu.VMEM((together, list_rows, queries), CAST),
         pltpu.VMEM((together, list_rows, queries), CAST),
     ]
-    if last:
-        scratch.append(pltpu.VMEM(sums, jnp.float32))
+    scratch += [pltpu.VMEM(sums, jnp.float32)] * 2 + [pltpu.SemaphoreType.DMA((blocks,))]
     scratch.append(pltpu.VMEM((blocks, queries, width), CAST))
     pairs = blocks * (levels + 1) * rows * queries
     return pl.pallas_call(
         functools.partial(attention_kernel, blocks, rows, first_query, queries, together),
         out_shape=tuple(out_shape),
-        in_specs=[small] * 2 + [whole] * (len(inputs) - 2),
-        out_specs=(whole,) * len(out_shape),
+        in_specs=[small] * 2 + [whole] * (len(inputs) - 3) + [apart if last else whole],
+        out_specs=(whole,) * (len(out_shape) - 1) + (whole if last else apart,),
         scratch_shapes=scratch,
         cost_estimate=pl.CostEstimate(flops=pairs * HD * 2 * 6 * 4, transcendentals=2 * pairs, bytes_accessed=8 << 20),
         compiler_params=pltpu.CompilerParams(vmem_limit_bytes=56 * 1024 * 1024),
@@ -414,40 +444,63 @@
     return jnp.where(lane < HD, first, swap(second)), jnp.where(lane < HD, swap(first), second)
 
 
-def pack_kernel(heads, pieces, apart, *refs):
+def pack_kernel(heads, pieces, apart, count, *refs):
     me = refs[0][0]
-    inputs = refs[1 : 1 + 1 + max(max(piece[:2]) for piece in pieces)]
-    packed = refs[-1]
-    for pair in range(heads // 2):
-        lanes = slice(pair * 2 * HD, (pair + 1) * 2 * HD)
-        at = 0
-        for first, second, low, count in pieces:
-            both = interleave(inputs[first][low : low + count, lanes], inputs[second][low : low + count, lanes])
-            packed[2 * pair, at : at + count, :] = both[0]
-            packed[2 * pair + 1, at : at + count, :] = both[1]
-            at += count
+    sources, results = refs[1 : 1 + count], refs[1 + count : -3]
+    packed, inputs, arrived = refs[-3:]
+    rows = sources[0].shape[0]
+    parts = 2
+
+    def copy(i, part):
+        place = pl.ds(part * (rows // parts), rows // parts)
+        return pltpu.make_async_copy(sources[i].at[place], inputs.at[i, place], arrived.at[i * parts + part])
+
+    for i in range(count):
+        for part in range(parts):
+            copy(i, part).start()
+    ready = set()
+    at = 0
+    for first, second, low, size in pieces:
+        for i in (first, second):
+            if i not in ready:
+                for part in range(parts):
+                    copy(i, part).wait()
+                ready.add(i)
+        for pair in range(heads // 2):
+            lanes = slice(pair * 2 * HD, (pair + 1) * 2 * HD)
+            both = interleave(inputs[first, low : low + size, lanes], inputs[second, low : low + size, lanes])
+            packed[2 * pair, at : at + size, :] = both[0]
+            packed[2 * pair + 1, at : at + size, :] = both[1]
+        at += size
     if apart:
-        for k, out in enumerate(refs[1 + len(inputs) : -1]):
+        for k, out in enumerate(results):
             out[...] = packed[wrapped(me + k, heads)]
+    else:
+        results[0][...] = packed[...]
 
 
 def pack(me, arrays, pieces, apart):
-    heads = arrays[0].shape[1] // HD
+    rows, columns = arrays[0].shape
+    heads = columns // HD
     total = sum(piece[3] for piece in pieces)
     whole = pl.BlockSpec(memory_space=pltpu.VMEM)
     all_heads = (heads, total, 2 * HD)
     if apart:
         out_shape = (jax.ShapeDtypeStruct((total, 2 * HD), CAST),) * heads
         out_specs = (whole,) * heads
-        scratch = [pltpu.VMEM(all_heads, CAST)]
     else:
-        out_shape, out_specs, scratch = jax.ShapeDtypeStruct(all_heads, CAST), whole, []
+        out_shape, out_specs = jax.ShapeDtypeStruct(all_heads, CAST), whole
     return pl.pallas_call(
-        functools.partial(pack_kernel, heads, pieces, apart),
+        functools.partial(pack_kernel, heads, pieces, apart, len(arrays)),
         out_shape=out_shape,
-        in_specs=[pl.BlockSpec(memory_space=pltpu.SMEM)] + [whole] * len(arrays),
+        in_specs=[pl.BlockSpec(memory_space=pltpu.SMEM)] + [pl.BlockSpec(memory_space=pl.ANY)] * len(arrays),
         out_specs=out_specs,
-        scratch_shapes=scratch,
+        scratch_shapes=[
+            pltpu.VMEM(all_heads, CAST),
+            pltpu.VMEM((len(arrays), rows, columns), CAST),
+            pltpu.SemaphoreType.DMA((2 * len(arrays),)),
+        ],
+        compiler_params=pltpu.CompilerParams(vmem_limit_bytes=56 * 1024 * 1024),
         cost_estimate=pl.CostEstimate(flops=0, transcendentals=0, bytes_accessed=8 * total * heads * HD),
     )(me, *arrays)
 
@@ -476,6 +529,7 @@
         in_specs=[pl.BlockSpec(memory_space=pltpu.SMEM)] + [whole] * (1 + heads),
         out_specs=(whole,) * 4,
         scratch_shapes=[pltpu.VMEM((heads,) + late[0].shape, CAST)],
+        compiler_params=pltpu.CompilerParams(vmem_limit_bytes=10 * 1024 * 1024),
     )(me, early, *late)
 
 

time: 126 us -> 124 us (0.984)
  Pallas kernels: 40 us -> 37.6 us
    pallas_call x1, Pallas kernels: 3.53 us -> 1.92 us  [unpack(): pl.pallas_call(functools.partial(unpack_kernel, heads, rows), out_shape=(...]
where the time goes in v2:
time: 124 us; the launch traced here: 123 us
  waiting for transfers between devices  56.6 us (46%)
  Pallas kernels  37.6 us (30%)
  starting transfers between devices  27.2 us (22%)
    ppermute x14, waiting for transfers between devices, shifted_all(): lax.ppermute(pieces[k], 'tm', [(i, (i + k) % count) for i in range(count)])  56.6 us
    pallas_call x2, Pallas kernels, attention(): pl.pallas_call(functools.partial(attention_kernel, blocks, rows, first_qu...  30.4 us
    ppermute x14, starting transfers between devices, shifted_all(): lax.ppermute(pieces[k], 'tm', [(i, (i + k) % count) for i in range(count)])  15.9 us
    all_to_all x2, starting transfers between devices, all_heads(): return lax.all_to_all(packed, 'tm', split_axis=0, concat_axis=0, tiled=True)  11.3 us
    pallas_call x2, Pallas kernels, pack(): pl.pallas_call(functools.partial(pack_kernel, heads, pieces, apart, len(a...  5.31 us
  transfers between devices with their start and end apart: 16, of which 11 were waited for; matrix products, arithmetic and copies ran while one was open for 0% of the time, Pallas kernels for 27%

profile of v2, /device:TPU:12, one launch (start us, length us, event | category | flops | bytes accessed | tf_op | source)
XLA Modules:
  0.0 123.1 jit_solution(17557587589716236422)
XLA Ops:
  0.6 3.0 %shard_map.84 = (bf16[768,128]{1,0:T(8,128)(2,1)}, bf16[768,128]{1,0:T(8,128)(2,1)}, bf16[768,128]{1,0:T(8,128)(2,1)}, bf16[768,128]{1,0:T(8,128)(2,1)}, bf16[76...) custom-call(s32[1]{0:T(128)} %bitcast.refs_0_, ...), custom_call_target="tpu_custom_call" | custom-call | bytes 3145728 | tf_op jit(solution)/shard_map/pallas_call | solution.py:493
  3.6 1.6 %collective-permute-start = (bf16[768,128]{1,0:T(8,128)(2,1)}, bf16[768,128]{1,0:T(8,128)(2,1)S(1)}, u32[]{:S(2)}, u32[]{:S(2)}) collective-permute-start(bf16[768,128]{1,0:T(8,128)(2,1)} %get-tuple-element.32), channel_id=1, source_target_pairs={{0,4},{4,8},{8,12},{12,16},{16,20},{20,24},{24,28},{28,0},{1,5},{5... | collective-permute-start | bytes 589832 | tf_op jit(solution)/shard_map/ppermute | solution.py:539
  5.2 1.6 %collective-permute-start.1 = (bf16[768,128]{1,0:T(8,128)(2,1)}, bf16[768,128]{1,0:T(8,128)(2,1)S(1)}, u32[]{:S(2)}, u32[]{:S(2)}) collective-permute-start(bf16[768,128]{1,0:T(8,128)(2,1)} %get-tuple-element.33), channel_id=1, source_target_pairs={{0,8},{4,12},{8,16},{12,20},{16,24},{20,28},{24,0},{28,4},{1,9},{5... | collective-permute-start | bytes 589832 | tf_op jit(solution)/shard_map/ppermute | solution.py:539
  6.7 1.2 collective-permute-start.2
  7.9 1.7 %collective-permute-start.3 = (bf16[768,128]{1,0:T(8,128)(2,1)}, bf16[768,128]{1,0:T(8,128)(2,1)S(1)}, u32[]{:S(2)}, u32[]{:S(2)}) collective-permute-start(bf16[768,128]{1,0:T(8,128)(2,1)} %get-tuple-element.35), channel_id=1, source_target_pairs={{0,16},{4,20},{8,24},{12,28},{16,0},{20,4},{24,8},{28,12},{1,17},{... | collective-permute-start | bytes 589832 | tf_op jit(solution)/shard_map/ppermute | solution.py:539
  9.6 1.3 %collective-permute-start.4 = (bf16[768,128]{1,0:T(8,128)(2,1)}, bf16[768,128]{1,0:T(8,128)(2,1)S(1)}, u32[]{:S(2)}, u32[]{:S(2)}) collective-permute-start(bf16[768,128]{1,0:T(8,128)(2,1)} %get-tuple-element.36), channel_id=1, source_target_pairs={{0,20},{4,24},{8,28},{12,0},{16,4},{20,8},{24,12},{28,16},{1,21},{... | collective-permute-start | bytes 589832 | tf_op jit(solution)/shard_map/ppermute | solution.py:539
  10.9 0.0 collective-permute-done.refs_3_
  10.9 0.0 copy-start.2
  10.9 1.2 %collective-permute-start.5 = (bf16[768,128]{1,0:T(8,128)(2,1)}, bf16[768,128]{1,0:T(8,128)(2,1)S(1)}, u32[]{:S(2)}, u32[]{:S(2)}) collective-permute-start(bf16[768,128]{1,0:T(8,128)(2,1)} %get-tuple-element.37), channel_id=1, source_target_pairs={{0,24},{4,28},{8,0},{12,4},{16,8},{20,12},{24,16},{28,20},{1,25},{... | collective-permute-start | bytes 589832 | tf_op jit(solution)/shard_map/ppermute | solution.py:539
  12.2 19.7 %collective-permute-done.1.refs_4_ = bf16[768,128]{1,0:T(8,128)(2,1)S(1)} collective-permute-done((bf16[768,128]{1,0:T(8,128)(2,1)}, bf16[768,128]{1,0:T(8,128)(2,1)S(1)}, u32[]{:S(2)}, u32[]{:S(2)}) %collective-permute-start.1) | collective-permute-done | bytes 196640 | tf_op jit(solution)/shard_map/ppermute | solution.py:539
  31.9 0.0 collective-permute-start.6
  31.9 2.4 %shard_map.85 = bf16[8,256,128]{2,1,0:T(8,128)(2,1)} custom-call(s32[1]{0:T(128)} %bitcast.refs_0_, bf16[512,512]{1,0:T(8,128)(2,1)} %refs_1_.5, bf16[512,512]{1,0:T(8,128)(2,1)} %refs_2_.3), custom_call_target="tpu_custom_call" | custom-call | bytes 1048576 | tf_op jit(solution)/shard_map/pallas_call | solution.py:493
  34.2 1.8 %collective-permute-done.2.refs_5_ = bf16[768,128]{1,0:T(8,128)(2,1)S(1)} collective-permute-done((bf16[768,128]{1,0:T(8,128)(2,1)}, bf16[768,128]{1,0:T(8,128)(2,1)S(1)}, u32[]{:S(2)}, u32[]{:S(2)}) %collective-permute-start.2) | collective-permute-done | bytes 196640 | tf_op jit(solution)/shard_map/ppermute | solution.py:539
  36.1 3.1 %collective-permute-done.3.refs_6_ = bf16[768,128]{1,0:T(8,128)(2,1)S(1)} collective-permute-done((bf16[768,128]{1,0:T(8,128)(2,1)}, bf16[768,128]{1,0:T(8,128)(2,1)S(1)}, u32[]{:S(2)}, u32[]{:S(2)}) %collective-permute-start.3) | collective-permute-done | bytes 196640 | tf_op jit(solution)/shard_map/ppermute | solution.py:539
  39.1 0.0 collective-permute-done.4.refs_7_
  39.1 1.8 %collective-permute-done.5.refs_8_ = bf16[768,128]{1,0:T(8,128)(2,1)S(1)} collective-permute-done((bf16[768,128]{1,0:T(8,128)(2,1)}, bf16[768,128]{1,0:T(8,128)(2,1)S(1)}, u32[]{:S(2)}, u32[]{:S(2)}) %collective-permute-start.5) | collective-permute-done | bytes 196640 | tf_op jit(solution)/shard_map/ppermute | solution.py:539
  40.9 1.1 collective-permute-done.6.refs_9_
  42.0 5.3 %all-to-all-start.1 = ((bf16[8,256,128]{2,1,0:T(8,128)(2,1)}), bf16[8,256,128]{2,1,0:T(8,128)(2,1)S(1)}, u32[]{:S(2)}, u32[]{:S(2)}) async-start(bf16[8,256,128]{2,1,0:T(8,128)(2,1)} %shard_map.85), calls=%async_computation.1 | async-start | bytes 1048576 | tf_op jit(solution)/shard_map/all_to_all | solution.py:544
  47.3 0.0 copy-done.2
  47.3 0.0 copy-done.3
  47.3 0.0 copy-done.4
  47.3 0.0 copy-done.5
  47.4 0.0 copy-done.6
  47.4 0.0 copy-done.7
  47.4 0.0 copy-done.8
  47.4 14.4 %shard_map.86 = (bf16[8,256,128]{2,1,0:T(8,128)(2,1)}, f32[8,512,128]{2,1,0:T(8,128)}) custom-call(s32[1]{0:T(128)} %bitcast.refs_0_, s32[8,16]{1,0:T(8,128)} %refs_1_.7, bf16[768,128]{1,0:T(8,128)(2,1)} %get-tuple-element.39.refs_2_, bf16[768,128]{1,0:T(8,128)(2,1)} %copy-done.2, bf16[768,128]{1,0:T(8,128)(2,1)} %copy-done.3, bf16[768,128]{1,0:T(8,128)(2,1)} %copy-done.4, ...), custom_call_target="tpu_custom_call" | custom-call | flops 12884901888 | bytes 8388608 | tf_op jit(solution)/shard_map/pallas_call | solution.py:427
  61.8 0.0 all-to-all-done.1.refs_10_
  61.8 0.0 copy-start.1
  61.8 6.0 %all-to-all-start = ((bf16[8,256,128]{2,1,0:T(8,128)(2,1)}), bf16[8,256,128]{2,1,0:T(8,128)(2,1)S(1)}, u32[]{:S(2)}, u32[]{:S(2)}) async-start(bf16[8,256,128]{2,1,0:T(8,128)(2,1)} %get-tuple-element.47), calls=%async_computation | async-start | bytes 1048576 | tf_op jit(solution)/shard_map/all_to_all | solution.py:544
  67.8 0.0 copy-done.1
  67.9 16.0 %shard_map.87 = (bf16[768,128]{1,0:T(8,128)(2,1)}, bf16[768,128]{1,0:T(8,128)(2,1)}, bf16[768,128]{1,0:T(8,128)(2,1)}, bf16[768,128]{1,0:T(8,128)(2,1)}, bf16[76...) custom-call(s32[1]{0:T(128)} %bitcast.refs_0_, ...), custom_call_target="tpu_custom_call" | custom-call | flops 12884901888 | bytes 8388608 | tf_op jit(solution)/shard_map/pallas_call | solution.py:427
  83.8 1.5 %collective-permute-start.7 = (bf16[768,128]{1,0:T(8,128)(2,1)}, bf16[768,128]{1,0:T(8,128)(2,1)S(1)}, u32[]{:S(2)}, u32[]{:S(2)}) collective-permute-start(bf16[768,128]{1,0:T(8,128)(2,1)} %get-tuple-element.51), channel_id=1, source_target_pairs={{0,4},{4,8},{8,12},{12,16},{16,20},{20,24},{24,28},{28,0},{1,5},{5... | collective-permute-start | bytes 589832 | tf_op jit(solution)/shard_map/ppermute | solution.py:539
  85.4 1.5 %collective-permute-start.8 = (bf16[768,128]{1,0:T(8,128)(2,1)}, bf16[768,128]{1,0:T(8,128)(2,1)S(1)}, u32[]{:S(2)}, u32[]{:S(2)}) collective-permute-start(bf16[768,128]{1,0:T(8,128)(2,1)} %get-tuple-element.52), channel_id=1, source_target_pairs={{0,8},{4,12},{8,16},{12,20},{16,24},{20,28},{24,0},{28,4},{1,9},{5... | collective-permute-start | bytes 589832 | tf_op jit(solution)/shard_map/ppermute | solution.py:539
  86.8 1.5 %collective-permute-start.9 = (bf16[768,128]{1,0:T(8,128)(2,1)}, bf16[768,128]{1,0:T(8,128)(2,1)S(1)}, u32[]{:S(2)}, u32[]{:S(2)}) collective-permute-start(bf16[768,128]{1,0:T(8,128)(2,1)} %get-tuple-element.53), channel_id=1, source_target_pairs={{0,12},{4,16},{8,20},{12,24},{16,28},{20,0},{24,4},{28,8},{1,13},{... | collective-permute-start | bytes 589832 | tf_op jit(solution)/shard_map/ppermute | solution.py:539
  88.3 1.5 %collective-permute-start.10 = (bf16[768,128]{1,0:T(8,128)(2,1)}, bf16[768,128]{1,0:T(8,128)(2,1)S(1)}, u32[]{:S(2)}, u32[]{:S(2)}) collective-permute-start(bf16[768,128]{1,0:T(8,128)(2,1)} %get-tuple-element.54), channel_id=1, source_target_pairs={{0,16},{4,20},{8,24},{12,28},{16,0},{20,4},{24,8},{28,12},{1,17},{... | collective-permute-start | bytes 589832 | tf_op jit(solution)/shard_map/ppermute | solution.py:539
  89.7 1.5 %collective-permute-start.11 = (bf16[768,128]{1,0:T(8,128)(2,1)}, bf16[768,128]{1,0:T(8,128)(2,1)S(1)}, u32[]{:S(2)}, u32[]{:S(2)}) collective-permute-start(bf16[768,128]{1,0:T(8,128)(2,1)} %get-tuple-element.55), channel_id=1, source_target_pairs={{0,20},{4,24},{8,28},{12,0},{16,4},{20,8},{24,12},{28,16},{1,21},{... | collective-permute-start | bytes 589832 | tf_op jit(solution)/shard_map/ppermute | solution.py:539
  91.2 1.6 %collective-permute-done.7.refs_3_ = bf16[768,128]{1,0:T(8,128)(2,1)S(1)} collective-permute-done((bf16[768,128]{1,0:T(8,128)(2,1)}, bf16[768,128]{1,0:T(8,128)(2,1)S(1)}, u32[]{:S(2)}, u32[]{:S(2)}) %collective-permute-start.7) | collective-permute-done | bytes 196640 | tf_op jit(solution)/shard_map/ppermute | solution.py:539
  92.8 0.0 collective-permute-start.12
  92.8 19.3 %collective-permute-done.8.refs_4_ = bf16[768,128]{1,0:T(8,128)(2,1)S(1)} collective-permute-done((bf16[768,128]{1,0:T(8,128)(2,1)}, bf16[768,128]{1,0:T(8,128)(2,1)S(1)}, u32[]{:S(2)}, u32[]{:S(2)}) %collective-permute-start.8) | collective-permute-done | bytes 196640 | tf_op jit(solution)/shard_map/ppermute | solution.py:539
  112.1 0.0 collective-permute-start.13
  112.1 0.0 all-to-all-done.refs_1_
  112.1 3.1 %collective-permute-done.9.refs_5_ = bf16[768,128]{1,0:T(8,128)(2,1)S(1)} collective-permute-done((bf16[768,128]{1,0:T(8,128)(2,1)}, bf16[768,128]{1,0:T(8,128)(2,1)S(1)}, u32[]{:S(2)}, u32[]{:S(2)}) %collective-permute-start.9) | collective-permute-done | bytes 196640 | tf_op jit(solution)/shard_map/ppermute | solution.py:539
  115.2 2.1 %collective-permute-done.10.refs_6_ = bf16[768,128]{1,0:T(8,128)(2,1)S(1)} collective-permute-done((bf16[768,128]{1,0:T(8,128)(2,1)}, bf16[768,128]{1,0:T(8,128)(2,1)S(1)}, u32[]{:S(2)}, u32[]{:S(2)}) %collective-permute-start.10) | collective-permute-done | bytes 196640 | tf_op jit(solution)/shard_map/ppermute | solution.py:539
  117.3 0.0 collective-permute-done.11.refs_7_
  117.3 1.6 %collective-permute-done.12.refs_8_ = bf16[768,128]{1,0:T(8,128)(2,1)S(1)} collective-permute-done((bf16[768,128]{1,0:T(8,128)(2,1)}, bf16[768,128]{1,0:T(8,128)(2,1)S(1)}, u32[]{:S(2)}, u32[]{:S(2)}) %collective-permute-start.12) | collective-permute-done | bytes 196640 | tf_op jit(solution)/shard_map/ppermute | solution.py:539
  118.8 1.4 %collective-permute-done.13.refs_9_ = bf16[768,128]{1,0:T(8,128)(2,1)S(1)} collective-permute-done((bf16[768,128]{1,0:T(8,128)(2,1)}, bf16[768,128]{1,0:T(8,128)(2,1)S(1)}, u32[]{:S(2)}, u32[]{:S(2)}) %collective-permute-start.13) | collective-permute-done | bytes 196640 | tf_op jit(solution)/shard_map/ppermute | solution.py:539
  120.3 0.9 copy-done
  121.2 1.9 %shard_map.88 = (bf16[512,512]{1,0:T(8,128)(2,1)}, bf16[512,512]{1,0:T(8,128)(2,1)}, bf16[512,512]{1,0:T(8,128)(2,1)}, bf16[512,512]{1,0:T(8,128)(2,1)}) custom-call(s32[1]{0:T(128)} %bitcast.refs_0_, bf16[8,256,128]{2,1,0:T(8,128)(2,1)S(1)} %all-to-all-done.refs_1_, bf16[768,128]{1,0:T(8,128)(2,1)S(1)} %copy-done, ...), custom_call_target="tpu_custom_call" | custom-call | tf_op jit(solution)/shard_map/pallas_call | solution.py:526
  (7 shorter events, 0.0 us)
Async XLA Ops:
  3.6 7.3 %collective-permute-start = (bf16[768,128]{1,0:T(8,128)(2,1)}, bf16[768,128]{1,0:T(8,128)(2,1)S(1)}, u32[]{:S(2)}, u32[]{:S(2)}) collective-permute-start(bf16[768,128]{1,0:T(8,128)(2,1)} %get-tuple-element.32), channel_id=1, source_target_pairs={{0,4},{4,8},{8,12},{12,16},{16,20},{20,24},{24,28},{28,0},{1,5},{5... | collective-permute-start | bytes 589832 | tf_op jit(solution)/shard_map/ppermute | solution.py:539
  5.2 26.7 %collective-permute-start.1 = (bf16[768,128]{1,0:T(8,128)(2,1)}, bf16[768,128]{1,0:T(8,128)(2,1)S(1)}, u32[]{:S(2)}, u32[]{:S(2)}) collective-permute-start(bf16[768,128]{1,0:T(8,128)(2,1)} %get-tuple-element.33), channel_id=1, source_target_pairs={{0,8},{4,12},{8,16},{12,20},{16,24},{20,28},{24,0},{28,4},{1,9},{5... | collective-permute-start | bytes 589832 | tf_op jit(solution)/shard_map/ppermute | solution.py:539
  6.7 29.3 %collective-permute-start.2 = (bf16[768,128]{1,0:T(8,128)(2,1)}, bf16[768,128]{1,0:T(8,128)(2,1)S(1)}, u32[]{:S(2)}, u32[]{:S(2)}) collective-permute-start(bf16[768,128]{1,0:T(8,128)(2,1)} %get-tuple-element.34), channel_id=1, source_target_pairs={{0,12},{4,16},{8,20},{12,24},{16,28},{20,0},{24,4},{28,8},{1,13},{... | collective-permute-start | bytes 589832 | tf_op jit(solution)/shard_map/ppermute | solution.py:539
  7.9 31.2 %collective-permute-start.3 = (bf16[768,128]{1,0:T(8,128)(2,1)}, bf16[768,128]{1,0:T(8,128)(2,1)S(1)}, u32[]{:S(2)}, u32[]{:S(2)}) collective-permute-start(bf16[768,128]{1,0:T(8,128)(2,1)} %get-tuple-element.35), channel_id=1, source_target_pairs={{0,16},{4,20},{8,24},{12,28},{16,0},{20,4},{24,8},{28,12},{1,17},{... | collective-permute-start | bytes 589832 | tf_op jit(solution)/shard_map/ppermute | solution.py:539
  9.6 29.5 %collective-permute-start.4 = (bf16[768,128]{1,0:T(8,128)(2,1)}, bf16[768,128]{1,0:T(8,128)(2,1)S(1)}, u32[]{:S(2)}, u32[]{:S(2)}) collective-permute-start(bf16[768,128]{1,0:T(8,128)(2,1)} %get-tuple-element.36), channel_id=1, source_target_pairs={{0,20},{4,24},{8,28},{12,0},{16,4},{20,8},{24,12},{28,16},{1,21},{... | collective-permute-start | bytes 589832 | tf_op jit(solution)/shard_map/ppermute | solution.py:539
  10.9 36.4 %copy-start.2 = (bf16[768,128]{1,0:T(8,128)(2,1)}, bf16[768,128]{1,0:T(8,128)(2,1)S(1)}, u32[]{:S(2)}) copy-start(bf16[768,128]{1,0:T(8,128)(2,1)S(1)} %collective-permute-done.refs_3_) | copy-start | bytes 589828
  10.9 30.0 %collective-permute-start.5 = (bf16[768,128]{1,0:T(8,128)(2,1)}, bf16[768,128]{1,0:T(8,128)(2,1)S(1)}, u32[]{:S(2)}, u32[]{:S(2)}) collective-permute-start(bf16[768,128]{1,0:T(8,128)(2,1)} %get-tuple-element.37), channel_id=1, source_target_pairs={{0,24},{4,28},{8,0},{12,4},{16,8},{20,12},{24,16},{28,20},{1,25},{... | collective-permute-start | bytes 589832 | tf_op jit(solution)/shard_map/ppermute | solution.py:539
  31.9 15.5 %copy-start.3 = (bf16[768,128]{1,0:T(8,128)(2,1)}, bf16[768,128]{1,0:T(8,128)(2,1)S(1)}, u32[]{:S(2)}) copy-start(bf16[768,128]{1,0:T(8,128)(2,1)S(1)} %collective-permute-done.1.refs_4_) | copy-start | bytes 589828
  31.9 10.2 %collective-permute-start.6 = (bf16[768,128]{1,0:T(8,128)(2,1)}, bf16[768,128]{1,0:T(8,128)(2,1)S(1)}, u32[]{:S(2)}, u32[]{:S(2)}) collective-permute-start(bf16[768,128]{1,0:T(8,128)(2,1)} %get-tuple-element.38), channel_id=1, source_target_pairs={{0,28},{4,0},{8,4},{12,8},{16,12},{20,16},{24,20},{28,24},{1,29},{... | collective-permute-start | bytes 589832 | tf_op jit(solution)/shard_map/ppermute | solution.py:539
  36.1 11.3 %copy-start.4 = (bf16[768,128]{1,0:T(8,128)(2,1)}, bf16[768,128]{1,0:T(8,128)(2,1)S(1)}, u32[]{:S(2)}) copy-start(bf16[768,128]{1,0:T(8,128)(2,1)S(1)} %collective-permute-done.2.refs_5_) | copy-start | bytes 589828
  39.1 8.2 %copy-start.5 = (bf16[768,128]{1,0:T(8,128)(2,1)}, bf16[768,128]{1,0:T(8,128)(2,1)S(1)}, u32[]{:S(2)}) copy-start(bf16[768,128]{1,0:T(8,128)(2,1)S(1)} %collective-permute-done.3.refs_6_) | copy-start | bytes 589828
  39.1 8.2 %copy-start.6 = (bf16[768,128]{1,0:T(8,128)(2,1)}, bf16[768,128]{1,0:T(8,128)(2,1)S(1)}, u32[]{:S(2)}) copy-start(bf16[768,128]{1,0:T(8,128)(2,1)S(1)} %collective-permute-done.4.refs_7_) | copy-start | bytes 589828
  40.9 6.4 %copy-start.7 = (bf16[768,128]{1,0:T(8,128)(2,1)}, bf16[768,128]{1,0:T(8,128)(2,1)S(1)}, u32[]{:S(2)}) copy-start(bf16[768,128]{1,0:T(8,128)(2,1)S(1)} %collective-permute-done.5.refs_8_) | copy-start | bytes 589828
  42.0 5.3 %copy-start.8 = (bf16[768,128]{1,0:T(8,128)(2,1)}, bf16[768,128]{1,0:T(8,128)(2,1)S(1)}, u32[]{:S(2)}) copy-start(bf16[768,128]{1,0:T(8,128)(2,1)S(1)} %collective-permute-done.6.refs_9_) | copy-start | bytes 589828
  42.0 19.8 %all-to-all-start.1 = ((bf16[8,256,128]{2,1,0:T(8,128)(2,1)}), bf16[8,256,128]{2,1,0:T(8,128)(2,1)S(1)}, u32[]{:S(2)}, u32[]{:S(2)}) async-start(bf16[8,256,128]{2,1,0:T(8,128)(2,1)} %shard_map.85), calls=%async_computation.1 | async-start | bytes 1048576 | tf_op jit(solution)/shard_map/all_to_all | solution.py:544
  61.8 6.0 %copy-start.1 = (bf16[8,256,128]{2,1,0:T(8,128)(2,1)}, bf16[8,256,128]{2,1,0:T(8,128)(2,1)S(1)}, u32[]{:S(2)}) copy-start(bf16[8,256,128]{2,1,0:T(8,128)(2,1)S(1)} %all-to-all-done.1.refs_10_) | copy-start | bytes 1572868
  61.8 50.3 %all-to-all-start = ((bf16[8,256,128]{2,1,0:T(8,128)(2,1)}), bf16[8,256,128]{2,1,0:T(8,128)(2,1)S(1)}, u32[]{:S(2)}, u32[]{:S(2)}) async-start(bf16[8,256,128]{2,1,0:T(8,128)(2,1)} %get-tuple-element.47), calls=%async_computation | async-start | bytes 1048576 | tf_op jit(solution)/shard_map/all_to_all | solution.py:544
  83.8 8.9 %collective-permute-start.7 = (bf16[768,128]{1,0:T(8,128)(2,1)}, bf16[768,128]{1,0:T(8,128)(2,1)S(1)}, u32[]{:S(2)}, u32[]{:S(2)}) collective-permute-start(bf16[768,128]{1,0:T(8,128)(2,1)} %get-tuple-element.51), channel_id=1, source_target_pairs={{0,4},{4,8},{8,12},{12,16},{16,20},{20,24},{24,28},{28,0},{1,5},{5... | collective-permute-start | bytes 589832 | tf_op jit(solution)/shard_map/ppermute | solution.py:539
  85.4 26.7 %collective-permute-start.8 = (bf16[768,128]{1,0:T(8,128)(2,1)}, bf16[768,128]{1,0:T(8,128)(2,1)S(1)}, u32[]{:S(2)}, u32[]{:S(2)}) collective-permute-start(bf16[768,128]{1,0:T(8,128)(2,1)} %get-tuple-element.52), channel_id=1, source_target_pairs={{0,8},{4,12},{8,16},{12,20},{16,24},{20,28},{24,0},{28,4},{1,9},{5... | collective-permute-start | bytes 589832 | tf_op jit(solution)/shard_map/ppermute | solution.py:539
  86.8 28.4 %collective-permute-start.9 = (bf16[768,128]{1,0:T(8,128)(2,1)}, bf16[768,128]{1,0:T(8,128)(2,1)S(1)}, u32[]{:S(2)}, u32[]{:S(2)}) collective-permute-start(bf16[768,128]{1,0:T(8,128)(2,1)} %get-tuple-element.53), channel_id=1, source_target_pairs={{0,12},{4,16},{8,20},{12,24},{16,28},{20,0},{24,4},{28,8},{1,13},{... | collective-permute-start | bytes 589832 | tf_op jit(solution)/shard_map/ppermute | solution.py:539
  88.3 29.0 %collective-permute-start.10 = (bf16[768,128]{1,0:T(8,128)(2,1)}, bf16[768,128]{1,0:T(8,128)(2,1)S(1)}, u32[]{:S(2)}, u32[]{:S(2)}) collective-permute-start(bf16[768,128]{1,0:T(8,128)(2,1)} %get-tuple-element.54), channel_id=1, source_target_pairs={{0,16},{4,20},{8,24},{12,28},{16,0},{20,4},{24,8},{28,12},{1,17},{... | collective-permute-start | bytes 589832 | tf_op jit(solution)/shard_map/ppermute | solution.py:539
  89.7 27.6 %collective-permute-start.11 = (bf16[768,128]{1,0:T(8,128)(2,1)}, bf16[768,128]{1,0:T(8,128)(2,1)S(1)}, u32[]{:S(2)}, u32[]{:S(2)}) collective-permute-start(bf16[768,128]{1,0:T(8,128)(2,1)} %get-tuple-element.55), channel_id=1, source_target_pairs={{0,20},{4,24},{8,28},{12,0},{16,4},{20,8},{24,12},{28,16},{1,21},{... | collective-permute-start | bytes 589832 | tf_op jit(solution)/shard_map/ppermute | solution.py:539
  92.8 26.1 %collective-permute-start.12 = (bf16[768,128]{1,0:T(8,128)(2,1)}, bf16[768,128]{1,0:T(8,128)(2,1)S(1)}, u32[]{:S(2)}, u32[]{:S(2)}) collective-permute-start(bf16[768,128]{1,0:T(8,128)(2,1)} %get-tuple-element.56), channel_id=1, source_target_pairs={{0,24},{4,28},{8,0},{12,4},{16,8},{20,12},{24,16},{28,20},{1,25},{... | collective-permute-start | bytes 589832 | tf_op jit(solution)/shard_map/ppermute | solution.py:539
  112.1 8.2 %collective-permute-start.13 = (bf16[768,128]{1,0:T(8,128)(2,1)}, bf16[768,128]{1,0:T(8,128)(2,1)S(1)}, u32[]{:S(2)}, u32[]{:S(2)}) collective-permute-start(bf16[768,128]{1,0:T(8,128)(2,1)} %get-tuple-element.57), channel_id=1, source_target_pairs={{0,28},{4,0},{8,4},{12,8},{16,12},{20,16},{24,20},{28,24},{1,29},{... | collective-permute-start | bytes 589832 | tf_op jit(solution)/shard_map/ppermute | solution.py:539
  120.3 0.9 copy-start

commit v3 on v2

--- a/solution.py
+++ b/solution.py
@@ -14,6 +14,7 @@
 CAP = 2
 TILE = 256
 LOWEST = -1e30
+LOG2E = math.log2(math.e)
 CAST = jnp.bfloat16
 TOGETHER = 2
 
@@ -269,7 +270,7 @@
     def score(self):
         peak = jnp.full((8, self.queries), LOWEST, jnp.float32)
         for chunk, place in zip(self.chunks, self.places):
-            s = nn(self.keys(chunk), self.q_t)
+            s = nn(self.keys(chunk), self.q_t) * LOG2E
             row = lax.broadcasted_iota(jnp.int32, s.shape, 0)
             if chunk[3] == "own":
                 s = jnp.where(row <= lax.broadcasted_iota(jnp.int32, s.shape, 1), s, LOWEST)
@@ -284,7 +285,7 @@
         total = jnp.zeros((8, self.queries), jnp.float32)
         mixed = jnp.zeros((HD, self.queries), jnp.float32)
         for chunk, place in zip(self.chunks, self.places):
-            w = jnp.exp(self.scores[place, :] - self.top)
+            w = jnp.exp2(self.scores[place, :] - self.top)
             total = total + by_eights(w, jnp.add)
             mixed = mixed + nn(self.keys_t(chunk)[HD:], w.astype(CAST))
             yield
@@ -292,11 +293,11 @@
         self.mixed = mixed / total
         low = self.mixed.astype(CAST).astype(jnp.float32)
         self.delta = jnp.sum(self.block_t[HD:] * low, axis=0, keepdims=True)
-        self.norm = self.top + jnp.log(total)
+        self.norm = self.top + jnp.log(total) * LOG2E
 
     def factors(self):
         for chunk, place in zip(self.chunks, self.places):
-            w = jnp.exp(self.scores[place, :] - self.norm)
+            w = jnp.exp2(self.scores[place, :] - self.norm)
             self.sg[place, :] = (w * (nn(self.keys(chunk), self.g_t) - self.delta)).astype(CAST)
             self.wl[place, :] = w.astype(CAST)
             yield
@@ -403,13 +404,14 @@
     last = first_query + queries == rows
     whole = pl.BlockSpec(memory_space=pltpu.VMEM)
     small = pl.BlockSpec(memory_space=pltpu.SMEM)
-    apart = pl.BlockSpec(memory_space=pl.ANY)
+    apart = pl.BlockSpec(memory_space=pltpu.HBM)
     sums = (blocks, rows, width)
     if last:
         out_shape = [jax.ShapeDtypeStruct((rows + queries, width), CAST)] * blocks
+        before = pltpu.with_memory_space_constraint(before, pltpu.HBM)
         inputs = [me, table] + list(early) + [late, before]
     else:
-        out_shape = [jax.ShapeDtypeStruct((blocks, queries, width), CAST), jax.ShapeDtypeStruct(sums, jnp.float32)]
+        out_shape = [jax.ShapeDtypeStruct((blocks, queries, width), CAST), pltpu.HBM(sums, jnp.float32)]
         inputs = [me, table] + list(early)
     extra_rows = min(entries, CAP * ((1 << levels) - 1)) * SUB
     list_rows = first_query + queries + levels * rows + extra_rows
@@ -431,7 +433,7 @@
         out_specs=(whole,) * (len(out_shape) - 1) + (whole if last else apart,),
         scratch_shapes=scratch,
         cost_estimate=pl.CostEstimate(flops=pairs * HD * 2 * 6 * 4, transcendentals=2 * pairs, bytes_accessed=8 << 20),
-        compiler_params=pltpu.CompilerParams(vmem_limit_bytes=56 * 1024 * 1024),
+        compiler_params=pltpu.CompilerParams(vmem_limit_bytes=30 * 1024 * 1024),
     )(*inputs)
 
 
@@ -493,16 +495,16 @@
     return pl.pallas_call(
         functools.partial(pack_kernel, heads, pieces, apart, len(arrays)),
         out_shape=out_shape,
-        in_specs=[pl.BlockSpec(memory_space=pltpu.SMEM)] + [pl.BlockSpec(memory_space=pl.ANY)] * len(arrays),
+        in_specs=[pl.BlockSpec(memory_space=pltpu.SMEM)] + [pl.BlockSpec(memory_space=pltpu.HBM)] * len(arrays),
         out_specs=out_specs,
         scratch_shapes=[
             pltpu.VMEM(all_heads, CAST),
             pltpu.VMEM((len(arrays), rows, columns), CAST),
             pltpu.SemaphoreType.DMA((2 * len(arrays),)),
         ],
-        compiler_params=pltpu.CompilerParams(vmem_limit_bytes=56 * 1024 * 1024),
+        compiler_params=pltpu.CompilerParams(vmem_limit_bytes=12 * 1024 * 1024),
         cost_estimate=pl.CostEstimate(flops=0, transcendentals=0, bytes_accessed=8 * total * heads * HD),
-    )(me, *arrays)
+    )(me, *[pltpu.with_memory_space_constraint(array, pltpu.HBM) for array in arrays])
 
 
 def unpack_kernel(heads, rows, *refs):
@@ -535,9 +537,10 @@
 
 def shifted_all(pieces):
     count = len(pieces)
-    return [pieces[0]] + [
-        lax.ppermute(pieces[k], "tm", [(i, (i + k) % count) for i in range(count)]) for k in range(1, count)
-    ]
+    got = {0: pieces[0]}
+    for k in sorted(range(1, count), key=lambda k: k):
+        got[k] = lax.ppermute(pieces[k], "tm", [(i, (i + k) % count) for i in range(count)])
+    return [got[k] for k in range(count)]
 
 
 def all_heads(packed):

time: 124 us -> 120 us (0.968)
  Pallas kernels: 37.6 us -> 33.9 us
    pallas_call x2, Pallas kernels: 30.4 us -> 27.8 us  [attention(): pl.pallas_call(functools.partial(attention_kernel, blocks, rows, first_qu...]
  transfers between devices with their start and end apart: 16 -> 16, of which waited for: 11 -> 11; matrix products, arithmetic and copies ran while one was open for 0% -> 0% of each run, Pallas kernels for 27% -> 25%
where the time goes in v3:
time: 120 us; the launch traced here: 119 us
  waiting for transfers between devices  56.4 us (47%)
  Pallas kernels  33.9 us (28%)
  starting transfers between devices  27.2 us (23%)
    ppermute x14, waiting for transfers between devices, shifted_all(): lax.ppermute(pieces[k], 'tm', [(i, (i + k) % count) for i in range(count)])  56.4 us
    pallas_call x2, Pallas kernels, attention(): pl.pallas_call(functools.partial(attention_kernel, blocks, rows, first_qu...  27.8 us
    ppermute x14, starting transfers between devices, shifted_all(): lax.ppermute(pieces[k], 'tm', [(i, (i + k) % count) for i in range(count)])  16 us
    all_to_all x2, starting transfers between devices, all_heads(): return lax.all_to_all(packed, 'tm', split_axis=0, concat_axis=0, tiled=True)  11.3 us
    pallas_call x2, Pallas kernels, pack(): pl.pallas_call(functools.partial(pack_kernel, heads, pieces, apart, len(a...  4.2 us
  transfers between devices with their start and end apart: 16, of which 11 were waited for; matrix products, arithmetic and copies ran while one was open for 0% of the time, Pallas kernels for 25%

profile of v3, /device:TPU:12, one launch (start us, length us, event | category | flops | bytes accessed | tf_op | source)
XLA Modules:
  0.0 119.2 jit_solution(3973680835887028220)
XLA Ops:
  0.6 0.0 copy-start.2
  0.6 1.9 %shard_map.84 = (bf16[768,128]{1,0:T(8,128)(2,1)S(1)}, bf16[768,128]{1,0:T(8,128)(2,1)S(1)}, bf16[768,128]{1,0:T(8,128)(2,1)S(1)}, bf16[768,128]{1,0:T(8,128)(2,...) custom-call(s32[1]{0:T(128)} %bitcast.refs_0_, ...), custom_call_target="tpu_custom_call" | custom-call | bytes 3145728 | tf_op jit(solution)/shard_map/pallas_call | solution.py:495
  2.6 1.6 %collective-permute-start = (bf16[768,128]{1,0:T(8,128)(2,1)S(1)}, bf16[768,128]{1,0:T(8,128)(2,1)S(1)}, u32[]{:S(2)}, u32[]{:S(2)}) collective-permute-start(bf16[768,128]{1,0:T(8,128)(2,1)S(1)} %get-tuple-element.32), channel_id=1, source_target_pairs={{0,4},{4,8},{8,12},{12,16},{16,20},{20,24},{24,28},{28,0},{1,5},{5... | collective-permute-start | bytes 589832 | tf_op jit(solution)/shard_map/ppermute | solution.py:542
  4.1 1.6 %collective-permute-start.1 = (bf16[768,128]{1,0:T(8,128)(2,1)S(1)}, bf16[768,128]{1,0:T(8,128)(2,1)S(1)}, u32[]{:S(2)}, u32[]{:S(2)}) collective-permute-start(bf16[768,128]{1,0:T(8,128)(2,1)S(1)} %get-tuple-element.33), channel_id=1, source_target_pairs={{0,8},{4,12},{8,16},{12,20},{16,24},{20,28},{24,0},{28,4},{1,9},{5... | collective-permute-start | bytes 589832 | tf_op jit(solution)/shard_map/ppermute | solution.py:542
  5.7 1.2 collective-permute-start.2
  6.9 1.7 %collective-permute-start.3 = (bf16[768,128]{1,0:T(8,128)(2,1)S(1)}, bf16[768,128]{1,0:T(8,128)(2,1)S(1)}, u32[]{:S(2)}, u32[]{:S(2)}) collective-permute-start(bf16[768,128]{1,0:T(8,128)(2,1)S(1)} %get-tuple-element.35), channel_id=1, source_target_pairs={{0,16},{4,20},{8,24},{12,28},{16,0},{20,4},{24,8},{28,12},{1,17},{... | collective-permute-start | bytes 589832 | tf_op jit(solution)/shard_map/ppermute | solution.py:542
  8.6 1.3 %collective-permute-start.4 = (bf16[768,128]{1,0:T(8,128)(2,1)S(1)}, bf16[768,128]{1,0:T(8,128)(2,1)S(1)}, u32[]{:S(2)}, u32[]{:S(2)}) collective-permute-start(bf16[768,128]{1,0:T(8,128)(2,1)S(1)} %get-tuple-element.36), channel_id=1, source_target_pairs={{0,20},{4,24},{8,28},{12,0},{16,4},{20,8},{24,12},{28,16},{1,21},{... | collective-permute-start | bytes 589832 | tf_op jit(solution)/shard_map/ppermute | solution.py:542
  9.9 0.0 collective-permute-done.refs_3_
  9.9 1.2 %collective-permute-start.5 = (bf16[768,128]{1,0:T(8,128)(2,1)S(1)}, bf16[768,128]{1,0:T(8,128)(2,1)S(1)}, u32[]{:S(2)}, u32[]{:S(2)}) collective-permute-start(bf16[768,128]{1,0:T(8,128)(2,1)S(1)} %get-tuple-element.37), channel_id=1, source_target_pairs={{0,24},{4,28},{8,0},{12,4},{16,8},{20,12},{24,16},{28,20},{1,25},{... | collective-permute-start | bytes 589832 | tf_op jit(solution)/shard_map/ppermute | solution.py:542
  11.1 19.4 %collective-permute-done.1.refs_4_ = bf16[768,128]{1,0:T(8,128)(2,1)S(1)} collective-permute-done((bf16[768,128]{1,0:T(8,128)(2,1)S(1)}, bf16[768,128]{1,0:T(8,128)(2,1)S(1)}, u32[]{:S(2)}, u32[]{:S(2)}) %collective-permute-start.1) | collective-permute-done | bytes 196640 | tf_op jit(solution)/shard_map/ppermute | solution.py:542
  30.5 0.0 collective-permute-start.6
  30.5 2.3 %shard_map.85 = bf16[8,256,128]{2,1,0:T(8,128)(2,1)} custom-call(s32[1]{0:T(128)} %bitcast.refs_0_, bf16[512,512]{1,0:T(8,128)(2,1)} %refs_1_.5, bf16[512,512]{1,0:T(8,128)(2,1)} %refs_2_.3), custom_call_target="tpu_custom_call" | custom-call | bytes 1048576 | tf_op jit(solution)/shard_map/pallas_call | solution.py:495
  32.8 1.9 %collective-permute-done.2.refs_5_ = bf16[768,128]{1,0:T(8,128)(2,1)S(1)} collective-permute-done((bf16[768,128]{1,0:T(8,128)(2,1)S(1)}, bf16[768,128]{1,0:T(8,128)(2,1)S(1)}, u32[]{:S(2)}, u32[]{:S(2)}) %collective-permute-start.2) | collective-permute-done | bytes 196640 | tf_op jit(solution)/shard_map/ppermute | solution.py:542
  34.7 3.1 %collective-permute-done.3.refs_6_ = bf16[768,128]{1,0:T(8,128)(2,1)S(1)} collective-permute-done((bf16[768,128]{1,0:T(8,128)(2,1)S(1)}, bf16[768,128]{1,0:T(8,128)(2,1)S(1)}, u32[]{:S(2)}, u32[]{:S(2)}) %collective-permute-start.3) | collective-permute-done | bytes 196640 | tf_op jit(solution)/shard_map/ppermute | solution.py:542
  37.8 0.0 collective-permute-done.4.refs_7_
  37.8 1.9 %collective-permute-done.5.refs_8_ = bf16[768,128]{1,0:T(8,128)(2,1)S(1)} collective-permute-done((bf16[768,128]{1,0:T(8,128)(2,1)S(1)}, bf16[768,128]{1,0:T(8,128)(2,1)S(1)}, u32[]{:S(2)}, u32[]{:S(2)}) %collective-permute-start.5) | collective-permute-done | bytes 196640 | tf_op jit(solution)/shard_map/ppermute | solution.py:542
  39.7 1.1 collective-permute-done.6.refs_9_
  40.8 0.0 copy-start
  40.8 5.3 %all-to-all-start.1 = ((bf16[8,256,128]{2,1,0:T(8,128)(2,1)}), bf16[8,256,128]{2,1,0:T(8,128)(2,1)S(1)}, u32[]{:S(2)}, u32[]{:S(2)}) async-start(bf16[8,256,128]{2,1,0:T(8,128)(2,1)} %shard_map.85), calls=%async_computation.1 | async-start | bytes 1048576 | tf_op jit(solution)/shard_map/all_to_all | solution.py:547
  46.1 0.0 copy-done.2
  46.1 13.4 %shard_map.86 = (bf16[8,256,128]{2,1,0:T(8,128)(2,1)}, f32[8,512,128]{2,1,0:T(8,128)}) custom-call(s32[1]{0:T(128)} %bitcast.refs_0_, s32[8,16]{1,0:T(8,128)S(1)} %copy-done.2, bf16[768,128]{1,0:T(8,128)(2,1)S(1)} %get-tuple-element.39.refs_2_, bf16[768,128]{1,0:T(8,128)(2,1)S(1)} %collective-permute-done.refs_3_, ...), custom_call_target="tpu_custom_call" | custom-call | flops 12884901888 | bytes 8388608 | tf_op jit(solution)/shard_map/pallas_call | solution.py:429
  59.5 0.0 copy-done
  59.5 0.0 all-to-all-done.1.refs_10_
  59.5 6.0 %all-to-all-start = ((bf16[8,256,128]{2,1,0:T(8,128)(2,1)}), bf16[8,256,128]{2,1,0:T(8,128)(2,1)S(1)}, u32[]{:S(2)}, u32[]{:S(2)}) async-start(bf16[8,256,128]{2,1,0:T(8,128)(2,1)} %get-tuple-element.47), calls=%async_computation | async-start | bytes 1048576 | tf_op jit(solution)/shard_map/all_to_all | solution.py:547
  65.5 0.0 copy-start.1
  65.5 0.9 copy-done.1
  66.5 14.3 %shard_map.87 = (bf16[768,128]{1,0:T(8,128)(2,1)S(1)}, bf16[768,128]{1,0:T(8,128)(2,1)S(1)}, bf16[768,128]{1,0:T(8,128)(2,1)S(1)}, bf16[768,128]{1,0:T(8,128)(2,...) custom-call(s32[1]{0:T(128)} %bitcast.refs_0_, ...), custom_call_target="tpu_custom_call" | custom-call | flops 12884901888 | bytes 8388608 | tf_op jit(solution)/shard_map/pallas_call | solution.py:429
  80.8 1.5 %collective-permute-start.7 = (bf16[768,128]{1,0:T(8,128)(2,1)S(1)}, bf16[768,128]{1,0:T(8,128)(2,1)S(1)}, u32[]{:S(2)}, u32[]{:S(2)}) collective-permute-start(bf16[768,128]{1,0:T(8,128)(2,1)S(1)} %get-tuple-element.51), channel_id=1, source_target_pairs={{0,4},{4,8},{8,12},{12,16},{16,20},{20,24},{24,28},{28,0},{1,5},{5... | collective-permute-start | bytes 589832 | tf_op jit(solution)/shard_map/ppermute | solution.py:542
  82.3 1.5 %collective-permute-start.8 = (bf16[768,128]{1,0:T(8,128)(2,1)S(1)}, bf16[768,128]{1,0:T(8,128)(2,1)S(1)}, u32[]{:S(2)}, u32[]{:S(2)}) collective-permute-start(bf16[768,128]{1,0:T(8,128)(2,1)S(1)} %get-tuple-element.52), channel_id=1, source_target_pairs={{0,8},{4,12},{8,16},{12,20},{16,24},{20,28},{24,0},{28,4},{1,9},{5... | collective-permute-start | bytes 589832 | tf_op jit(solution)/shard_map/ppermute | solution.py:542
  83.8 1.5 %collective-permute-start.9 = (bf16[768,128]{1,0:T(8,128)(2,1)}, bf16[768,128]{1,0:T(8,128)(2,1)S(1)}, u32[]{:S(2)}, u32[]{:S(2)}) collective-permute-start(bf16[768,128]{1,0:T(8,128)(2,1)} %get-tuple-element.53), channel_id=1, source_target_pairs={{0,12},{4,16},{8,20},{12,24},{16,28},{20,0},{24,4},{28,8},{1,13},{... | collective-permute-start | bytes 589832 | tf_op jit(solution)/shard_map/ppermute | solution.py:542
  85.3 1.5 %collective-permute-start.10 = (bf16[768,128]{1,0:T(8,128)(2,1)S(1)}, bf16[768,128]{1,0:T(8,128)(2,1)S(1)}, u32[]{:S(2)}, u32[]{:S(2)}) collective-permute-start(bf16[768,128]{1,0:T(8,128)(2,1)S(1)} %get-tuple-element.54), channel_id=1, source_target_pairs={{0,16},{4,20},{8,24},{12,28},{16,0},{20,4},{24,8},{28,12},{1,17},{... | collective-permute-start | bytes 589832 | tf_op jit(solution)/shard_map/ppermute | solution.py:542
  86.7 1.5 %collective-permute-start.11 = (bf16[768,128]{1,0:T(8,128)(2,1)S(1)}, bf16[768,128]{1,0:T(8,128)(2,1)S(1)}, u32[]{:S(2)}, u32[]{:S(2)}) collective-permute-start(bf16[768,128]{1,0:T(8,128)(2,1)S(1)} %get-tuple-element.55), channel_id=1, source_target_pairs={{0,20},{4,24},{8,28},{12,0},{16,4},{20,8},{24,12},{28,16},{1,21},{... | collective-permute-start | bytes 589832 | tf_op jit(solution)/shard_map/ppermute | solution.py:542
  88.2 1.3 %collective-permute-done.7.refs_3_ = bf16[768,128]{1,0:T(8,128)(2,1)S(1)} collective-permute-done((bf16[768,128]{1,0:T(8,128)(2,1)S(1)}, bf16[768,128]{1,0:T(8,128)(2,1)S(1)}, u32[]{:S(2)}, u32[]{:S(2)}) %collective-permute-start.7) | collective-permute-done | bytes 196640 | tf_op jit(solution)/shard_map/ppermute | solution.py:542
  89.5 0.0 collective-permute-start.12
  89.5 19.3 %collective-permute-done.8.refs_4_ = bf16[768,128]{1,0:T(8,128)(2,1)S(1)} collective-permute-done((bf16[768,128]{1,0:T(8,128)(2,1)S(1)}, bf16[768,128]{1,0:T(8,128)(2,1)S(1)}, u32[]{:S(2)}, u32[]{:S(2)}) %collective-permute-start.8) | collective-permute-done | bytes 196640 | tf_op jit(solution)/shard_map/ppermute | solution.py:542
  108.8 0.0 collective-permute-start.13
  108.8 0.0 all-to-all-done.refs_1_
  108.8 3.2 %collective-permute-done.9.refs_5_ = bf16[768,128]{1,0:T(8,128)(2,1)S(1)} collective-permute-done((bf16[768,128]{1,0:T(8,128)(2,1)}, bf16[768,128]{1,0:T(8,128)(2,1)S(1)}, u32[]{:S(2)}, u32[]{:S(2)}) %collective-permute-start.9) | collective-permute-done | bytes 196640 | tf_op jit(solution)/shard_map/ppermute | solution.py:542
  112.0 2.0 %collective-permute-done.10.refs_6_ = bf16[768,128]{1,0:T(8,128)(2,1)S(1)} collective-permute-done((bf16[768,128]{1,0:T(8,128)(2,1)S(1)}, bf16[768,128]{1,0:T(8,128)(2,1)S(1)}, u32[]{:S(2)}, u32[]{:S(2)}) %collective-permute-start.10) | collective-permute-done | bytes 196640 | tf_op jit(solution)/shard_map/ppermute | solution.py:542
  114.0 0.0 collective-permute-done.11.refs_7_
  114.0 1.6 %collective-permute-done.12.refs_8_ = bf16[768,128]{1,0:T(8,128)(2,1)S(1)} collective-permute-done((bf16[768,128]{1,0:T(8,128)(2,1)S(1)}, bf16[768,128]{1,0:T(8,128)(2,1)S(1)}, u32[]{:S(2)}, u32[]{:S(2)}) %collective-permute-start.12) | collective-permute-done | bytes 196640 | tf_op jit(solution)/shard_map/ppermute | solution.py:542
  115.6 1.6 %collective-permute-done.13.refs_9_ = bf16[768,128]{1,0:T(8,128)(2,1)S(1)} collective-permute-done((bf16[768,128]{1,0:T(8,128)(2,1)S(1)}, bf16[768,128]{1,0:T(8,128)(2,1)S(1)}, u32[]{:S(2)}, u32[]{:S(2)}) %collective-permute-start.13) | collective-permute-done | bytes 196640 | tf_op jit(solution)/shard_map/ppermute | solution.py:542
  117.3 1.9 %shard_map.88 = (bf16[512,512]{1,0:T(8,128)(2,1)}, bf16[512,512]{1,0:T(8,128)(2,1)}, bf16[512,512]{1,0:T(8,128)(2,1)}, bf16[512,512]{1,0:T(8,128)(2,1)}) custom-call(s32[1]{0:T(128)} %bitcast.refs_0_, bf16[8,256,128]{2,1,0:T(8,128)(2,1)S(1)} %all-to-all-done.refs_1_, bf16[768,128]{1,0:T(8,128)(2,1)S(1)} %get-tuple-element.50.refs_2_, ...), custom_call_target="tpu_custom_call" | custom-call | tf_op jit(solution)/shard_map/pallas_call | solution.py:528
Async XLA Ops:
  0.6 45.4 %copy-start.2 = (s32[8,16]{1,0:T(8,128)S(1)}, s32[8,16]{1,0:T(8,128)}, u32[]{:S(2)}) copy-start(s32[8,16]{1,0:T(8,128)} %refs_1_.7) | copy-start | bytes 1540
  2.6 7.3 %collective-permute-start = (bf16[768,128]{1,0:T(8,128)(2,1)S(1)}, bf16[768,128]{1,0:T(8,128)(2,1)S(1)}, u32[]{:S(2)}, u32[]{:S(2)}) collective-permute-start(bf16[768,128]{1,0:T(8,128)(2,1)S(1)} %get-tuple-element.32), channel_id=1, source_target_pairs={{0,4},{4,8},{8,12},{12,16},{16,20},{20,24},{24,28},{28,0},{1,5},{5... | collective-permute-start | bytes 589832 | tf_op jit(solution)/shard_map/ppermute | solution.py:542
  4.1 26.4 %collective-permute-start.1 = (bf16[768,128]{1,0:T(8,128)(2,1)S(1)}, bf16[768,128]{1,0:T(8,128)(2,1)S(1)}, u32[]{:S(2)}, u32[]{:S(2)}) collective-permute-start(bf16[768,128]{1,0:T(8,128)(2,1)S(1)} %get-tuple-element.33), channel_id=1, source_target_pairs={{0,8},{4,12},{8,16},{12,20},{16,24},{20,28},{24,0},{28,4},{1,9},{5... | collective-permute-start | bytes 589832 | tf_op jit(solution)/shard_map/ppermute | solution.py:542
  5.7 29.0 %collective-permute-start.2 = (bf16[768,128]{1,0:T(8,128)(2,1)S(1)}, bf16[768,128]{1,0:T(8,128)(2,1)S(1)}, u32[]{:S(2)}, u32[]{:S(2)}) collective-permute-start(bf16[768,128]{1,0:T(8,128)(2,1)S(1)} %get-tuple-element.34), channel_id=1, source_target_pairs={{0,12},{4,16},{8,20},{12,24},{16,28},{20,0},{24,4},{28,8},{1,13},{... | collective-permute-start | bytes 589832 | tf_op jit(solution)/shard_map/ppermute | solution.py:542
  6.9 30.9 %collective-permute-start.3 = (bf16[768,128]{1,0:T(8,128)(2,1)S(1)}, bf16[768,128]{1,0:T(8,128)(2,1)S(1)}, u32[]{:S(2)}, u32[]{:S(2)}) collective-permute-start(bf16[768,128]{1,0:T(8,128)(2,1)S(1)} %get-tuple-element.35), channel_id=1, source_target_pairs={{0,16},{4,20},{8,24},{12,28},{16,0},{20,4},{24,8},{28,12},{1,17},{... | collective-permute-start | bytes 589832 | tf_op jit(solution)/shard_map/ppermute | solution.py:542
  8.6 29.2 %collective-permute-start.4 = (bf16[768,128]{1,0:T(8,128)(2,1)S(1)}, bf16[768,128]{1,0:T(8,128)(2,1)S(1)}, u32[]{:S(2)}, u32[]{:S(2)}) collective-permute-start(bf16[768,128]{1,0:T(8,128)(2,1)S(1)} %get-tuple-element.36), channel_id=1, source_target_pairs={{0,20},{4,24},{8,28},{12,0},{16,4},{20,8},{24,12},{28,16},{1,21},{... | collective-permute-start | bytes 589832 | tf_op jit(solution)/shard_map/ppermute | solution.py:542
  9.9 29.8 %collective-permute-start.5 = (bf16[768,128]{1,0:T(8,128)(2,1)S(1)}, bf16[768,128]{1,0:T(8,128)(2,1)S(1)}, u32[]{:S(2)}, u32[]{:S(2)}) collective-permute-start(bf16[768,128]{1,0:T(8,128)(2,1)S(1)} %get-tuple-element.37), channel_id=1, source_target_pairs={{0,24},{4,28},{8,0},{12,4},{16,8},{20,12},{24,16},{28,20},{1,25},{... | collective-permute-start | bytes 589832 | tf_op jit(solution)/shard_map/ppermute | solution.py:542
  30.5 10.3 %collective-permute-start.6 = (bf16[768,128]{1,0:T(8,128)(2,1)S(1)}, bf16[768,128]{1,0:T(8,128)(2,1)S(1)}, u32[]{:S(2)}, u32[]{:S(2)}) collective-permute-start(bf16[768,128]{1,0:T(8,128)(2,1)S(1)} %get-tuple-element.38), channel_id=1, source_target_pairs={{0,28},{4,0},{8,4},{12,8},{16,12},{20,16},{24,20},{28,24},{1,29},{... | collective-permute-start | bytes 589832 | tf_op jit(solution)/shard_map/ppermute | solution.py:542
  40.8 18.7 %copy-start = (bf16[768,128]{1,0:T(8,128)(2,1)}, bf16[768,128]{1,0:T(8,128)(2,1)S(1)}, u32[]{:S(2)}) copy-start(bf16[768,128]{1,0:T(8,128)(2,1)S(1)} %collective-permute-done.6.refs_9_) | copy-start | bytes 589828
  40.8 18.7 %all-to-all-start.1 = ((bf16[8,256,128]{2,1,0:T(8,128)(2,1)}), bf16[8,256,128]{2,1,0:T(8,128)(2,1)S(1)}, u32[]{:S(2)}, u32[]{:S(2)}) async-start(bf16[8,256,128]{2,1,0:T(8,128)(2,1)} %shard_map.85), calls=%async_computation.1 | async-start | bytes 1048576 | tf_op jit(solution)/shard_map/all_to_all | solution.py:547
  59.5 49.2 %all-to-all-start = ((bf16[8,256,128]{2,1,0:T(8,128)(2,1)}), bf16[8,256,128]{2,1,0:T(8,128)(2,1)S(1)}, u32[]{:S(2)}, u32[]{:S(2)}) async-start(bf16[8,256,128]{2,1,0:T(8,128)(2,1)} %get-tuple-element.47), calls=%async_computation | async-start | bytes 1048576 | tf_op jit(solution)/shard_map/all_to_all | solution.py:547
  65.5 0.9 copy-start.1
  80.8 8.7 %collective-permute-start.7 = (bf16[768,128]{1,0:T(8,128)(2,1)S(1)}, bf16[768,128]{1,0:T(8,128)(2,1)S(1)}, u32[]{:S(2)}, u32[]{:S(2)}) collective-permute-start(bf16[768,128]{1,0:T(8,128)(2,1)S(1)} %get-tuple-element.51), channel_id=1, source_target_pairs={{0,4},{4,8},{8,12},{12,16},{16,20},{20,24},{24,28},{28,0},{1,5},{5... | collective-permute-start | bytes 589832 | tf_op jit(solution)/shard_map/ppermute | solution.py:542
  82.3 26.4 %collective-permute-start.8 = (bf16[768,128]{1,0:T(8,128)(2,1)S(1)}, bf16[768,128]{1,0:T(8,128)(2,1)S(1)}, u32[]{:S(2)}, u32[]{:S(2)}) collective-permute-start(bf16[768,128]{1,0:T(8,128)(2,1)S(1)} %get-tuple-element.52), channel_id=1, source_target_pairs={{0,8},{4,12},{8,16},{12,20},{16,24},{20,28},{24,0},{28,4},{1,9},{5... | collective-permute-start | bytes 589832 | tf_op jit(solution)/shard_map/ppermute | solution.py:542
  83.8 28.2 %collective-permute-start.9 = (bf16[768,128]{1,0:T(8,128)(2,1)}, bf16[768,128]{1,0:T(8,128)(2,1)S(1)}, u32[]{:S(2)}, u32[]{:S(2)}) collective-permute-start(bf16[768,128]{1,0:T(8,128)(2,1)} %get-tuple-element.53), channel_id=1, source_target_pairs={{0,12},{4,16},{8,20},{12,24},{16,28},{20,0},{24,4},{28,8},{1,13},{... | collective-permute-start | bytes 589832 | tf_op jit(solution)/shard_map/ppermute | solution.py:542
  85.3 28.7 %collective-permute-start.10 = (bf16[768,128]{1,0:T(8,128)(2,1)S(1)}, bf16[768,128]{1,0:T(8,128)(2,1)S(1)}, u32[]{:S(2)}, u32[]{:S(2)}) collective-permute-start(bf16[768,128]{1,0:T(8,128)(2,1)S(1)} %get-tuple-element.54), channel_id=1, source_target_pairs={{0,16},{4,20},{8,24},{12,28},{16,0},{20,4},{24,8},{28,12},{1,17},{... | collective-permute-start | bytes 589832 | tf_op jit(solution)/shard_map/ppermute | solution.py:542
  86.7 27.2 %collective-permute-start.11 = (bf16[768,128]{1,0:T(8,128)(2,1)S(1)}, bf16[768,128]{1,0:T(8,128)(2,1)S(1)}, u32[]{:S(2)}, u32[]{:S(2)}) collective-permute-start(bf16[768,128]{1,0:T(8,128)(2,1)S(1)} %get-tuple-element.55), channel_id=1, source_target_pairs={{0,20},{4,24},{8,28},{12,0},{16,4},{20,8},{24,12},{28,16},{1,21},{... | collective-permute-start | bytes 589832 | tf_op jit(solution)/shard_map/ppermute | solution.py:542
  89.5 26.1 %collective-permute-start.12 = (bf16[768,128]{1,0:T(8,128)(2,1)S(1)}, bf16[768,128]{1,0:T(8,128)(2,1)S(1)}, u32[]{:S(2)}, u32[]{:S(2)}) collective-permute-start(bf16[768,128]{1,0:T(8,128)(2,1)S(1)} %get-tuple-element.56), channel_id=1, source_target_pairs={{0,24},{4,28},{8,0},{12,4},{16,8},{20,12},{24,16},{28,20},{1,25},{... | collective-permute-start | bytes 589832 | tf_op jit(solution)/shard_map/ppermute | solution.py:542
  108.8 8.5 %collective-permute-start.13 = (bf16[768,128]{1,0:T(8,128)(2,1)S(1)}, bf16[768,128]{1,0:T(8,128)(2,1)S(1)}, u32[]{:S(2)}, u32[]{:S(2)}) collective-permute-start(bf16[768,128]{1,0:T(8,128)(2,1)S(1)} %get-tuple-element.57), channel_id=1, source_target_pairs={{0,28},{4,0},{8,4},{12,8},{16,12},{20,16},{24,20},{28,24},{1,29},{... | collective-permute-start | bytes 589832 | tf_op jit(solution)/shard_map/ppermute | solution.py:542

commit v4 on v3

--- a/solution.py
+++ b/solution.py
@@ -213,10 +213,14 @@
                 steps.remove(step)
 
 
+def tn(a, b):
+    return lax.dot_general(a, b, (((0,), (0,)), ((), ())), preferred_element_type=jnp.float32)
+
+
 class Block:
-    def __init__(self, b, partners, rows, first_query, table, kv, kv_t, block, scores, gathered, sg, wl, dacc, oq):
+    def __init__(self, b, partners, rows, first_query, table, kv, block, scores, gathered, sg, wl, dacc, oq):
         self.oq = oq
-        self.kv, self.kv_t, self.scores, self.gathered, self.dacc, self.b = kv, kv_t, scores, gathered, dacc, b
+        self.kv, self.scores, self.gathered, self.dacc, self.b = kv, scores, gathered, dacc, b
         self.sg, self.wl = sg, wl
         self.queries = queries = block.shape[0]
         width = 2 * HD
@@ -247,7 +251,6 @@
                 place = (entry // (rows // SUB), pl.multiple_of(entry % (rows // SUB) * SUB, SUB))
                 self.extra_places.append(place)
                 gathered[e * SUB : (e + 1) * SUB, :] = kv[place[0], pl.ds(place[1], SUB), :]
-            self.gathered_t = jnp.transpose(gathered[: entries * SUB, :])
             self.chunks.append((None, 0, entries * SUB, "extra"))
         self.places = []
         at = 0
@@ -260,12 +263,6 @@
         if kind == "extra":
             return self.gathered[:count, :]
         return self.kv[block, first : first + count, :]
-
-    def keys_t(self, chunk):
-        block, first, count, kind = chunk
-        if kind == "extra":
-            return self.gathered_t
-        return self.kv_t[block, :, first : first + count]
 
     def score(self):
         peak = jnp.full((8, self.queries), LOWEST, jnp.float32)
@@ -287,7 +284,7 @@
         for chunk, place in zip(self.chunks, self.places):
             w = jnp.exp2(self.scores[place, :] - self.top)
             total = total + by_eights(w, jnp.add)
-            mixed = mixed + nn(self.keys_t(chunk)[HD:], w.astype(CAST))
+            mixed = mixed + tn(self.keys(chunk), w.astype(CAST))[HD:]
             yield
         total = jnp.sum(total, axis=0, keepdims=True)
         self.mixed = mixed / total
@@ -306,7 +303,7 @@
         query_grad = jnp.zeros((HD, self.queries), jnp.float32)
         for chunk, place in zip(self.chunks, self.places):
             sg = self.sg[place, :]
-            query_grad = query_grad + nn(self.keys_t(chunk)[:HD], sg)
+            query_grad = query_grad + tn(self.keys(chunk), sg)[:HD]
             part = nn(jnp.concatenate([sg, self.wl[place, :]], axis=1), self.qg_part)
             block, first, count, kind = chunk
             if kind == "extra":
@@ -334,24 +331,23 @@
     if last:
         qd, sums = take(2)
         out = take(blocks)
-        kv, kv_t, scores, gathered, sg, wl, dacc, held, moved, oq = take(10)
+        kv, scores, gathered, sg, wl, dacc, held, moved, oq = take(9)
         for b in range(blocks):
             pltpu.make_async_copy(sums.at[b], held.at[b], moved.at[b]).start()
     else:
-        oq, sums, kv, kv_t, scores, gathered, sg, wl, dacc, held, moved, qd = take(12)
+        oq, sums, kv, scores, gathered, sg, wl, dacc, held, moved, qd = take(11)
     dacc[...] = jnp.zeros_like(dacc)
     for k in range(blocks):
         b = wrapped(me - k, blocks)
         keys = early[k][:rows, :]
         kv[b] = keys
-        kv_t[b] = jnp.transpose(keys)
         if not last:
             qd[b] = early[k][rows:, :]
     levels = (blocks - 1).bit_length()
 
     def run(partners, ids):
         work = [
-            Block(b, partners, rows, first_query, table, kv, kv_t, qd[b], scores.at[i], gathered.at[i], sg.at[i],
+            Block(b, partners, rows, first_query, table, kv, qd[b], scores.at[i], gathered.at[i], sg.at[i],
                   wl.at[i], dacc, oq)
             for i, b in enumerate(ids)
         ]
@@ -417,7 +413,6 @@
     list_rows = first_query + queries + levels * rows + extra_rows
     scratch = [
         pltpu.VMEM((blocks, rows, width), CAST),
-        pltpu.VMEM((blocks, width, rows), CAST),
         pltpu.VMEM((together, list_rows, queries), jnp.float32),
         pltpu.VMEM((together, extra_rows, width), CAST),
         pltpu.VMEM((together, list_rows, queries), CAST),

time: 120 us -> 119 us (level)
  no operation moved by 1% of the time
where the time goes in v4:
time: 119 us
  waiting for transfers between devices  56.4 us (47%)
  Pallas kernels  33.7 us (28%)
  starting transfers between devices  27.2 us (23%)
    ppermute x14, waiting for transfers between devices, shifted_all(): lax.ppermute(pieces[k], 'tm', [(i, (i + k) % count) for i in range(count)])  56.4 us
    pallas_call x2, Pallas kernels, attention(): pl.pallas_call(functools.partial(attention_kernel, blocks, rows, first_qu...  27.6 us
    ppermute x14, starting transfers between devices, shifted_all(): lax.ppermute(pieces[k], 'tm', [(i, (i + k) % count) for i in range(count)])  15.9 us
    all_to_all x2, starting transfers between devices, all_heads(): return lax.all_to_all(packed, 'tm', split_axis=0, concat_axis=0, tiled=True)  11.3 us
    pallas_call x2, Pallas kernels, pack(): pl.pallas_call(functools.partial(pack_kernel, heads, pieces, apart, len(a...  4.2 us
  transfers between devices with their start and end apart: 16, of which 11 were waited for; matrix products, arithmetic and copies ran while one was open for 0% of the time, Pallas kernels for 25%

profile of v4, /device:TPU:12, one launch (start us, length us, event | category | flops | bytes accessed | tf_op | source)
XLA Modules:
  0.0 119.0 jit_solution(2448691247598560906)
XLA Ops:
  0.6 0.0 copy-start.2
  0.6 1.9 %shard_map.84 = (bf16[768,128]{1,0:T(8,128)(2,1)S(1)}, bf16[768,128]{1,0:T(8,128)(2,1)S(1)}, bf16[768,128]{1,0:T(8,128)(2,1)S(1)}, bf16[768,128]{1,0:T(8,128)(2,...) custom-call(s32[1]{0:T(128)} %bitcast.refs_0_, ...), custom_call_target="tpu_custom_call" | custom-call | bytes 3145728 | tf_op jit(solution)/shard_map/pallas_call | solution.py:490
  2.6 1.6 %collective-permute-start = (bf16[768,128]{1,0:T(8,128)(2,1)S(1)}, bf16[768,128]{1,0:T(8,128)(2,1)S(1)}, u32[]{:S(2)}, u32[]{:S(2)}) collective-permute-start(bf16[768,128]{1,0:T(8,128)(2,1)S(1)} %get-tuple-element.32), channel_id=1, source_target_pairs={{0,4},{4,8},{8,12},{12,16},{16,20},{20,24},{24,28},{28,0},{1,5},{5... | collective-permute-start | bytes 589832 | tf_op jit(solution)/shard_map/ppermute | solution.py:537
  4.1 1.6 %collective-permute-start.1 = (bf16[768,128]{1,0:T(8,128)(2,1)S(1)}, bf16[768,128]{1,0:T(8,128)(2,1)S(1)}, u32[]{:S(2)}, u32[]{:S(2)}) collective-permute-start(bf16[768,128]{1,0:T(8,128)(2,1)S(1)} %get-tuple-element.33), channel_id=1, source_target_pairs={{0,8},{4,12},{8,16},{12,20},{16,24},{20,28},{24,0},{28,4},{1,9},{5... | collective-permute-start | bytes 589832 | tf_op jit(solution)/shard_map/ppermute | solution.py:537
  5.7 1.2 collective-permute-start.2
  6.9 1.7 %collective-permute-start.3 = (bf16[768,128]{1,0:T(8,128)(2,1)S(1)}, bf16[768,128]{1,0:T(8,128)(2,1)S(1)}, u32[]{:S(2)}, u32[]{:S(2)}) collective-permute-start(bf16[768,128]{1,0:T(8,128)(2,1)S(1)} %get-tuple-element.35), channel_id=1, source_target_pairs={{0,16},{4,20},{8,24},{12,28},{16,0},{20,4},{24,8},{28,12},{1,17},{... | collective-permute-start | bytes 589832 | tf_op jit(solution)/shard_map/ppermute | solution.py:537
  8.6 1.3 %collective-permute-start.4 = (bf16[768,128]{1,0:T(8,128)(2,1)S(1)}, bf16[768,128]{1,0:T(8,128)(2,1)S(1)}, u32[]{:S(2)}, u32[]{:S(2)}) collective-permute-start(bf16[768,128]{1,0:T(8,128)(2,1)S(1)} %get-tuple-element.36), channel_id=1, source_target_pairs={{0,20},{4,24},{8,28},{12,0},{16,4},{20,8},{24,12},{28,16},{1,21},{... | collective-permute-start | bytes 589832 | tf_op jit(solution)/shard_map/ppermute | solution.py:537
  9.9 0.0 collective-permute-done.refs_3_
  9.9 1.2 %collective-permute-start.5 = (bf16[768,128]{1,0:T(8,128)(2,1)S(1)}, bf16[768,128]{1,0:T(8,128)(2,1)S(1)}, u32[]{:S(2)}, u32[]{:S(2)}) collective-permute-start(bf16[768,128]{1,0:T(8,128)(2,1)S(1)} %get-tuple-element.37), channel_id=1, source_target_pairs={{0,24},{4,28},{8,0},{12,4},{16,8},{20,12},{24,16},{28,20},{1,25},{... | collective-permute-start | bytes 589832 | tf_op jit(solution)/shard_map/ppermute | solution.py:537
  11.1 19.4 %collective-permute-done.1.refs_4_ = bf16[768,128]{1,0:T(8,128)(2,1)S(1)} collective-permute-done((bf16[768,128]{1,0:T(8,128)(2,1)S(1)}, bf16[768,128]{1,0:T(8,128)(2,1)S(1)}, u32[]{:S(2)}, u32[]{:S(2)}) %collective-permute-start.1) | collective-permute-done | bytes 196640 | tf_op jit(solution)/shard_map/ppermute | solution.py:537
  30.5 0.0 collective-permute-start.6
  30.5 2.3 %shard_map.85 = bf16[8,256,128]{2,1,0:T(8,128)(2,1)} custom-call(s32[1]{0:T(128)} %bitcast.refs_0_, bf16[512,512]{1,0:T(8,128)(2,1)} %refs_1_.5, bf16[512,512]{1,0:T(8,128)(2,1)} %refs_2_.3), custom_call_target="tpu_custom_call" | custom-call | bytes 1048576 | tf_op jit(solution)/shard_map/pallas_call | solution.py:490
  32.8 1.9 %collective-permute-done.2.refs_5_ = bf16[768,128]{1,0:T(8,128)(2,1)S(1)} collective-permute-done((bf16[768,128]{1,0:T(8,128)(2,1)S(1)}, bf16[768,128]{1,0:T(8,128)(2,1)S(1)}, u32[]{:S(2)}, u32[]{:S(2)}) %collective-permute-start.2) | collective-permute-done | bytes 196640 | tf_op jit(solution)/shard_map/ppermute | solution.py:537
  34.7 3.1 %collective-permute-done.3.refs_6_ = bf16[768,128]{1,0:T(8,128)(2,1)S(1)} collective-permute-done((bf16[768,128]{1,0:T(8,128)(2,1)S(1)}, bf16[768,128]{1,0:T(8,128)(2,1)S(1)}, u32[]{:S(2)}, u32[]{:S(2)}) %collective-permute-start.3) | collective-permute-done | bytes 196640 | tf_op jit(solution)/shard_map/ppermute | solution.py:537
  37.8 0.0 collective-permute-done.4.refs_7_
  37.8 1.9 %collective-permute-done.5.refs_8_ = bf16[768,128]{1,0:T(8,128)(2,1)S(1)} collective-permute-done((bf16[768,128]{1,0:T(8,128)(2,1)S(1)}, bf16[768,128]{1,0:T(8,128)(2,1)S(1)}, u32[]{:S(2)}, u32[]{:S(2)}) %collective-permute-start.5) | collective-permute-done | bytes 196640 | tf_op jit(solution)/shard_map/ppermute | solution.py:537
  39.7 1.1 collective-permute-done.6.refs_9_
  40.8 0.0 copy-start
  40.8 5.3 %all-to-all-start.1 = ((bf16[8,256,128]{2,1,0:T(8,128)(2,1)}), bf16[8,256,128]{2,1,0:T(8,128)(2,1)S(1)}, u32[]{:S(2)}, u32[]{:S(2)}) async-start(bf16[8,256,128]{2,1,0:T(8,128)(2,1)} %shard_map.85), calls=%async_computation.1 | async-start | bytes 1048576 | tf_op jit(solution)/shard_map/all_to_all | solution.py:542
  46.1 0.0 copy-done.2
  46.1 13.3 %shard_map.86 = (bf16[8,256,128]{2,1,0:T(8,128)(2,1)}, f32[8,512,128]{2,1,0:T(8,128)}) custom-call(s32[1]{0:T(128)} %bitcast.refs_0_, s32[8,16]{1,0:T(8,128)S(1)} %copy-done.2, bf16[768,128]{1,0:T(8,128)(2,1)S(1)} %get-tuple-element.39.refs_2_, bf16[768,128]{1,0:T(8,128)(2,1)S(1)} %collective-permute-done.refs_3_, ...), custom_call_target="tpu_custom_call" | custom-call | flops 12884901888 | bytes 8388608 | tf_op jit(solution)/shard_map/pallas_call | solution.py:424
  59.4 0.0 copy-done
  59.4 0.0 all-to-all-done.1.refs_10_
  59.4 6.0 %all-to-all-start = ((bf16[8,256,128]{2,1,0:T(8,128)(2,1)}), bf16[8,256,128]{2,1,0:T(8,128)(2,1)S(1)}, u32[]{:S(2)}, u32[]{:S(2)}) async-start(bf16[8,256,128]{2,1,0:T(8,128)(2,1)} %get-tuple-element.47), calls=%async_computation | async-start | bytes 1048576 | tf_op jit(solution)/shard_map/all_to_all | solution.py:542
  65.4 0.0 copy-start.1
  65.4 0.9 copy-done.1
  66.4 14.3 %shard_map.87 = (bf16[768,128]{1,0:T(8,128)(2,1)S(1)}, bf16[768,128]{1,0:T(8,128)(2,1)S(1)}, bf16[768,128]{1,0:T(8,128)(2,1)S(1)}, bf16[768,128]{1,0:T(8,128)(2,...) custom-call(s32[1]{0:T(128)} %bitcast.refs_0_, ...), custom_call_target="tpu_custom_call" | custom-call | flops 12884901888 | bytes 8388608 | tf_op jit(solution)/shard_map/pallas_call | solution.py:424
  80.6 1.5 %collective-permute-start.7 = (bf16[768,128]{1,0:T(8,128)(2,1)S(1)}, bf16[768,128]{1,0:T(8,128)(2,1)S(1)}, u32[]{:S(2)}, u32[]{:S(2)}) collective-permute-start(bf16[768,128]{1,0:T(8,128)(2,1)S(1)} %get-tuple-element.51), channel_id=1, source_target_pairs={{0,4},{4,8},{8,12},{12,16},{16,20},{20,24},{24,28},{28,0},{1,5},{5... | collective-permute-start | bytes 589832 | tf_op jit(solution)/shard_map/ppermute | solution.py:537
  82.1 1.5 %collective-permute-start.8 = (bf16[768,128]{1,0:T(8,128)(2,1)S(1)}, bf16[768,128]{1,0:T(8,128)(2,1)S(1)}, u32[]{:S(2)}, u32[]{:S(2)}) collective-permute-start(bf16[768,128]{1,0:T(8,128)(2,1)S(1)} %get-tuple-element.52), channel_id=1, source_target_pairs={{0,8},{4,12},{8,16},{12,20},{16,24},{20,28},{24,0},{28,4},{1,9},{5... | collective-permute-start | bytes 589832 | tf_op jit(solution)/shard_map/ppermute | solution.py:537
  83.6 1.5 %collective-permute-start.9 = (bf16[768,128]{1,0:T(8,128)(2,1)}, bf16[768,128]{1,0:T(8,128)(2,1)S(1)}, u32[]{:S(2)}, u32[]{:S(2)}) collective-permute-start(bf16[768,128]{1,0:T(8,128)(2,1)} %get-tuple-element.53), channel_id=1, source_target_pairs={{0,12},{4,16},{8,20},{12,24},{16,28},{20,0},{24,4},{28,8},{1,13},{... | collective-permute-start | bytes 589832 | tf_op jit(solution)/shard_map/ppermute | solution.py:537
  85.1 1.5 %collective-permute-start.10 = (bf16[768,128]{1,0:T(8,128)(2,1)S(1)}, bf16[768,128]{1,0:T(8,128)(2,1)S(1)}, u32[]{:S(2)}, u32[]{:S(2)}) collective-permute-start(bf16[768,128]{1,0:T(8,128)(2,1)S(1)} %get-tuple-element.54), channel_id=1, source_target_pairs={{0,16},{4,20},{8,24},{12,28},{16,0},{20,4},{24,8},{28,12},{1,17},{... | collective-permute-start | bytes 589832 | tf_op jit(solution)/shard_map/ppermute | solution.py:537
  86.5 1.5 %collective-permute-start.11 = (bf16[768,128]{1,0:T(8,128)(2,1)S(1)}, bf16[768,128]{1,0:T(8,128)(2,1)S(1)}, u32[]{:S(2)}, u32[]{:S(2)}) collective-permute-start(bf16[768,128]{1,0:T(8,128)(2,1)S(1)} %get-tuple-element.55), channel_id=1, source_target_pairs={{0,20},{4,24},{8,28},{12,0},{16,4},{20,8},{24,12},{28,16},{1,21},{... | collective-permute-start | bytes 589832 | tf_op jit(solution)/shard_map/ppermute | solution.py:537
  88.0 1.2 %collective-permute-done.7.refs_3_ = bf16[768,128]{1,0:T(8,128)(2,1)S(1)} collective-permute-done((bf16[768,128]{1,0:T(8,128)(2,1)S(1)}, bf16[768,128]{1,0:T(8,128)(2,1)S(1)}, u32[]{:S(2)}, u32[]{:S(2)}) %collective-permute-start.7) | collective-permute-done | bytes 196640 | tf_op jit(solution)/shard_map/ppermute | solution.py:537
  89.2 0.0 collective-permute-start.12
  89.2 19.3 %collective-permute-done.8.refs_4_ = bf16[768,128]{1,0:T(8,128)(2,1)S(1)} collective-permute-done((bf16[768,128]{1,0:T(8,128)(2,1)S(1)}, bf16[768,128]{1,0:T(8,128)(2,1)S(1)}, u32[]{:S(2)}, u32[]{:S(2)}) %collective-permute-start.8) | collective-permute-done | bytes 196640 | tf_op jit(solution)/shard_map/ppermute | solution.py:537
  108.6 0.0 collective-permute-start.13
  108.6 0.0 all-to-all-done.refs_1_
  108.6 3.2 %collective-permute-done.9.refs_5_ = bf16[768,128]{1,0:T(8,128)(2,1)S(1)} collective-permute-done((bf16[768,128]{1,0:T(8,128)(2,1)}, bf16[768,128]{1,0:T(8,128)(2,1)S(1)}, u32[]{:S(2)}, u32[]{:S(2)}) %collective-permute-start.9) | collective-permute-done | bytes 196640 | tf_op jit(solution)/shard_map/ppermute | solution.py:537
  111.8 2.0 %collective-permute-done.10.refs_6_ = bf16[768,128]{1,0:T(8,128)(2,1)S(1)} collective-permute-done((bf16[768,128]{1,0:T(8,128)(2,1)S(1)}, bf16[768,128]{1,0:T(8,128)(2,1)S(1)}, u32[]{:S(2)}, u32[]{:S(2)}) %collective-permute-start.10) | collective-permute-done | bytes 196640 | tf_op jit(solution)/shard_map/ppermute | solution.py:537
  113.8 0.0 collective-permute-done.11.refs_7_
  113.8 1.6 %collective-permute-done.12.refs_8_ = bf16[768,128]{1,0:T(8,128)(2,1)S(1)} collective-permute-done((bf16[768,128]{1,0:T(8,128)(2,1)S(1)}, bf16[768,128]{1,0:T(8,128)(2,1)S(1)}, u32[]{:S(2)}, u32[]{:S(2)}) %collective-permute-start.12) | collective-permute-done | bytes 196640 | tf_op jit(solution)/shard_map/ppermute | solution.py:537
  115.4 1.6 %collective-permute-done.13.refs_9_ = bf16[768,128]{1,0:T(8,128)(2,1)S(1)} collective-permute-done((bf16[768,128]{1,0:T(8,128)(2,1)S(1)}, bf16[768,128]{1,0:T(8,128)(2,1)S(1)}, u32[]{:S(2)}, u32[]{:S(2)}) %collective-permute-start.13) | collective-permute-done | bytes 196640 | tf_op jit(solution)/shard_map/ppermute | solution.py:537
  117.1 1.9 %shard_map.88 = (bf16[512,512]{1,0:T(8,128)(2,1)}, bf16[512,512]{1,0:T(8,128)(2,1)}, bf16[512,512]{1,0:T(8,128)(2,1)}, bf16[512,512]{1,0:T(8,128)(2,1)}) custom-call(s32[1]{0:T(128)} %bitcast.refs_0_, bf16[8,256,128]{2,1,0:T(8,128)(2,1)S(1)} %all-to-all-done.refs_1_, bf16[768,128]{1,0:T(8,128)(2,1)S(1)} %get-tuple-element.50.refs_2_, ...), custom_call_target="tpu_custom_call" | custom-call | tf_op jit(solution)/shard_map/pallas_call | solution.py:523
Async XLA Ops:
  0.6 45.4 %copy-start.2 = (s32[8,16]{1,0:T(8,128)S(1)}, s32[8,16]{1,0:T(8,128)}, u32[]{:S(2)}) copy-start(s32[8,16]{1,0:T(8,128)} %refs_1_.7) | copy-start | bytes 1540
  2.6 7.3 %collective-permute-start = (bf16[768,128]{1,0:T(8,128)(2,1)S(1)}, bf16[768,128]{1,0:T(8,128)(2,1)S(1)}, u32[]{:S(2)}, u32[]{:S(2)}) collective-permute-start(bf16[768,128]{1,0:T(8,128)(2,1)S(1)} %get-tuple-element.32), channel_id=1, source_target_pairs={{0,4},{4,8},{8,12},{12,16},{16,20},{20,24},{24,28},{28,0},{1,5},{5... | collective-permute-start | bytes 589832 | tf_op jit(solution)/shard_map/ppermute | solution.py:537
  4.1 26.4 %collective-permute-start.1 = (bf16[768,128]{1,0:T(8,128)(2,1)S(1)}, bf16[768,128]{1,0:T(8,128)(2,1)S(1)}, u32[]{:S(2)}, u32[]{:S(2)}) collective-permute-start(bf16[768,128]{1,0:T(8,128)(2,1)S(1)} %get-tuple-element.33), channel_id=1, source_target_pairs={{0,8},{4,12},{8,16},{12,20},{16,24},{20,28},{24,0},{28,4},{1,9},{5... | collective-permute-start | bytes 589832 | tf_op jit(solution)/shard_map/ppermute | solution.py:537
  5.7 29.0 %collective-permute-start.2 = (bf16[768,128]{1,0:T(8,128)(2,1)S(1)}, bf16[768,128]{1,0:T(8,128)(2,1)S(1)}, u32[]{:S(2)}, u32[]{:S(2)}) collective-permute-start(bf16[768,128]{1,0:T(8,128)(2,1)S(1)} %get-tuple-element.34), channel_id=1, source_target_pairs={{0,12},{4,16},{8,20},{12,24},{16,28},{20,0},{24,4},{28,8},{1,13},{... | collective-permute-start | bytes 589832 | tf_op jit(solution)/shard_map/ppermute | solution.py:537
  6.9 30.9 %collective-permute-start.3 = (bf16[768,128]{1,0:T(8,128)(2,1)S(1)}, bf16[768,128]{1,0:T(8,128)(2,1)S(1)}, u32[]{:S(2)}, u32[]{:S(2)}) collective-permute-start(bf16[768,128]{1,0:T(8,128)(2,1)S(1)} %get-tuple-element.35), channel_id=1, source_target_pairs={{0,16},{4,20},{8,24},{12,28},{16,0},{20,4},{24,8},{28,12},{1,17},{... | collective-permute-start | bytes 589832 | tf_op jit(solution)/shard_map/ppermute | solution.py:537
  8.6 29.2 %collective-permute-start.4 = (bf16[768,128]{1,0:T(8,128)(2,1)S(1)}, bf16[768,128]{1,0:T(8,128)(2,1)S(1)}, u32[]{:S(2)}, u32[]{:S(2)}) collective-permute-start(bf16[768,128]{1,0:T(8,128)(2,1)S(1)} %get-tuple-element.36), channel_id=1, source_target_pairs={{0,20},{4,24},{8,28},{12,0},{16,4},{20,8},{24,12},{28,16},{1,21},{... | collective-permute-start | bytes 589832 | tf_op jit(solution)/shard_map/ppermute | solution.py:537
  9.9 29.8 %collective-permute-start.5 = (bf16[768,128]{1,0:T(8,128)(2,1)S(1)}, bf16[768,128]{1,0:T(8,128)(2,1)S(1)}, u32[]{:S(2)}, u32[]{:S(2)}) collective-permute-start(bf16[768,128]{1,0:T(8,128)(2,1)S(1)} %get-tuple-element.37), channel_id=1, source_target_pairs={{0,24},{4,28},{8,0},{12,4},{16,8},{20,12},{24,16},{28,20},{1,25},{... | collective-permute-start | bytes 589832 | tf_op jit(solution)/shard_map/ppermute | solution.py:537
  30.5 10.3 %collective-permute-start.6 = (bf16[768,128]{1,0:T(8,128)(2,1)S(1)}, bf16[768,128]{1,0:T(8,128)(2,1)S(1)}, u32[]{:S(2)}, u32[]{:S(2)}) collective-permute-start(bf16[768,128]{1,0:T(8,128)(2,1)S(1)} %get-tuple-element.38), channel_id=1, source_target_pairs={{0,28},{4,0},{8,4},{12,8},{16,12},{20,16},{24,20},{28,24},{1,29},{... | collective-permute-start | bytes 589832 | tf_op jit(solution)/shard_map/ppermute | solution.py:537
  40.8 18.6 %copy-start = (bf16[768,128]{1,0:T(8,128)(2,1)}, bf16[768,128]{1,0:T(8,128)(2,1)S(1)}, u32[]{:S(2)}) copy-start(bf16[768,128]{1,0:T(8,128)(2,1)S(1)} %collective-permute-done.6.refs_9_) | copy-start | bytes 589828
  40.8 18.6 %all-to-all-start.1 = ((bf16[8,256,128]{2,1,0:T(8,128)(2,1)}), bf16[8,256,128]{2,1,0:T(8,128)(2,1)S(1)}, u32[]{:S(2)}, u32[]{:S(2)}) async-start(bf16[8,256,128]{2,1,0:T(8,128)(2,1)} %shard_map.85), calls=%async_computation.1 | async-start | bytes 1048576 | tf_op jit(solution)/shard_map/all_to_all | solution.py:542
  59.4 49.1 %all-to-all-start = ((bf16[8,256,128]{2,1,0:T(8,128)(2,1)}), bf16[8,256,128]{2,1,0:T(8,128)(2,1)S(1)}, u32[]{:S(2)}, u32[]{:S(2)}) async-start(bf16[8,256,128]{2,1,0:T(8,128)(2,1)} %get-tuple-element.47), calls=%async_computation | async-start | bytes 1048576 | tf_op jit(solution)/shard_map/all_to_all | solution.py:542
  65.4 0.9 copy-start.1
  80.6 8.6 %collective-permute-start.7 = (bf16[768,128]{1,0:T(8,128)(2,1)S(1)}, bf16[768,128]{1,0:T(8,128)(2,1)S(1)}, u32[]{:S(2)}, u32[]{:S(2)}) collective-permute-start(bf16[768,128]{1,0:T(8,128)(2,1)S(1)} %get-tuple-element.51), channel_id=1, source_target_pairs={{0,4},{4,8},{8,12},{12,16},{16,20},{20,24},{24,28},{28,0},{1,5},{5... | collective-permute-start | bytes 589832 | tf_op jit(solution)/shard_map/ppermute | solution.py:537
  82.1 26.4 %collective-permute-start.8 = (bf16[768,128]{1,0:T(8,128)(2,1)S(1)}, bf16[768,128]{1,0:T(8,128)(2,1)S(1)}, u32[]{:S(2)}, u32[]{:S(2)}) collective-permute-start(bf16[768,128]{1,0:T(8,128)(2,1)S(1)} %get-tuple-element.52), channel_id=1, source_target_pairs={{0,8},{4,12},{8,16},{12,20},{16,24},{20,28},{24,0},{28,4},{1,9},{5... | collective-permute-start | bytes 589832 | tf_op jit(solution)/shard_map/ppermute | solution.py:537
  83.6 28.2 %collective-permute-start.9 = (bf16[768,128]{1,0:T(8,128)(2,1)}, bf16[768,128]{1,0:T(8,128)(2,1)S(1)}, u32[]{:S(2)}, u32[]{:S(2)}) collective-permute-start(bf16[768,128]{1,0:T(8,128)(2,1)} %get-tuple-element.53), channel_id=1, source_target_pairs={{0,12},{4,16},{8,20},{12,24},{16,28},{20,0},{24,4},{28,8},{1,13},{... | collective-permute-start | bytes 589832 | tf_op jit(solution)/shard_map/ppermute | solution.py:537
  85.1 28.7 %collective-permute-start.10 = (bf16[768,128]{1,0:T(8,128)(2,1)S(1)}, bf16[768,128]{1,0:T(8,128)(2,1)S(1)}, u32[]{:S(2)}, u32[]{:S(2)}) collective-permute-start(bf16[768,128]{1,0:T(8,128)(2,1)S(1)} %get-tuple-element.54), channel_id=1, source_target_pairs={{0,16},{4,20},{8,24},{12,28},{16,0},{20,4},{24,8},{28,12},{1,17},{... | collective-permute-start | bytes 589832 | tf_op jit(solution)/shard_map/ppermute | solution.py:537
  86.5 27.2 %collective-permute-start.11 = (bf16[768,128]{1,0:T(8,128)(2,1)S(1)}, bf16[768,128]{1,0:T(8,128)(2,1)S(1)}, u32[]{:S(2)}, u32[]{:S(2)}) collective-permute-start(bf16[768,128]{1,0:T(8,128)(2,1)S(1)} %get-tuple-element.55), channel_id=1, source_target_pairs={{0,20},{4,24},{8,28},{12,0},{16,4},{20,8},{24,12},{28,16},{1,21},{... | collective-permute-start | bytes 589832 | tf_op jit(solution)/shard_map/ppermute | solution.py:537
  89.2 26.2 %collective-permute-start.12 = (bf16[768,128]{1,0:T(8,128)(2,1)S(1)}, bf16[768,128]{1,0:T(8,128)(2,1)S(1)}, u32[]{:S(2)}, u32[]{:S(2)}) collective-permute-start(bf16[768,128]{1,0:T(8,128)(2,1)S(1)} %get-tuple-element.56), channel_id=1, source_target_pairs={{0,24},{4,28},{8,0},{12,4},{16,8},{20,12},{24,16},{28,20},{1,25},{... | collective-permute-start | bytes 589832 | tf_op jit(solution)/shard_map/ppermute | solution.py:537
  108.6 8.5 %collective-permute-start.13 = (bf16[768,128]{1,0:T(8,128)(2,1)S(1)}, bf16[768,128]{1,0:T(8,128)(2,1)S(1)}, u32[]{:S(2)}, u32[]{:S(2)}) collective-permute-start(bf16[768,128]{1,0:T(8,128)(2,1)S(1)} %get-tuple-element.57), channel_id=1, source_target_pairs={{0,28},{4,0},{8,4},{12,8},{16,12},{20,16},{24,20},{28,24},{1,29},{... | collective-permute-start | bytes 589832 | tf_op jit(solution)/shard_map/ppermute | solution.py:537

commit v5 on v4

--- a/solution.py
+++ b/solution.py
@@ -550,7 +550,7 @@
         pack(me, (key_rows, value_rows, queries, grad_output), ((0, 1, 0, rows), (2, 3, 0, half)), True)
     )
     late_packed = pack(me, (queries, grad_output), ((0, 1, half, half),), False)
-    *early, late_packed = lax.optimization_barrier((*early, late_packed))
+    *early[:4], late_packed = lax.optimization_barrier((*early[:4], late_packed))
     late = all_heads(late_packed)
     early_rows, sums = attention(me, extra_blocks, early, None, None, rows, 0, half)
     early_back = all_heads(early_rows)

time: 119 us -> 114 us (0.958)
  waiting for transfers between devices: 56.4 us -> 49.3 us
  starting transfers between devices: 27.2 us -> 28.9 us
    ppermute x14, waiting for transfers between devices: 56.4 us -> 49.3 us  [shifted_all(): lax.ppermute(pieces[k], 'tm', [(i, (i + k) % count) for i in range(count)])]
    all_to_all x2, starting transfers between devices: 11.3 us -> 13 us  [all_heads(): return lax.all_to_all(packed, 'tm', split_axis=0, concat_axis=0, tiled=True)]
  transfers between devices with their start and end apart: 16 -> 16, of which waited for: 11 -> 8; matrix products, arithmetic and copies ran while one was open for 0% -> 0% of each run, Pallas kernels for 25% -> 26%
where the time goes in v5:
time: 114 us
  waiting for transfers between devices  49.3 us (43%)
  Pallas kernels  33.7 us (30%)
  starting transfers between devices  28.9 us (25%)
    ppermute x14, waiting for transfers between devices, shifted_all(): lax.ppermute(pieces[k], 'tm', [(i, (i + k) % count) for i in range(count)])  49.3 us
    pallas_call x2, Pallas kernels, attention(): pl.pallas_call(functools.partial(attention_kernel, blocks, rows, first_qu...  27.6 us
    ppermute x14, starting transfers between devices, shifted_all(): lax.ppermute(pieces[k], 'tm', [(i, (i + k) % count) for i in range(count)])  15.9 us
    all_to_all x2, starting transfers between devices, all_heads(): return lax.all_to_all(packed, 'tm', split_axis=0, concat_axis=0, tiled=True)  13 us
    pallas_call x2, Pallas kernels, pack(): pl.pallas_call(functools.partial(pack_kernel, heads, pieces, apart, len(a...  4.2 us
  transfers between devices with their start and end apart: 16, of which 8 were waited for; matrix products, arithmetic and copies ran while one was open for 0% of the time, Pallas kernels for 26%

profile of v5, /device:TPU:12, one launch (start us, length us, event | category | flops | bytes accessed | tf_op | source)
XLA Modules:
  0.0 113.6 jit_solution(11561486995350701967)
XLA Ops:
  0.6 0.0 copy-start.2
  0.6 1.9 %shard_map.84 = (bf16[768,128]{1,0:T(8,128)(2,1)S(1)}, bf16[768,128]{1,0:T(8,128)(2,1)S(1)}, bf16[768,128]{1,0:T(8,128)(2,1)S(1)}, bf16[768,128]{1,0:T(8,128)(2,...) custom-call(s32[1]{0:T(128)} %bitcast.refs_0_, ...), custom_call_target="tpu_custom_call" | custom-call | bytes 3145728 | tf_op jit(solution)/shard_map/pallas_call | solution.py:490
  2.6 1.6 %collective-permute-start = (bf16[768,128]{1,0:T(8,128)(2,1)S(1)}, bf16[768,128]{1,0:T(8,128)(2,1)S(1)}, u32[]{:S(2)}, u32[]{:S(2)}) collective-permute-start(bf16[768,128]{1,0:T(8,128)(2,1)S(1)} %get-tuple-element.28), channel_id=1, source_target_pairs={{0,4},{4,8},{8,12},{12,16},{16,20},{20,24},{24,28},{28,0},{1,5},{5... | collective-permute-start | bytes 589832 | tf_op jit(solution)/shard_map/ppermute | solution.py:537
  4.1 1.6 %collective-permute-start.1 = (bf16[768,128]{1,0:T(8,128)(2,1)S(1)}, bf16[768,128]{1,0:T(8,128)(2,1)S(1)}, u32[]{:S(2)}, u32[]{:S(2)}) collective-permute-start(bf16[768,128]{1,0:T(8,128)(2,1)S(1)} %get-tuple-element.29), channel_id=1, source_target_pairs={{0,8},{4,12},{8,16},{12,20},{16,24},{20,28},{24,0},{28,4},{1,9},{5... | collective-permute-start | bytes 589832 | tf_op jit(solution)/shard_map/ppermute | solution.py:537
  5.7 1.2 %collective-permute-start.2 = (bf16[768,128]{1,0:T(8,128)(2,1)S(1)}, bf16[768,128]{1,0:T(8,128)(2,1)S(1)}, u32[]{:S(2)}, u32[]{:S(2)}) collective-permute-start(bf16[768,128]{1,0:T(8,128)(2,1)S(1)} %get-tuple-element.30), channel_id=1, source_target_pairs={{0,12},{4,16},{8,20},{12,24},{16,28},{20,0},{24,4},{28,8},{1,13},{... | collective-permute-start | bytes 589832 | tf_op jit(solution)/shard_map/ppermute | solution.py:537
  6.9 1.7 %collective-permute-start.3 = (bf16[768,128]{1,0:T(8,128)(2,1)S(1)}, bf16[768,128]{1,0:T(8,128)(2,1)S(1)}, u32[]{:S(2)}, u32[]{:S(2)}) collective-permute-start(bf16[768,128]{1,0:T(8,128)(2,1)S(1)} %get-tuple-element.35), channel_id=1, source_target_pairs={{0,16},{4,20},{8,24},{12,28},{16,0},{20,4},{24,8},{28,12},{1,17},{... | collective-permute-start | bytes 589832 | tf_op jit(solution)/shard_map/ppermute | solution.py:537
  8.6 1.3 %collective-permute-start.4 = (bf16[768,128]{1,0:T(8,128)(2,1)S(1)}, bf16[768,128]{1,0:T(8,128)(2,1)S(1)}, u32[]{:S(2)}, u32[]{:S(2)}) collective-permute-start(bf16[768,128]{1,0:T(8,128)(2,1)S(1)} %get-tuple-element.36), channel_id=1, source_target_pairs={{0,20},{4,24},{8,28},{12,0},{16,4},{20,8},{24,12},{28,16},{1,21},{... | collective-permute-start | bytes 589832 | tf_op jit(solution)/shard_map/ppermute | solution.py:537
  9.9 0.0 collective-permute-done.refs_3_
  9.9 1.2 %collective-permute-start.5 = (bf16[768,128]{1,0:T(8,128)(2,1)S(1)}, bf16[768,128]{1,0:T(8,128)(2,1)S(1)}, u32[]{:S(2)}, u32[]{:S(2)}) collective-permute-start(bf16[768,128]{1,0:T(8,128)(2,1)S(1)} %get-tuple-element.37), channel_id=1, source_target_pairs={{0,24},{4,28},{8,0},{12,4},{16,8},{20,12},{24,16},{28,20},{1,25},{... | collective-permute-start | bytes 589832 | tf_op jit(solution)/shard_map/ppermute | solution.py:537
  11.1 19.4 %collective-permute-done.1.refs_4_ = bf16[768,128]{1,0:T(8,128)(2,1)S(1)} collective-permute-done((bf16[768,128]{1,0:T(8,128)(2,1)S(1)}, bf16[768,128]{1,0:T(8,128)(2,1)S(1)}, u32[]{:S(2)}, u32[]{:S(2)}) %collective-permute-start.1) | collective-permute-done | bytes 196640 | tf_op jit(solution)/shard_map/ppermute | solution.py:537
  30.5 0.0 collective-permute-start.6
  30.5 2.3 %shard_map.85 = bf16[8,256,128]{2,1,0:T(8,128)(2,1)} custom-call(s32[1]{0:T(128)} %bitcast.refs_0_, bf16[512,512]{1,0:T(8,128)(2,1)} %refs_1_.5, bf16[512,512]{1,0:T(8,128)(2,1)} %refs_2_.3), custom_call_target="tpu_custom_call" | custom-call | bytes 1048576 | tf_op jit(solution)/shard_map/pallas_call | solution.py:490
  32.8 1.9 %collective-permute-done.2.refs_5_ = bf16[768,128]{1,0:T(8,128)(2,1)S(1)} collective-permute-done((bf16[768,128]{1,0:T(8,128)(2,1)S(1)}, bf16[768,128]{1,0:T(8,128)(2,1)S(1)}, u32[]{:S(2)}, u32[]{:S(2)}) %collective-permute-start.2) | collective-permute-done | bytes 196640 | tf_op jit(solution)/shard_map/ppermute | solution.py:537
  34.7 7.0 %all-to-all-start.1 = ((bf16[8,256,128]{2,1,0:T(8,128)(2,1)}), bf16[8,256,128]{2,1,0:T(8,128)(2,1)S(1)}, u32[]{:S(2)}, u32[]{:S(2)}) async-start(bf16[8,256,128]{2,1,0:T(8,128)(2,1)} %shard_map.85), calls=%async_computation.1 | async-start | bytes 1048576 | tf_op jit(solution)/shard_map/all_to_all | solution.py:542
  41.7 0.0 collective-permute-done.3.refs_6_
  41.7 0.0 collective-permute-done.4.refs_7_
  41.7 0.0 collective-permute-done.5.refs_8_
  41.8 0.0 collective-permute-done.6.refs_9_
  41.8 0.0 copy-done.2
  41.8 0.0 copy-start
  41.8 13.3 %shard_map.86 = (bf16[8,256,128]{2,1,0:T(8,128)(2,1)}, f32[8,512,128]{2,1,0:T(8,128)}) custom-call(s32[1]{0:T(128)} %bitcast.refs_0_, s32[8,16]{1,0:T(8,128)S(1)} %copy-done.2, bf16[768,128]{1,0:T(8,128)(2,1)S(1)} %get-tuple-element.31.refs_2_, bf16[768,128]{1,0:T(8,128)(2,1)S(1)} %collective-permute-done.refs_3_, ...), custom_call_target="tpu_custom_call" | custom-call | flops 12884901888 | bytes 8388608 | tf_op jit(solution)/shard_map/pallas_call | solution.py:424
  55.1 0.0 copy-done
  55.1 0.0 all-to-all-done.1.refs_10_
  55.1 6.0 %all-to-all-start = ((bf16[8,256,128]{2,1,0:T(8,128)(2,1)}), bf16[8,256,128]{2,1,0:T(8,128)(2,1)S(1)}, u32[]{:S(2)}, u32[]{:S(2)}) async-start(bf16[8,256,128]{2,1,0:T(8,128)(2,1)} %get-tuple-element.39), calls=%async_computation | async-start | bytes 1048576 | tf_op jit(solution)/shard_map/all_to_all | solution.py:542
  61.2 0.0 copy-start.1
  61.2 0.9 copy-done.1
  62.1 14.3 %shard_map.87 = (bf16[768,128]{1,0:T(8,128)(2,1)S(1)}, bf16[768,128]{1,0:T(8,128)(2,1)S(1)}, bf16[768,128]{1,0:T(8,128)(2,1)S(1)}, bf16[768,128]{1,0:T(8,128)(2,...) custom-call(s32[1]{0:T(128)} %bitcast.refs_0_, ...), custom_call_target="tpu_custom_call" | custom-call | flops 12884901888 | bytes 8388608 | tf_op jit(solution)/shard_map/pallas_call | solution.py:424
  76.3 1.5 %collective-permute-start.7 = (bf16[768,128]{1,0:T(8,128)(2,1)S(1)}, bf16[768,128]{1,0:T(8,128)(2,1)S(1)}, u32[]{:S(2)}, u32[]{:S(2)}) collective-permute-start(bf16[768,128]{1,0:T(8,128)(2,1)S(1)} %get-tuple-element.43), channel_id=1, source_target_pairs={{0,4},{4,8},{8,12},{12,16},{16,20},{20,24},{24,28},{28,0},{1,5},{5... | collective-permute-start | bytes 589832 | tf_op jit(solution)/shard_map/ppermute | solution.py:537
  77.9 1.5 %collective-permute-start.8 = (bf16[768,128]{1,0:T(8,128)(2,1)S(1)}, bf16[768,128]{1,0:T(8,128)(2,1)S(1)}, u32[]{:S(2)}, u32[]{:S(2)}) collective-permute-start(bf16[768,128]{1,0:T(8,128)(2,1)S(1)} %get-tuple-element.44), channel_id=1, source_target_pairs={{0,8},{4,12},{8,16},{12,20},{16,24},{20,28},{24,0},{28,4},{1,9},{5... | collective-permute-start | bytes 589832 | tf_op jit(solution)/shard_map/ppermute | solution.py:537
  79.3 1.5 %collective-permute-start.9 = (bf16[768,128]{1,0:T(8,128)(2,1)}, bf16[768,128]{1,0:T(8,128)(2,1)S(1)}, u32[]{:S(2)}, u32[]{:S(2)}) collective-permute-start(bf16[768,128]{1,0:T(8,128)(2,1)} %get-tuple-element.45), channel_id=1, source_target_pairs={{0,12},{4,16},{8,20},{12,24},{16,28},{20,0},{24,4},{28,8},{1,13},{... | collective-permute-start | bytes 589832 | tf_op jit(solution)/shard_map/ppermute | solution.py:537
  80.8 1.5 %collective-permute-start.10 = (bf16[768,128]{1,0:T(8,128)(2,1)S(1)}, bf16[768,128]{1,0:T(8,128)(2,1)S(1)}, u32[]{:S(2)}, u32[]{:S(2)}) collective-permute-start(bf16[768,128]{1,0:T(8,128)(2,1)S(1)} %get-tuple-element.46), channel_id=1, source_target_pairs={{0,16},{4,20},{8,24},{12,28},{16,0},{20,4},{24,8},{28,12},{1,17},{... | collective-permute-start | bytes 589832 | tf_op jit(solution)/shard_map/ppermute | solution.py:537
  82.2 1.5 %collective-permute-start.11 = (bf16[768,128]{1,0:T(8,128)(2,1)S(1)}, bf16[768,128]{1,0:T(8,128)(2,1)S(1)}, u32[]{:S(2)}, u32[]{:S(2)}) collective-permute-start(bf16[768,128]{1,0:T(8,128)(2,1)S(1)} %get-tuple-element.47), channel_id=1, source_target_pairs={{0,20},{4,24},{8,28},{12,0},{16,4},{20,8},{24,12},{28,16},{1,21},{... | collective-permute-start | bytes 589832 | tf_op jit(solution)/shard_map/ppermute | solution.py:537
  83.7 3.6 %collective-permute-done.7.refs_3_ = bf16[768,128]{1,0:T(8,128)(2,1)S(1)} collective-permute-done((bf16[768,128]{1,0:T(8,128)(2,1)S(1)}, bf16[768,128]{1,0:T(8,128)(2,1)S(1)}, u32[]{:S(2)}, u32[]{:S(2)}) %collective-permute-start.7) | collective-permute-done | bytes 196640 | tf_op jit(solution)/shard_map/ppermute | solution.py:537
  87.3 0.0 collective-permute-start.12
  87.3 16.9 %collective-permute-done.8.refs_4_ = bf16[768,128]{1,0:T(8,128)(2,1)S(1)} collective-permute-done((bf16[768,128]{1,0:T(8,128)(2,1)S(1)}, bf16[768,128]{1,0:T(8,128)(2,1)S(1)}, u32[]{:S(2)}, u32[]{:S(2)}) %collective-permute-start.8) | collective-permute-done | bytes 196640 | tf_op jit(solution)/shard_map/ppermute | solution.py:537
  104.2 0.0 collective-permute-start.13
  104.2 0.0 all-to-all-done.refs_1_
  104.2 2.2 %collective-permute-done.9.refs_5_ = bf16[768,128]{1,0:T(8,128)(2,1)S(1)} collective-permute-done((bf16[768,128]{1,0:T(8,128)(2,1)}, bf16[768,128]{1,0:T(8,128)(2,1)S(1)}, u32[]{:S(2)}, u32[]{:S(2)}) %collective-permute-start.9) | collective-permute-done | bytes 196640 | tf_op jit(solution)/shard_map/ppermute | solution.py:537
  106.4 2.0 %collective-permute-done.10.refs_6_ = bf16[768,128]{1,0:T(8,128)(2,1)S(1)} collective-permute-done((bf16[768,128]{1,0:T(8,128)(2,1)S(1)}, bf16[768,128]{1,0:T(8,128)(2,1)S(1)}, u32[]{:S(2)}, u32[]{:S(2)}) %collective-permute-start.10) | collective-permute-done | bytes 196640 | tf_op jit(solution)/shard_map/ppermute | solution.py:537
  108.4 0.0 collective-permute-done.11.refs_7_
  108.4 1.6 %collective-permute-done.12.refs_8_ = bf16[768,128]{1,0:T(8,128)(2,1)S(1)} collective-permute-done((bf16[768,128]{1,0:T(8,128)(2,1)S(1)}, bf16[768,128]{1,0:T(8,128)(2,1)S(1)}, u32[]{:S(2)}, u32[]{:S(2)}) %collective-permute-start.12) | collective-permute-done | bytes 196640 | tf_op jit(solution)/shard_map/ppermute | solution.py:537
  110.0 1.6 %collective-permute-done.13.refs_9_ = bf16[768,128]{1,0:T(8,128)(2,1)S(1)} collective-permute-done((bf16[768,128]{1,0:T(8,128)(2,1)S(1)}, bf16[768,128]{1,0:T(8,128)(2,1)S(1)}, u32[]{:S(2)}, u32[]{:S(2)}) %collective-permute-start.13) | collective-permute-done | bytes 196640 | tf_op jit(solution)/shard_map/ppermute | solution.py:537
  111.7 1.9 %shard_map.88 = (bf16[512,512]{1,0:T(8,128)(2,1)}, bf16[512,512]{1,0:T(8,128)(2,1)}, bf16[512,512]{1,0:T(8,128)(2,1)}, bf16[512,512]{1,0:T(8,128)(2,1)}) custom-call(s32[1]{0:T(128)} %bitcast.refs_0_, bf16[8,256,128]{2,1,0:T(8,128)(2,1)S(1)} %all-to-all-done.refs_1_, bf16[768,128]{1,0:T(8,128)(2,1)S(1)} %get-tuple-element.42.refs_2_, ...), custom_call_target="tpu_custom_call" | custom-call | tf_op jit(solution)/shard_map/pallas_call | solution.py:523
Async XLA Ops:
  0.6 41.1 %copy-start.2 = (s32[8,16]{1,0:T(8,128)S(1)}, s32[8,16]{1,0:T(8,128)}, u32[]{:S(2)}) copy-start(s32[8,16]{1,0:T(8,128)} %refs_1_.7) | copy-start | bytes 1540
  2.6 7.3 %collective-permute-start = (bf16[768,128]{1,0:T(8,128)(2,1)S(1)}, bf16[768,128]{1,0:T(8,128)(2,1)S(1)}, u32[]{:S(2)}, u32[]{:S(2)}) collective-permute-start(bf16[768,128]{1,0:T(8,128)(2,1)S(1)} %get-tuple-element.28), channel_id=1, source_target_pairs={{0,4},{4,8},{8,12},{12,16},{16,20},{20,24},{24,28},{28,0},{1,5},{5... | collective-permute-start | bytes 589832 | tf_op jit(solution)/shard_map/ppermute | solution.py:537
  4.1 26.4 %collective-permute-start.1 = (bf16[768,128]{1,0:T(8,128)(2,1)S(1)}, bf16[768,128]{1,0:T(8,128)(2,1)S(1)}, u32[]{:S(2)}, u32[]{:S(2)}) collective-permute-start(bf16[768,128]{1,0:T(8,128)(2,1)S(1)} %get-tuple-element.29), channel_id=1, source_target_pairs={{0,8},{4,12},{8,16},{12,20},{16,24},{20,28},{24,0},{28,4},{1,9},{5... | collective-permute-start | bytes 589832 | tf_op jit(solution)/shard_map/ppermute | solution.py:537
  5.7 29.0 %collective-permute-start.2 = (bf16[768,128]{1,0:T(8,128)(2,1)S(1)}, bf16[768,128]{1,0:T(8,128)(2,1)S(1)}, u32[]{:S(2)}, u32[]{:S(2)}) collective-permute-start(bf16[768,128]{1,0:T(8,128)(2,1)S(1)} %get-tuple-element.30), channel_id=1, source_target_pairs={{0,12},{4,16},{8,20},{12,24},{16,28},{20,0},{24,4},{28,8},{1,13},{... | collective-permute-start | bytes 589832 | tf_op jit(solution)/shard_map/ppermute | solution.py:537
  6.9 34.8 %collective-permute-start.3 = (bf16[768,128]{1,0:T(8,128)(2,1)S(1)}, bf16[768,128]{1,0:T(8,128)(2,1)S(1)}, u32[]{:S(2)}, u32[]{:S(2)}) collective-permute-start(bf16[768,128]{1,0:T(8,128)(2,1)S(1)} %get-tuple-element.35), channel_id=1, source_target_pairs={{0,16},{4,20},{8,24},{12,28},{16,0},{20,4},{24,8},{28,12},{1,17},{... | collective-permute-start | bytes 589832 | tf_op jit(solution)/shard_map/ppermute | solution.py:537
  8.6 33.2 %collective-permute-start.4 = (bf16[768,128]{1,0:T(8,128)(2,1)S(1)}, bf16[768,128]{1,0:T(8,128)(2,1)S(1)}, u32[]{:S(2)}, u32[]{:S(2)}) collective-permute-start(bf16[768,128]{1,0:T(8,128)(2,1)S(1)} %get-tuple-element.36), channel_id=1, source_target_pairs={{0,20},{4,24},{8,28},{12,0},{16,4},{20,8},{24,12},{28,16},{1,21},{... | collective-permute-start | bytes 589832 | tf_op jit(solution)/shard_map/ppermute | solution.py:537
  9.9 31.9 %collective-permute-start.5 = (bf16[768,128]{1,0:T(8,128)(2,1)S(1)}, bf16[768,128]{1,0:T(8,128)(2,1)S(1)}, u32[]{:S(2)}, u32[]{:S(2)}) collective-permute-start(bf16[768,128]{1,0:T(8,128)(2,1)S(1)} %get-tuple-element.37), channel_id=1, source_target_pairs={{0,24},{4,28},{8,0},{12,4},{16,8},{20,12},{24,16},{28,20},{1,25},{... | collective-permute-start | bytes 589832 | tf_op jit(solution)/shard_map/ppermute | solution.py:537
  30.5 11.2 %collective-permute-start.6 = (bf16[768,128]{1,0:T(8,128)(2,1)S(1)}, bf16[768,128]{1,0:T(8,128)(2,1)S(1)}, u32[]{:S(2)}, u32[]{:S(2)}) collective-permute-start(bf16[768,128]{1,0:T(8,128)(2,1)S(1)} %get-tuple-element.38), channel_id=1, source_target_pairs={{0,28},{4,0},{8,4},{12,8},{16,12},{20,16},{24,20},{28,24},{1,29},{... | collective-permute-start | bytes 589832 | tf_op jit(solution)/shard_map/ppermute | solution.py:537
  34.7 20.4 %all-to-all-start.1 = ((bf16[8,256,128]{2,1,0:T(8,128)(2,1)}), bf16[8,256,128]{2,1,0:T(8,128)(2,1)S(1)}, u32[]{:S(2)}, u32[]{:S(2)}) async-start(bf16[8,256,128]{2,1,0:T(8,128)(2,1)} %shard_map.85), calls=%async_computation.1 | async-start | bytes 1048576 | tf_op jit(solution)/shard_map/all_to_all | solution.py:542
  41.8 13.3 %copy-start = (bf16[768,128]{1,0:T(8,128)(2,1)}, bf16[768,128]{1,0:T(8,128)(2,1)S(1)}, u32[]{:S(2)}) copy-start(bf16[768,128]{1,0:T(8,128)(2,1)S(1)} %collective-permute-done.6.refs_9_) | copy-start | bytes 589828
  55.1 49.0 %all-to-all-start = ((bf16[8,256,128]{2,1,0:T(8,128)(2,1)}), bf16[8,256,128]{2,1,0:T(8,128)(2,1)S(1)}, u32[]{:S(2)}, u32[]{:S(2)}) async-start(bf16[8,256,128]{2,1,0:T(8,128)(2,1)} %get-tuple-element.39), calls=%async_computation | async-start | bytes 1048576 | tf_op jit(solution)/shard_map/all_to_all | solution.py:542
  61.2 0.9 copy-start.1
  76.3 10.9 %collective-permute-start.7 = (bf16[768,128]{1,0:T(8,128)(2,1)S(1)}, bf16[768,128]{1,0:T(8,128)(2,1)S(1)}, u32[]{:S(2)}, u32[]{:S(2)}) collective-permute-start(bf16[768,128]{1,0:T(8,128)(2,1)S(1)} %get-tuple-element.43), channel_id=1, source_target_pairs={{0,4},{4,8},{8,12},{12,16},{16,20},{20,24},{24,28},{28,0},{1,5},{5... | collective-permute-start | bytes 589832 | tf_op jit(solution)/shard_map/ppermute | solution.py:537
  77.9 26.3 %collective-permute-start.8 = (bf16[768,128]{1,0:T(8,128)(2,1)S(1)}, bf16[768,128]{1,0:T(8,128)(2,1)S(1)}, u32[]{:S(2)}, u32[]{:S(2)}) collective-permute-start(bf16[768,128]{1,0:T(8,128)(2,1)S(1)} %get-tuple-element.44), channel_id=1, source_target_pairs={{0,8},{4,12},{8,16},{12,20},{16,24},{20,28},{24,0},{28,4},{1,9},{5... | collective-permute-start | bytes 589832 | tf_op jit(solution)/shard_map/ppermute | solution.py:537
  79.3 27.1 %collective-permute-start.9 = (bf16[768,128]{1,0:T(8,128)(2,1)}, bf16[768,128]{1,0:T(8,128)(2,1)S(1)}, u32[]{:S(2)}, u32[]{:S(2)}) collective-permute-start(bf16[768,128]{1,0:T(8,128)(2,1)} %get-tuple-element.45), channel_id=1, source_target_pairs={{0,12},{4,16},{8,20},{12,24},{16,28},{20,0},{24,4},{28,8},{1,13},{... | collective-permute-start | bytes 589832 | tf_op jit(solution)/shard_map/ppermute | solution.py:537
  80.8 27.6 %collective-permute-start.10 = (bf16[768,128]{1,0:T(8,128)(2,1)S(1)}, bf16[768,128]{1,0:T(8,128)(2,1)S(1)}, u32[]{:S(2)}, u32[]{:S(2)}) collective-permute-start(bf16[768,128]{1,0:T(8,128)(2,1)S(1)} %get-tuple-element.46), channel_id=1, source_target_pairs={{0,16},{4,20},{8,24},{12,28},{16,0},{20,4},{24,8},{28,12},{1,17},{... | collective-permute-start | bytes 589832 | tf_op jit(solution)/shard_map/ppermute | solution.py:537
  82.2 26.1 %collective-permute-start.11 = (bf16[768,128]{1,0:T(8,128)(2,1)S(1)}, bf16[768,128]{1,0:T(8,128)(2,1)S(1)}, u32[]{:S(2)}, u32[]{:S(2)}) collective-permute-start(bf16[768,128]{1,0:T(8,128)(2,1)S(1)} %get-tuple-element.47), channel_id=1, source_target_pairs={{0,20},{4,24},{8,28},{12,0},{16,4},{20,8},{24,12},{28,16},{1,21},{... | collective-permute-start | bytes 589832 | tf_op jit(solution)/shard_map/ppermute | solution.py:537
  87.3 22.7 %collective-permute-start.12 = (bf16[768,128]{1,0:T(8,128)(2,1)S(1)}, bf16[768,128]{1,0:T(8,128)(2,1)S(1)}, u32[]{:S(2)}, u32[]{:S(2)}) collective-permute-start(bf16[768,128]{1,0:T(8,128)(2,1)S(1)} %get-tuple-element.48), channel_id=1, source_target_pairs={{0,24},{4,28},{8,0},{12,4},{16,8},{20,12},{24,16},{28,20},{1,25},{... | collective-permute-start | bytes 589832 | tf_op jit(solution)/shard_map/ppermute | solution.py:537
  104.2 7.5 %collective-permute-start.13 = (bf16[768,128]{1,0:T(8,128)(2,1)S(1)}, bf16[768,128]{1,0:T(8,128)(2,1)S(1)}, u32[]{:S(2)}, u32[]{:S(2)}) collective-permute-start(bf16[768,128]{1,0:T(8,128)(2,1)S(1)} %get-tuple-element.49), channel_id=1, source_target_pairs={{0,28},{4,0},{8,4},{12,8},{16,12},{20,16},{24,20},{28,24},{1,29},{... | collective-permute-start | bytes 589832 | tf_op jit(solution)/shard_map/ppermute | solution.py:537
